TPU v7x, 256 devices: a whole 4x4x8 slice. The times are simulated.
256 devices in a mesh: seq: 32 (over y_lo, z, core), head: 8 (over x, y_hi).
Axes of the slice: x: 4, y: 4 (y_hi: 2, y_lo: 2; y = y_hi * 2 + y_lo), z: 8, core: 2. Of those that a mesh axis runs over, the one named last changes fastest.
Arguments:
- span_qkv: bfloat16 [3, 8192, 4096], P(None, ('seq', 'head')), may hold values from -35 to 35
- cache_kv: bfloat16 [2, 4096, 4096], P(None, 'seq', 'head'), may hold values from -6 to 6
- audio_kv: bfloat16 [2, 512, 4096], P(None, None, 'head'), may hold values from -35 to 35
- video_kv: bfloat16 [2, 512, 4096], P(None, None, 'head'), may hold values from -35 to 35
- block_mask: int32 [8, 128, 192], P('head'), may hold values 0 or 1
- mem_lengths: int32 [2], replicated, may hold values from 128 to 512, as said below
- cross_gates: float32 [2, 32], P(None, 'head'), may hold values from -2 to 2
- out_weight: bfloat16 [4096, 4096], P('head'), may hold values from -1 to 1
Outputs:
- attn_out: bfloat16 [8192, 4096], P(('seq', 'head'))
Inputs may be any that keep to these rules, and one draw needn't show every extreme that they name: `mem_lengths`: one of the two lengths is 512.
All inputs are finite; a program needn't handle non-finite values. No bound on the sum of `block_mask` on one device may be relied on, other than what follows from the above.
Results may differ from a plain program's by a relative error of at most 0.019.
Values may be sent and summed in bfloat16 or wider, within the bound.
No kernel may reach another device: no remote copies, remote signals or barrier semaphores. Data moves between devices by JAX's collectives and lax.ppermute only.
A program may use at most 128 MiB of HBM per device.

v0:
```python
import math

import jax
import jax.numpy as jnp
from jax import lax
from jax.sharding import PartitionSpec as P

H = 32
HD = 128
G = 8
BLK = 64
CH_DEV = 256


neg_large = -1e30


def seq_positions(storage, dev_count, per_dev):
    half_len = per_dev // 2
    device = storage // per_dev
    within = storage % per_dev
    segment = jnp.where(within < half_len, device, 2 * dev_count - 1 - device)
    return segment * half_len + within % half_len


def attend_block(carried, queries, key_rows, values, allowed):
    run_max, run_sum, run_acc = carried
    score_scale = 1.0 / math.sqrt(queries.shape[2])
    scores = (
        jnp.einsum("qhd,khd->qhk", queries, key_rows, preferred_element_type=jnp.float32)
        * score_scale
    )
    masked = jnp.where(allowed, scores, neg_large)
    new_max = jnp.maximum(run_max, jnp.max(masked, axis=2))
    factor = jnp.exp(run_max - new_max)
    weights = jnp.where(allowed, jnp.exp(masked - new_max[:, :, None]), 0.0)
    new_sum = run_sum * factor + jnp.sum(weights, axis=2)
    update = jnp.einsum(
        "qhk,khd->qhd", weights.astype(jnp.bfloat16), values, preferred_element_type=jnp.float32
    )
    return (new_max, new_sum, run_acc * factor[:, :, None] + update)


def fold_keys(carried, segment, queries, allowed_fn):
    row_count = segment.shape[1]
    step_rows = math.gcd(row_count, 512)
    heads_here = queries.shape[1]

    def one_step(turn_index, running):
        offset = turn_index * step_rows
        slab_rows = lax.dynamic_slice_in_dim(segment, offset, step_rows, 1)
        key_rows = slab_rows[0].reshape(step_rows, heads_here, -1)
        values = slab_rows[1].reshape(step_rows, heads_here, -1)
        allowed = allowed_fn(offset + jnp.arange(step_rows, dtype=jnp.int32))
        return attend_block(running, queries, key_rows, values, allowed)

    return lax.fori_loop(0, row_count // step_rows, one_step, carried)


def cross_attend(queries, memory, length):
    slot_count = memory.shape[1]
    heads_here = queries.shape[1]
    score_scale = 1.0 / math.sqrt(queries.shape[2])
    mem_keys = memory[0].reshape(slot_count, heads_here, -1)
    mem_values = memory[1].reshape(slot_count, heads_here, -1)
    scores = (
        jnp.einsum("qhd,khd->qhk", queries, mem_keys, preferred_element_type=jnp.float32)
        * score_scale
    )
    live_slots = (jnp.arange(slot_count, dtype=jnp.int32) < length)[None, None, :]
    masked = jnp.where(live_slots, scores, neg_large)
    row_top = jnp.max(masked, axis=2, keepdims=True)
    weights = jnp.where(live_slots, jnp.exp(masked - row_top), 0.0)
    row_total = jnp.sum(weights, axis=2)
    product = jnp.einsum(
        "qhk,khd->qhd", weights.astype(jnp.bfloat16), mem_values, preferred_element_type=jnp.float32
    )
    return product / row_total[:, :, None]


def shards(
    span_qkv, cache_kv, audio_kv, video_kv, block_mask, mem_lengths, cross_gates, out_weight
):
    seq_count = lax.axis_size("seq")
    seq_index = lax.axis_index("seq")
    local_qkv = lax.all_to_all(span_qkv, "head", split_axis=2, concat_axis=1, tiled=True)
    rows_here = local_qkv.shape[1]
    heads_here = local_qkv.shape[2] // HD
    per_group = H // G
    queries = local_qkv[0].reshape(rows_here, heads_here, HD)
    span_pairs = local_qkv[1:3]
    storage = seq_index * rows_here + jnp.arange(rows_here, dtype=jnp.int32)
    query_pos = seq_positions(storage, seq_count, CH_DEV)
    query_blocks = query_pos // BLK
    mask_rows = jnp.transpose(jnp.take(block_mask, query_blocks, axis=1), (1, 0, 2))
    cache_count = cache_kv.shape[1] * seq_count // BLK

    def span_allowed(key_storage):
        key_pos = seq_positions(key_storage, seq_count, CH_DEV)
        key_blocks = key_pos // BLK
        block_ok = jnp.take(mask_rows, cache_count + key_blocks, axis=2) != 0
        same_block = key_blocks[None, None, :] == query_blocks[:, None, None]
        causal = key_pos[None, None, :] <= query_pos[:, None, None]
        return jnp.repeat(causal & (same_block | block_ok), per_group, axis=1)

    def cache_allowed(key_storage):
        block_ok = jnp.take(mask_rows, key_storage // BLK, axis=2) != 0
        return jnp.repeat(block_ok, per_group, axis=1)

    initial = (
        jnp.full((rows_here, heads_here), neg_large, jnp.float32),
        jnp.zeros((rows_here, heads_here), jnp.float32),
        jnp.zeros((rows_here, heads_here, HD), jnp.float32),
    )
    carried = fold_keys(
        fold_keys(
            initial, lax.all_gather(span_pairs, "seq", axis=1, tiled=True), queries, span_allowed
        ),
        lax.all_gather(cache_kv, "seq", axis=1, tiled=True),
        queries,
        cache_allowed,
    )
    run_max, run_sum, run_acc = carried
    own_attn = run_acc / run_sum[:, :, None]
    gate_values = jnp.tanh(cross_gates)
    audio_part = cross_attend(queries, audio_kv, mem_lengths[0])
    video_part = cross_attend(queries, video_kv, mem_lengths[1])
    combined = (
        own_attn
        + gate_values[0][None, :, None] * audio_part
        + gate_values[1][None, :, None] * video_part
    )
    mixed = combined.astype(jnp.bfloat16).reshape(rows_here, heads_here * HD)
    result = lax.psum_scatter(
        jnp.dot(mixed, out_weight, preferred_element_type=jnp.float32).astype(jnp.bfloat16),
        "head",
        scatter_dimension=0,
        tiled=True,
    )
    return result


def solution(mesh):
    placed = (
        P(None, ("seq", "head"), None),
        P(None, "seq", "head"),
        P(None, None, "head"),
        P(None, None, "head"),
        P("head", None, None),
        P(),
        P(None, "head"),
        P("head", None),
    )
    return jax.shard_map(
        shards, mesh=mesh, in_specs=placed, out_specs=P(("seq", "head"), None), check_vma=False
    )
```

profile of v0, /device:TPU:32, one launch (start us, length us, event | category | flops | bytes accessed | tf_op | source)
XLA Modules:
  0.0 420.6 jit_solution(9575415637956172686)
XLA Ops:
  6.5 6.0 %copy.69 = bf16[3,32,4096]{1,0,2:T(4,128)(2,1)} copy(bf16[3,32,4096]{2,1,0:T(8,128)(2,1)} %param.14) | data formatting | bytes 1572864 | tf_op args[0]
  12.5 6.2 %reshape.491 = bf16[8,2,24576]{2,1,0:T(2,128)(2,1)S(1)} reshape(bf16[4096,3,32]{2,1,0:T(4,128)(2,1)} %bitcast.196) | data formatting | bytes 1572864
  18.8 20.8 %all_to_all.15 = bf16[8,2,24576]{2,1,0:T(2,128)(2,1)S(1)} all-to-all(bf16[8,2,24576]{2,1,0:T(2,128)(2,1)S(1)} %reshape.491), channel_id=1, replica_groups=mesh['seq'=32,'head'=8] {'head'}, dimensions={0} | all-to-all | bytes 1572864 | tf_op jit(solution)/shard_map/all_to_all | solution.py:86
  39.5 4.8 %reshape.492 = bf16[4096,3,32]{2,1,0:T(4,128)(2,1)} reshape(bf16[8,2,24576]{2,1,0:T(2,128)(2,1)S(1)} %all_to_all.15) | data formatting | bytes 1572864
  44.4 4.2 %copy.97 = bf16[3,32,8,512]{3,2,1,0:T(8,128)(2,1)S(1)} copy(bf16[3,32,8,512]{1,0,3,2:T(4,128)(2,1)} %bitcast.195) | data formatting | bytes 1572864 | tf_op jit(solution)/shard_map/all_to_all | solution.py:86
  59.5 2.0 fusion.104
  62.6 85.8 %all-gather.3.cloned.1.call-done = bf16[2,8192,512]{2,1,0:T(8,128)(2,1)} async-done(((bf16[2,256,512]{2,1,0:T(8,128)(2,1)}), bf16[2,8192,512]{2,1,0:T(8,128)(2,1)}) %all-gather.3.cloned.1.call-update) | async-done | bytes 16777232 | tf_op jit(solution)/shard_map/all_gather | solution.py:117
  148.4 132.4 %while.43 = (s32[]{:T(128)}, f32[256,4]{0,1:T(4,128)S(1)}, f32[256,4]{0,1:T(4,128)S(1)}, f32[256,4,128]{0,2,1:T(8,128)}, s32[256,1,192]{0,2,1:T(8,128)S(1)}, /*i...) while((s32[]{:T(128)}, f32[256,4]{0,1:T(4,128)S(1)}, ...), condition=%wide.region_3.5_spmd.clone.clone.clone, body=%wide.region_0.4_spmd.clone.clone.clone.sunk | while | flops 276526336 | bytes 15031515 | solution.py:57
  148.4 1.6 gather_fusion.1
  151.9 1.5 fusion.157
  155.7 1.6 gather_fusion.1
  161.5 2.5 fusion.160
  164.0 1.6 gather_fusion.1
  167.5 1.6 fusion.157
  169.8 2.5 fusion.160
  172.4 1.6 gather_fusion.1
  178.2 2.5 fusion.160
  180.7 1.6 gather_fusion.1
  184.2 1.5 fusion.157
  186.5 2.5 fusion.160
  189.1 1.6 gather_fusion.1
  192.5 1.5 fusion.157
  194.8 2.5 fusion.160
  197.4 1.6 gather_fusion.1
  200.9 1.5 fusion.157
  203.2 2.5 fusion.160
  205.8 1.6 gather_fusion.1
  209.3 1.5 fusion.157
  211.6 2.5 fusion.160
  214.1 1.6 gather_fusion.1
  217.6 1.5 fusion.157
  219.9 2.5 fusion.160
  222.5 1.6 gather_fusion.1
  226.0 1.5 fusion.157
  228.3 2.5 fusion.160
  230.9 1.6 gather_fusion.1
  234.3 1.5 fusion.157
  236.7 2.5 fusion.160
  239.2 1.6 gather_fusion.1
  242.7 1.5 fusion.157
  245.0 2.5 fusion.160
  247.5 1.6 gather_fusion.1
  253.3 2.5 fusion.160
  255.9 1.6 gather_fusion.1
  259.3 1.5 fusion.157
  261.6 2.5 fusion.160
  264.2 1.6 gather_fusion.1
  267.6 1.5 fusion.157
  270.0 2.5 fusion.160
  272.5 1.6 gather_fusion.1
  276.0 1.5 fusion.157
  278.3 2.5 fusion.160
  280.8 46.6 %while.42 = (s32[]{:T(128)}, f32[256,4]{0,1:T(4,128)S(1)}, f32[256,4]{0,1:T(4,128)S(1)}, f32[256,4,128]{0,2,1:T(8,128)}, s32[256,1,192]{0,2,1:T(8,128)S(1)}, /*i...) while((s32[]{:T(128)}, f32[256,4]{0,1:T(4,128)S(1)}, ...), condition=%wide.region_7.9_spmd, body=%wide.region_4.8_spmd.sunk | while | flops 275799552 | bytes 18165012 | solution.py:57
  282.2 1.6 gather_fusion
  288.0 1.6 gather_fusion
  293.8 1.6 gather_fusion
  299.7 1.6 gather_fusion
  305.5 1.6 gather_fusion
  311.3 1.6 gather_fusion
  317.1 1.6 gather_fusion
  322.9 1.6 gather_fusion
  327.4 2.0 fusion.66
  330.3 2.6 convolution_convert_fusion
  332.9 81.1 %reduce-scatter.2.cloned.1.call-done = bf16[32,4096]{1,0:T(8,128)(2,1)} async-done(((bf16[256,4096]{1,0:T(8,128)(2,1)}), bf16[32,4096]{1,0:T(8,128)(2,1)}) %reduce-scatter.2.cloned.1.call-update) | async-done | bytes 262160 | tf_op jit(solution)/shard_map/reduce_scatter | solution.py:134
  (405 shorter events, 94.3 us)
Async XLA Ops:
  6.5 141.8 %all-gather.3.cloned.1.call-start = ((), (), s32[]{:S(2)}) async-start(), calls=%async_computation.2 | async-start | bytes 17301504 | tf_op jit(solution)/shard_map/all_gather | solution.py:117
  48.6 1.1 copy-start.7
  48.6 2.1 copy-start.8
  49.7 2.4 copy-start.2
  49.7 231.2 %all-gather.5.cloned.1.call-start = ((), (), s32[]{:S(2)}) async-start(), calls=%async_computation.3 | async-start | bytes 8650752 | tf_op jit(solution)/shard_map/all_gather | solution.py:119
  50.6 363.5 %reduce-scatter.2.cloned.1.call-start = ((), (), s32[]{:S(2)}) async-start(), calls=%async_computation.4 | async-start | bytes 2359296 | tf_op jit(solution)/shard_map/reduce_scatter | solution.py:134
  51.8 1.4 copy-start.9
  52.1 3.4 copy-start.10
  52.2 3.3 copy-start.3
  55.6 2.8 copy-start.6
  59.4 2.0 copy-start.5
  280.8 46.6 %copy-start.4 = (bf16[1,512,512]{1,2,0:T(8,128)(2,1)S(1)}, bf16[1,512,512]{1,2,0:T(8,128)(2,1)}, u32[]{:S(2)}) copy-start(bf16[1,512,512]{1,2,0:T(8,128)(2,1)} %copy.82) | copy-start | bytes 1572868
  282.2 1.8 copy-start
  284.0 1.1 copy-start.11
  285.9 0.8 copy-start.12
  288.0 1.8 copy-start
  289.8 1.1 copy-start.11
  291.7 0.8 copy-start.12
  293.8 1.8 copy-start
  295.6 1.1 copy-start.11
  297.5 0.8 copy-start.12
  299.6 1.8 copy-start
  301.4 1.1 copy-start.11
  303.4 0.8 copy-start.12
  305.5 1.8 copy-start
  307.3 1.1 copy-start.11
  309.2 0.8 copy-start.12
  311.3 1.8 copy-start
  313.1 1.1 copy-start.11
  315.0 0.8 copy-start.12
  317.1 1.8 copy-start
  318.9 1.1 copy-start.11
  320.8 0.8 copy-start.12
  322.9 1.8 copy-start
  324.7 1.1 copy-start.11
  326.6 0.8 copy-start.12
  327.4 2.8 copy-start.1
Sparse Core Ops, SparseCore 0:
  49.8 98.5 all-gather.2
  150.1 89.4 all-gather.4
  333.0 80.9 reduce-scatter.1
where the time goes:
time: 423 us; the launch traced here: 421 us
  waiting for transfers between devices  167 us (39%)
  local copies, waits for them, and re-layouts  112 us (26%)
  matrix products  83.2 us (20%)
  other arithmetic  22.6 us (5%)
  blocking collectives  20.8 us (5%)
  between operations  13.3 us (3%)
    all_gather x1, waiting for transfers between devices, shards(): lax.all_gather(span_pairs, 'seq', axis=1, tiled=True)  85.8 us
    reduce_scatter x1, waiting for transfers between devices, shards(): lax.psum_scatter(jnp.dot(mixed, out_weight, preferred_element_type=jnp.fl...  81.1 us
    dot_general x24, matrix products, attend_block(): jnp.einsum('qhk,khd->qhd', weights.astype(jnp.bfloat16), values, preferre...  45.4 us
    slice x24, local copies, waits for them, and re-layouts, one_step(): values = slab_rows[1].reshape(step_rows, heads_here, -1)  30.8 us
    dot_general x24, matrix products, attend_block(): jnp.einsum('qhd,khd->qhk', queries, key_rows, preferred_element_type=jnp....  29 us
    gather x16, local copies, waits for them, and re-layouts, span_allowed(): block_ok = jnp.take(mask_rows, cache_count + key_blocks, axis=2) != 0  25.2 us
    unnamed x29, local copies, waits for them, and re-layouts  21 us
    all_to_all x1, blocking collectives, shards(): lax.all_to_all(span_qkv, 'head', split_axis=2, concat_axis=1, tiled=True)  20.8 us
  transfers between devices with their start and end apart: 3, of which 2 were waited for; matrix products, arithmetic and copies ran while one was open for 34% of the time, Pallas kernels for 0%

commit v1 on v0

v1 whole, which is shorter than its diff:
```python
import functools
import math

import jax
import jax.numpy as jnp
from jax import lax
from jax.experimental import pallas as pl
from jax.experimental.pallas import tpu as pltpu
from jax.sharding import Mesh
from jax.sharding import PartitionSpec as P

HD = 128
neg_large = -1e30
score_scale = math.log2(math.e) / math.sqrt(HD)

AXES = ("yl", "z2", "z1", "z0", "c", "x", "yh")
SIZES = (2, 2, 2, 2, 2, 4, 2)
ZZ = ("z2", "z1")
HEADS = ("x", "yh")

VM = pltpu.VMEM
SM = pltpu.SMEM
whole = functools.partial(pl.BlockSpec, memory_space=VM)
scalars = functools.partial(pl.BlockSpec, memory_space=SM)
params = functools.partial(pltpu.CompilerParams, vmem_limit_bytes=40 * 2**20)


def xor_perm(count, k):
    return [(i, i ^ k) for i in range(count)]


def pack_kernel(where_ref, span_ref, cache_ref, span_out, cache_out):
    j = where_ref[1]
    for d in range(32):
        col = ((d % 8) * 4 + d // 8) * HD
        span_out[d] = span_ref[:, :, col:col + HD]
    for k in range(4):
        col = pl.multiple_of((j ^ k) * HD, HD)
        cache_out[k] = cache_ref[:, :, pl.ds(col, HD)]


def unpack_kernel(got_ref, q_out, kv_out):
    for t in range(8):
        first = (t if t < 4 else 7 - t) * 8 + (t // 4) * 4
        rows = slice(t * 128, (t + 1) * 128)
        q_out[rows, :] = got_ref[first:first + 4, 0].reshape(128, HD)
        kv_out[0, rows, :] = got_ref[first:first + 4, 1].reshape(128, HD)
        kv_out[1, rows, :] = got_ref[first:first + 4, 2].reshape(128, HD)


def segment_of(t, yl, z0, c):
    low = t < 4
    s = yl * 16 + jnp.where(low, t, 7 - t) * 4 + z0 * 2 + c
    return jnp.where(low, s, 63 - s)


def bias_kernel(where_ref, mask_ref, cache_out, *span_outs):
    yl, j, z0, c = where_ref[0], where_ref[1], where_ref[2], where_ref[3]
    mask = mask_ref[0].astype(jnp.float32).astype(jnp.bfloat16)
    r = lax.broadcasted_iota(jnp.int32, (16, 128), 0)
    qb = 2 * segment_of(r >> 1, yl, z0, c) + (r & 1)
    pick = (lax.broadcasted_iota(jnp.int32, (16, 128), 1) == qb).astype(jnp.float32)
    rows = jnp.dot(pick.astype(jnp.bfloat16), mask, preferred_element_type=jnp.float32)
    rows = rows.astype(jnp.bfloat16)

    def spread(block):
        n = block.shape[1]
        one = lax.broadcasted_iota(jnp.int32, (192, n), 0) == jnp.broadcast_to(block, (192, n))
        one = jnp.where(one, 1.0, 0.0).astype(jnp.bfloat16)
        return jnp.dot(rows, one, preferred_element_type=jnp.float32) > 0.5

    for g in range(4):
        dy, dz = g >> 1, g & 1
        lane = lax.broadcasted_iota(jnp.int32, (1, 1024), 1)
        dc, k, b = lane >> 9, (lane >> 7) & 3, (lane >> 6) & 1
        s = (yl ^ dy) * 16 + (j ^ k) * 4 + (z0 ^ dz) * 2 + (c ^ dc)
        ok = spread(2 * s + b)
        cache_out[:, g * 1024:(g + 1) * 1024] = jnp.where(ok, 0.0, neg_large)
        for half in range(2):
            t, b = lane >> 7, (lane >> 6) & 1
            kb = 2 * segment_of(t, yl ^ dy, z0 ^ dz, c ^ half) + b
            ok = spread(kb + 64).astype(jnp.int32)
            q_full = jnp.broadcast_to(qb[:, :1], (16, 1024))
            k_full = jnp.broadcast_to(kb, (16, 1024))
            ok = ((k_full < q_full) & (ok != 0)) | (k_full == q_full)
            span_outs[g][:, half * 1024:(half + 1) * 1024] = jnp.where(ok, 0.0, neg_large)


def score_tile(q, keys):
    return lax.dot_general(
        q, keys, (((1,), (1,)), ((), ())), preferred_element_type=jnp.float32
    )


def lane_sums(p):
    total = p[:, :HD]
    for i in range(1, p.shape[1] // HD):
        total = total + p[:, i * HD:(i + 1) * HD]
    return total


def fold(state, q, keys, values, bias_ref, block, lanes, causal=None):
    top, total, acc = state
    raw = score_tile(q, keys) * score_scale
    parts = []
    for i in range(q.shape[0] // 64):
        parts.append(raw[i * 64:(i + 1) * 64] + bias_ref[pl.ds(block + i, 1), lanes])
    s = jnp.concatenate(parts, axis=0)
    if causal is not None:
        s = s + causal
    new_top = jnp.maximum(top, jnp.max(s, axis=1, keepdims=True))
    factor = jnp.exp2(top - new_top)
    p = jnp.exp2(s - new_top[:, :1])
    total = total * factor + lane_sums(p)
    acc = acc * factor + jnp.dot(
        p.astype(jnp.bfloat16), values, preferred_element_type=jnp.float32
    )
    return new_top, total, acc


def cache_kernel(q_ref, *refs):
    kv, bias_ref, top_out, total_out, acc_out = refs[:8], refs[8], refs[9], refs[10], refs[11]

    def step(w, _):
        rows = pl.ds(pl.multiple_of(w * 256, 256), 256)
        q = q_ref[rows, :]
        state = (
            jnp.full((256, HD), neg_large, jnp.float32),
            jnp.zeros((256, HD), jnp.float32),
            jnp.zeros((256, HD), jnp.float32),
        )
        for n in range(8):
            state = fold(
                state, q, kv[n][:, 0].reshape(512, HD), kv[n][:, 1].reshape(512, HD),
                bias_ref, w * 4, slice(n * 512, (n + 1) * 512),
            )
        top_out[rows, :], total_out[rows, :], acc_out[rows, :] = state
        return 0

    lax.fori_loop(0, 4, step, 0)


def memory_kernel(where_ref, len_ref, gate_ref, q_ref, audio_ref, video_ref, out_ref):
    j = where_ref[1]
    slot = lax.broadcasted_iota(jnp.int32, (1, 512), 1)

    def step(w, _):
        rows = pl.ds(pl.multiple_of(w * 256, 256), 256)
        q = q_ref[rows, :]
        mixed = jnp.zeros((256, HD), jnp.float32)
        for n, mem_ref in enumerate((audio_ref, video_ref)):
            bias = jnp.where(slot < len_ref[n], 0.0, neg_large)
            s = score_tile(q, mem_ref[0]) * score_scale + bias
            p = jnp.exp2(s - jnp.max(s, axis=1, keepdims=True))
            total = jnp.sum(p, axis=1, keepdims=True)
            part = jnp.dot(
                p.astype(jnp.bfloat16), mem_ref[1], preferred_element_type=jnp.float32
            )
            gate = jnp.tanh(jnp.full((1, HD), gate_ref[n, j], jnp.float32))
            mixed = mixed + gate * (part / total)
        out_ref[rows, :] = mixed
        return 0

    lax.fori_loop(0, 4, step, 0)


def span_kernel(own, last, where_ref, q_ref, kv0_ref, kv1_ref, bias_ref, *refs):
    top_ref, total_ref, acc_ref = refs[:3]
    if last:
        extra_ref, out_ref = refs[3:]
    else:
        outs = refs[3:]
    j = where_ref[1]
    for w in range(4):
        rows = slice(w * 256, (w + 1) * 256)
        q = q_ref[rows, :]
        state = (top_ref[rows, :], total_ref[rows, :], acc_ref[rows, :])
        for dc, kv_ref in enumerate((kv0_ref, kv1_ref)):
            for half in range(1 if w < 2 else 2):
                keys = slice(half * 512, (half + 1) * 512)
                causal = None
                if own and dc == 0:
                    row = lax.broadcasted_iota(jnp.int32, (256, 512), 0) + w * 256
                    col = lax.broadcasted_iota(jnp.int32, (256, 512), 1) + half * 512
                    causal = jnp.where(col <= row, 0.0, neg_large)
                state = fold(
                    state, q, kv_ref[0, keys, :], kv_ref[1, keys, :], bias_ref, w * 4,
                    slice(dc * 1024 + half * 512, dc * 1024 + (half + 1) * 512), causal,
                )
        if last:
            top, total, acc = state
            mixed = acc / jnp.sum(total, axis=1, keepdims=True) + extra_ref[rows, :]
            mixed = mixed.astype(jnp.bfloat16)
            for i in range(2):
                t = w * 2 + i
                to = t if t < 4 else 7 - t
                half = t // 4
                out_ref[j ^ to, half * 128:(half + 1) * 128, :] = mixed[i * 128:(i + 1) * 128]
        else:
            outs[0][rows, :], outs[1][rows, :], outs[2][rows, :] = state


def project_kernel(where_ref, m0, m1, m2, m3, w_ref, out_ref, mixed):
    j = where_ref[1]

    @pl.when(pl.program_id(0) == 0)
    def _():
        for k, m in enumerate((m0, m1, m2, m3)):
            mixed[:, pl.ds(pl.multiple_of((j ^ k) * HD, HD), HD)] = m[...]

    part = jnp.dot(mixed[...], w_ref[...], preferred_element_type=jnp.float32)
    part = part.astype(jnp.bfloat16)
    for h in range(8):
        out_ref[h] = part[h * 32:(h + 1) * 32]


def cost(flops, size, exps=0):
    return pl.CostEstimate(flops=flops, bytes_accessed=size, transcendentals=exps)


def f32(*shape):
    return jax.ShapeDtypeStruct(shape, jnp.float32)


def b16(*shape):
    return jax.ShapeDtypeStruct(shape, jnp.bfloat16)


def shards(
    span_qkv, cache_kv, audio_kv, video_kv, block_mask, mem_lengths, cross_gates, out_weight
):
    j = lax.axis_index("z2") * 2 + lax.axis_index("z1")
    where = jnp.stack(
        [lax.axis_index("yl"), j, lax.axis_index("z0"), lax.axis_index("c")]
    ).astype(jnp.int32)

    span_packed, cache_packed = pl.pallas_call(
        pack_kernel,
        out_shape=(b16(32, 3, 32, HD), b16(4, 2, 128, HD)),
        in_specs=[scalars(), whole(), whole()],
        out_specs=(whole(), whole()),
        compiler_params=params(),
        cost_estimate=cost(0, 4 * 2**20),
        name="pack",
    )(where, span_qkv, cache_kv)

    cache_own = [cache_packed[0]] + [
        lax.ppermute(cache_packed[k], ZZ, xor_perm(4, k)) for k in range(1, 4)
    ]
    cache_own = jnp.stack(cache_own)

    def around(own):
        return [own] + [lax.ppermute(own, ("yl", "z0"), xor_perm(4, g)) for g in range(1, 4)]

    def sibling(part):
        return lax.ppermute(part, "c", xor_perm(2, 1))

    cache_parts = around(cache_own)

    got = lax.all_to_all(span_packed, ZZ + HEADS, split_axis=0, concat_axis=0, tiled=True)
    queries, span_own = pl.pallas_call(
        unpack_kernel,
        out_shape=(b16(1024, HD), b16(2, 1024, HD)),
        in_specs=[whole()],
        out_specs=(whole(), whole()),
        compiler_params=params(),
        cost_estimate=cost(0, 2 * 2**20),
        name="unpack",
    )(got)
    span_parts = around(span_own)

    biases = pl.pallas_call(
        bias_kernel,
        out_shape=(f32(16, 4096),) + (f32(16, 2048),) * 4,
        in_specs=[scalars(), whole()],
        out_specs=(whole(),) * 5,
        compiler_params=params(),
        cost_estimate=cost(2 * 16 * 192 * 12288, 2**20),
        name="bias",
    )(where, block_mask)

    extra = pl.pallas_call(
        memory_kernel,
        grid_spec=pltpu.PrefetchScalarGridSpec(
            num_scalar_prefetch=1,
            grid=(1,),
            in_specs=[
                scalars(),
                scalars(),
                pl.BlockSpec((1024, HD), lambda i, where: (0, 0)),
                pl.BlockSpec((2, 512, HD), lambda i, where: (0, 0, where[1])),
                pl.BlockSpec((2, 512, HD), lambda i, where: (0, 0, where[1])),
            ],
            out_specs=pl.BlockSpec((1024, HD), lambda i, where: (0, 0)),
        ),
        out_shape=f32(1024, HD),
        compiler_params=params(),
        cost_estimate=cost(4 * 1024 * 1024 * HD, 2**20, 2**20),
        name="memories",
    )(where, mem_lengths, cross_gates, queries, audio_kv, video_kv)

    cache_all = []
    for part in cache_parts:
        cache_all += [part, sibling(part)]
    state = pl.pallas_call(
        cache_kernel,
        out_shape=(f32(1024, HD),) * 3,
        in_specs=[whole()] * 10,
        out_specs=(whole(),) * 3,
        compiler_params=params(),
        cost_estimate=cost(4 * 1024 * 4096 * HD, 4 * 2**20, 4 * 2**20),
        name="cache_attention",
    )(queries, *cache_all, biases[0])

    for g, part in enumerate(span_parts):
        last = g == 3
        operands = [where, queries, part, sibling(part), biases[1 + g], *state]
        if last:
            operands.append(extra)
        state = pl.pallas_call(
            functools.partial(span_kernel, g == 0, last),
            out_shape=b16(4, 256, HD) if last else (f32(1024, HD),) * 3,
            in_specs=[scalars()] + [whole()] * (len(operands) - 1),
            out_specs=whole() if last else (whole(),) * 3,
            compiler_params=params(),
            cost_estimate=cost(4 * 1024 * 1536 * HD, 4 * 2**20, 3 * 2**19),
            name="span_attention",
        )(*operands)

    mixed = [state[0]] + [lax.ppermute(state[k], ZZ, xor_perm(4, k)) for k in range(1, 4)]
    partial_sums = pl.pallas_call(
        project_kernel,
        grid=(4,),
        out_shape=b16(8, 32, 4096),
        in_specs=[scalars()]
        + [pl.BlockSpec((256, HD), lambda i: (0, 0))] * 4
        + [pl.BlockSpec((512, 1024), lambda i: (0, i))],
        out_specs=pl.BlockSpec((8, 32, 1024), lambda i: (0, 0, i)),
        scratch_shapes=[pltpu.VMEM((256, 512), jnp.bfloat16)],
        compiler_params=params(),
        cost_estimate=cost(2 * 256 * 512 * 4096, 6 * 2**20),
        name="project",
    )(where, *mixed, out_weight)
    gathered = lax.all_to_all(partial_sums, HEADS, split_axis=0, concat_axis=0, tiled=True)
    return jnp.sum(gathered.astype(jnp.float32), axis=0).astype(jnp.bfloat16)


def solution(mesh):
    fine = Mesh(mesh.devices.reshape(SIZES), AXES)
    seq = ("yl", "z2", "z1", "z0", "c")
    placed = (
        P(None, seq + HEADS, None),
        P(None, seq, HEADS),
        P(None, None, HEADS),
        P(None, None, HEADS),
        P(HEADS, None, None),
        P(),
        P(None, HEADS),
        P(HEADS, None),
    )
    return jax.shard_map(
        shards, mesh=fine, in_specs=placed, out_specs=P(seq + HEADS, None), check_vma=False
    )
```

time: 423 us -> 179 us (0.42)
  waiting for transfers between devices: 167 us -> 51.6 us
  local copies, waits for them, and re-layouts: 112 us -> 5.44 us
  matrix products: 83.2 us -> 0 us
  Pallas kernels: 0 us -> 48 us
  starting transfers between devices: 0.09 us -> 35.8 us
  other arithmetic: 22.6 us -> 1.86 us
  blocking collectives: 20.8 us -> 35.1 us
  between operations: 13.3 us -> 0.23 us
    all_gather x2 -> x0, waiting for transfers between devices: 85.8 us -> none  [the longest x1 85.8 us: shards(): lax.all_gather(span_pairs, 'seq', axis=1, tiled=True)]
    reduce_scatter x1 -> x0, waiting for transfers between devices: 81.1 us -> none  [shards(): lax.psum_scatter(jnp.dot(mixed, out_weight, preferred_element_type=jnp.fl...]
    dot_general x51 -> x0, matrix products: 80.1 us -> none  [the longest x24 45.4 us: attend_block(): jnp.einsum('qhk,khd->qhd', weights.astype(jnp.bfloat16), values, preferre...]
    ppermute x0 -> x20, waiting for transfers between devices: none -> 51.6 us  [the longest x6 24.6 us: around(): lax.ppermute(own, ('yl', 'z0'), xor_perm(4, g))]
    pallas_call x0 -> x10, Pallas kernels: none -> 48 us  [the longest x4 26 us: shards(): pl.pallas_call(functools.partial(span_kernel, g == 0, last), out_shape=b1...]
    gather x25 -> x0, local copies, waits for them, and re-layouts: 38.7 us -> none  [the longest x16 25.2 us: span_allowed(): block_ok = jnp.take(mask_rows, cache_count + key_blocks, axis=2) != 0]
    slice x33 -> x1, local copies, waits for them, and re-layouts: 34.7 us -> 0.02 us  [shards(): cache_packed[0]]
    ppermute x0 -> x20, starting transfers between devices: none -> 22.6 us  [the longest x6 7.89 us: around(): lax.ppermute(own, ('yl', 'z0'), xor_perm(4, g))]
  transfers between devices with their start and end apart: 3 -> 21, of which waited for: 2 -> 11; matrix products, arithmetic and copies ran while one was open for 34% -> 1% of each run, Pallas kernels for 0% -> 21%
where the time goes in v1:
time: 179 us; the launch traced here: 178 us
  waiting for transfers between devices  51.6 us (29%)
  Pallas kernels  48 us (27%)
  starting transfers between devices  35.8 us (20%)
  blocking collectives  35.1 us (20%)
  local copies, waits for them, and re-layouts  5.44 us (3%)
  other arithmetic  1.86 us (1%)
    all_to_all x1, blocking collectives, shards(): lax.all_to_all(partial_sums, HEADS, split_axis=0, concat_axis=0, tiled=True)  35.1 us
    pallas_call x4, Pallas kernels, shards(): pl.pallas_call(functools.partial(span_kernel, g == 0, last), out_shape=b1...  26 us
    ppermute x6, waiting for transfers between devices, around(): lax.ppermute(own, ('yl', 'z0'), xor_perm(4, g))  24.6 us
    ppermute x3, waiting for transfers between devices, shards(): lax.ppermute(cache_packed[k], ZZ, xor_perm(4, k))  19.3 us
    all_to_all x1, starting transfers between devices, shards(): lax.all_to_all(span_packed, ZZ + HEADS, split_axis=0, concat_axis=0, tile...  13.2 us
    pallas_call x1, Pallas kernels, shards(): pl.pallas_call(cache_kernel, out_shape=(f32(1024, HD),) * 3, in_specs=[wh...  11.8 us
    ppermute x6, starting transfers between devices, around(): lax.ppermute(own, ('yl', 'z0'), xor_perm(4, g))  7.89 us
    ppermute x3, starting transfers between devices, shards(): lax.ppermute(state[k], ZZ, xor_perm(4, k))  6.58 us
  transfers between devices with their start and end apart: 21, of which 11 were waited for; matrix products, arithmetic and copies ran while one was open for 1% of the time, Pallas kernels for 21%

profile of v1, /device:TPU:32, one launch (start us, length us, event | category | flops | bytes accessed | tf_op | source)
XLA Modules:
  0.0 178.1 jit_solution(3514296611123302073)
XLA Ops:
  0.0 0.1 pad_add_fusion.where_ref
  0.1 1.1 copy-done.4
  1.2 0.9 copy-done.5
  2.2 0.7 pack.1
  2.9 0.0 copy-start.3
  2.9 0.9 copy-done.3
  3.8 13.2 %all-to-all-start = ((bf16[32,3,32,128]{3,2,1,0:T(8,128)(2,1)}), bf16[32,3,32,128]{3,2,1,0:T(8,128)(2,1)S(1)}, u32[]{:S(2)}, u32[]{:S(2)}) async-start(bf16[32,3,32,128]{3,2,1,0:T(8,128)(2,1)} %copy-done.3), calls=%async_computation | async-start | bytes 1572864 | tf_op jit(solution)/shard_map/all_to_all | solution.py:260
  17.0 2.8 %collective-permute-start.7 = (bf16[2,128,128]{2,1,0:T(8,128)(2,1)S(1)}, bf16[2,128,128]{2,1,0:T(8,128)(2,1)S(1)}, u32[]{:S(2)}, u32[]{:S(2)}) collective-permute-start(bf16[2,128,128]{2,1,0:T(8,128)(2,1)S(1)} %get-tuple-element.54), channel_id=1, source_target_pairs={{0,32},{32,0},{64,96},{96,64},{1,33},{33,1},{65,97},{97,65},{2,34}... | collective-permute-start | bytes 196616 | tf_op jit(solution)/shard_map/ppermute | solution.py:248
  19.8 3.6 %collective-permute-start.8 = (bf16[2,128,128]{2,1,0:T(8,128)(2,1)S(1)}, bf16[2,128,128]{2,1,0:T(8,128)(2,1)S(1)}, u32[]{:S(2)}, u32[]{:S(2)}) collective-permute-start(bf16[2,128,128]{2,1,0:T(8,128)(2,1)S(1)} %get-tuple-element.53), channel_id=1, source_target_pairs={{0,64},{32,96},{64,0},{96,32},{1,65},{33,97},{65,1},{97,33},{2,66}... | collective-permute-start | bytes 196616 | tf_op jit(solution)/shard_map/ppermute | solution.py:248
  23.4 0.2 collective-permute-start.9
  23.6 15.8 %collective-permute-done.7 = bf16[2,128,128]{2,1,0:T(8,128)(2,1)S(1)} collective-permute-done((bf16[2,128,128]{2,1,0:T(8,128)(2,1)S(1)}, bf16[2,128,128]{2,1,0:T(8,128)(2,1)S(1)}, u32[]{:S(2)}, u32[]{:S(2)}) %collective-permute-start.7) | collective-permute-done | bytes 65568 | tf_op jit(solution)/shard_map/ppermute | solution.py:248
  39.4 2.2 %collective-permute-done.8 = bf16[2,128,128]{2,1,0:T(8,128)(2,1)S(1)} collective-permute-done((bf16[2,128,128]{2,1,0:T(8,128)(2,1)S(1)}, bf16[2,128,128]{2,1,0:T(8,128)(2,1)S(1)}, u32[]{:S(2)}, u32[]{:S(2)}) %collective-permute-start.8) | collective-permute-done | bytes 65568 | tf_op jit(solution)/shard_map/ppermute | solution.py:248
  41.7 1.3 collective-permute-done.9
  42.9 0.7 pad_maximum_fusion.refs_0_
  43.7 3.0 %collective-permute-start.11 = (bf16[4,2,128,128]{3,2,1,0:T(8,128)(2,1)}, bf16[4,2,128,128]{3,2,1,0:T(8,128)(2,1)}, u32[]{:S(2)}, u32[]{:S(2)}) collective-permute-start(bf16[4,2,128,128]{3,2,1,0:T(8,128)(2,1)} %pad_maximum_fusion.refs_0_), channel_id=1, source_target_pairs={{0,16},{16,0},{128,144},{144,128},{1,17},{17,1},{129,145},{145,129... | collective-permute-start | bytes 786440 | tf_op jit(solution)/shard_map/ppermute | solution.py:253
  46.7 0.7 collective-permute-start.13
  47.4 0.8 collective-permute-start.15
  48.2 0.0 collective-permute-start.10
  48.2 0.0 all-to-all-done.got_ref
  48.2 0.9 unpack.1
  49.0 2.0 %collective-permute-start.4 = (bf16[2,1024,128]{2,1,0:T(8,128)(2,1)}, bf16[2,1024,128]{2,1,0:T(8,128)(2,1)S(1)}, u32[]{:S(2)}, u32[]{:S(2)}) collective-permute-start(bf16[2,1024,128]{2,1,0:T(8,128)(2,1)} %get-tuple-element.28.kv0_ref), channel_id=1, source_target_pairs={{0,16},{16,0},{128,144},{144,128},{1,17},{17,1},{129,145},{145,129... | collective-permute-start | bytes 1572872 | tf_op jit(solution)/shard_map/ppermute | solution.py:253
  51.1 3.2 %collective-permute-done.11.refs_2_ = bf16[4,2,128,128]{3,2,1,0:T(8,128)(2,1)} collective-permute-done((bf16[4,2,128,128]{3,2,1,0:T(8,128)(2,1)}, bf16[4,2,128,128]{3,2,1,0:T(8,128)(2,1)}, u32[]{:S(2)}, u32[]{:S(2)}) %collective-permute-start.11) | collective-permute-done | bytes 262176 | tf_op jit(solution)/shard_map/ppermute | solution.py:253
  54.2 0.7 collective-permute-start.2
  54.9 3.6 %collective-permute-done.13.refs_4_ = bf16[4,2,128,128]{3,2,1,0:T(8,128)(2,1)} collective-permute-done((bf16[4,2,128,128]{3,2,1,0:T(8,128)(2,1)}, bf16[4,2,128,128]{3,2,1,0:T(8,128)(2,1)}, u32[]{:S(2)}, u32[]{:S(2)}) %collective-permute-start.13) | collective-permute-done | bytes 262176 | tf_op jit(solution)/shard_map/ppermute | solution.py:253
  58.5 0.7 collective-permute-start
  59.2 0.7 collective-permute-done.15.refs_6_
  60.0 0.0 collective-permute-start.12
  60.0 0.0 collective-permute-done.10.refs_1_
  60.0 0.5 collective-permute-start.14
  60.5 1.2 collective-permute-done.12.refs_3_
  61.7 0.7 copy-done.8
  62.4 0.1 collective-permute-start.6
  62.5 0.0 collective-permute-done.14.refs_5_
  62.5 0.7 copy-done.10
  63.3 0.4 collective-permute-start.16
  63.6 7.3 %collective-permute-done.4.kv0_ref = bf16[2,1024,128]{2,1,0:T(8,128)(2,1)S(1)} collective-permute-done((bf16[2,1024,128]{2,1,0:T(8,128)(2,1)}, bf16[2,1024,128]{2,1,0:T(8,128)(2,1)S(1)}, u32[]{:S(2)}, u32[]{:S(2)}) %collective-permute-start.4) | collective-permute-done | bytes 524320 | tf_op jit(solution)/shard_map/ppermute | solution.py:253
  71.0 0.0 collective-permute-start.5
  71.0 9.7 %collective-permute-done.2.kv0_ref = bf16[2,1024,128]{2,1,0:T(8,128)(2,1)S(1)} collective-permute-done((bf16[2,1024,128]{2,1,0:T(8,128)(2,1)}, bf16[2,1024,128]{2,1,0:T(8,128)(2,1)S(1)}, u32[]{:S(2)}, u32[]{:S(2)}) %collective-permute-start.2) | collective-permute-done | bytes 524320 | tf_op jit(solution)/shard_map/ppermute | solution.py:253
  80.7 0.0 collective-permute-start.3
  80.7 0.0 collective-permute-done.kv0_ref
  80.7 0.5 collective-permute-start.1
  81.2 1.0 copy.9.mask_ref
  82.2 1.8 %bias.1 = (f32[16,4096]{1,0:T(8,128)S(1)}, f32[16,2048]{1,0:T(8,128)S(1)}, f32[16,2048]{1,0:T(8,128)S(1)}, f32[16,2048]{1,0:T(8,128)S(1)}, f32[16,2048]{1,0:T(8,128)S(1)}) custom-call(s32[4]{0:T(128)S(1)} %pad_add_fusion.where_ref, s32[1,128,192]{2,1,0:T(8,128)S(1)} %copy.9.mask_ref), custom_call_target="tpu_custom_call" | custom-call | flops 75497472 | bytes 1048576 | tf_op jit(solution)/shard_map/bias/pallas_call | solution.py:272
  84.1 4.1 %memories.1.refs_3_ = f32[1024,128]{1,0:T(8,128)S(1)} custom-call(s32[4]{0:T(128)S(1)} %pad_add_fusion.where_ref, s32[2]{0:T(128)S(1)} %copy-done.7, f32[2,4]{1,0:T(2,128)S(1)} %copy-done.6, bf16[1024,128]{1,0:T(8,128)(2,1)S(1)} %get-tuple-element.27.q_ref, bf16[2,512,512]{2,1,0:T(8,128)(2,1)S(1)} %copy-done.1, bf16[2,512,512]{2,1,0:T(8,128)(2,1)S(1)} %copy-done.2), custom_call_target="tpu_custom_call" | custom-call | flops 536870912 | bytes 1048576 | tf_op jit(solution)/shard_map/memories/pallas_call | solution.py:282
  88.2 0.0 collective-permute-done.16.refs_7_
  88.2 11.8 %cache_attention.1 = (f32[1024,128]{1,0:T(8,128)S(1)}, f32[1024,128]{1,0:T(8,128)S(1)}, f32[1024,128]{1,0:T(8,128)S(1)}) custom-call(bf16[1024,128]{1,0:T(8,128)(2,1)S(1)} %get-tuple-element.27.q_ref, bf16[4,2,128,128]{3,2,1,0:T(8,128)(2,1)} %pad_maximum_fusion.refs_0_, bf16[4,2,128,128]{3,2,1,0:T(8,128)(2,1)} %collective-permute-done.10.refs_1_, ...), custom_call_target="tpu_custom_call" | custom-call | flops 2147483648 | bytes 4194304 | tf_op jit(solution)/shard_map/cache_attention/pallas_call | solution.py:305
  100.0 0.0 collective-permute-done.6.kv1_ref
  100.1 6.5 %span_attention.4 = (f32[1024,128]{1,0:T(8,128)S(1)}, f32[1024,128]{1,0:T(8,128)S(1)}, f32[1024,128]{1,0:T(8,128)S(1)}) custom-call(s32[4]{0:T(128)S(1)} %pad_add_fusion.where_ref, bf16[1024,128]{1,0:T(8,128)(2,1)S(1)} %get-tuple-element.27.q_ref, bf16[2,1024,128]{2,1,0:T(8,128)(2,1)} %get-tuple-element.28.kv0_ref, ...), custom_call_target="tpu_custom_call" | custom-call | flops 805306368 | bytes 4194304 | tf_op jit(solution)/shard_map/span_attention/pallas_call | solution.py:320
  106.5 0.0 collective-permute-done.5.kv1_ref
  106.5 6.3 %span_attention.5 = (f32[1024,128]{1,0:T(8,128)S(1)}, f32[1024,128]{1,0:T(8,128)S(1)}, f32[1024,128]{1,0:T(8,128)S(1)}) custom-call(s32[4]{0:T(128)S(1)} %pad_add_fusion.where_ref, bf16[1024,128]{1,0:T(8,128)(2,1)S(1)} %get-tuple-element.27.q_ref, bf16[2,1024,128]{2,1,0:T(8,128)(2,1)S(1)} %collective-permute-done.4.kv0_ref, ...), custom_call_target="tpu_custom_call" | custom-call | flops 805306368 | bytes 4194304 | tf_op jit(solution)/shard_map/span_attention/pallas_call | solution.py:320
  112.9 0.0 collective-permute-done.3.kv1_ref
  112.9 6.3 %span_attention.6 = (f32[1024,128]{1,0:T(8,128)S(1)}, f32[1024,128]{1,0:T(8,128)S(1)}, f32[1024,128]{1,0:T(8,128)S(1)}) custom-call(s32[4]{0:T(128)S(1)} %pad_add_fusion.where_ref, bf16[1024,128]{1,0:T(8,128)(2,1)S(1)} %get-tuple-element.27.q_ref, bf16[2,1024,128]{2,1,0:T(8,128)(2,1)S(1)} %collective-permute-done.2.kv0_ref, ...), custom_call_target="tpu_custom_call" | custom-call | flops 805306368 | bytes 4194304 | tf_op jit(solution)/shard_map/span_attention/pallas_call | solution.py:320
  119.2 0.0 collective-permute-done.1.kv1_ref
  119.2 0.0 copy-start
  119.2 6.9 %span_attention.7 = bf16[4,256,128]{2,1,0:T(8,128)(2,1)S(1)} custom-call(s32[4]{0:T(128)S(1)} %pad_add_fusion.where_ref, bf16[1024,128]{1,0:T(8,128)(2,1)S(1)} %get-tuple-element.27.q_ref, bf16[2,1024,128]{2,1,0:T(8,128)(2,1)} %collective-permute-done.kv0_ref, bf16[2,1024,128]{2,1,0:T(8,128)(2,1)} %collective-permute-done.1.kv1_ref, ...), custom_call_target="tpu_custom_call" | custom-call | flops 805306368 | bytes 4194304 | tf_op jit(solution)/shard_map/span_attention/pallas_call | solution.py:320
  126.1 2.0 %collective-permute-start.17 = (bf16[256,128]{1,0:T(8,128)(2,1)S(1)}, bf16[256,128]{1,0:T(8,128)(2,1)S(1)}, u32[]{:S(2)}, u32[]{:S(2)}) collective-permute-start(bf16[256,128]{1,0:T(8,128)(2,1)S(1)} %get-tuple-element.49), channel_id=1, source_target_pairs={{0,32},{32,0},{64,96},{96,64},{1,33},{33,1},{65,97},{97,65},{2,34}... | collective-permute-start | bytes 196616 | tf_op jit(solution)/shard_map/ppermute | solution.py:330
  128.1 2.2 %collective-permute-start.18 = (bf16[256,128]{1,0:T(8,128)(2,1)S(1)}, bf16[256,128]{1,0:T(8,128)(2,1)S(1)}, u32[]{:S(2)}, u32[]{:S(2)}) collective-permute-start(bf16[256,128]{1,0:T(8,128)(2,1)S(1)} %get-tuple-element.48), channel_id=1, source_target_pairs={{0,64},{32,96},{64,0},{96,32},{1,65},{33,97},{65,1},{97,33},{2,66}... | collective-permute-start | bytes 196616 | tf_op jit(solution)/shard_map/ppermute | solution.py:330
  130.4 2.4 %collective-permute-start.19 = (bf16[256,128]{1,0:T(8,128)(2,1)S(1)}, bf16[256,128]{1,0:T(8,128)(2,1)S(1)}, u32[]{:S(2)}, u32[]{:S(2)}) collective-permute-start(bf16[256,128]{1,0:T(8,128)(2,1)S(1)} %get-tuple-element.47), channel_id=1, source_target_pairs={{0,96},{32,64},{64,32},{96,0},{1,97},{33,65},{65,33},{97,1},{2,98}... | collective-permute-start | bytes 196616 | tf_op jit(solution)/shard_map/ppermute | solution.py:330
  132.7 0.0 collective-permute-done.17.m1
  132.7 5.1 %collective-permute-done.18.m2 = bf16[256,128]{1,0:T(8,128)(2,1)S(1)} collective-permute-done((bf16[256,128]{1,0:T(8,128)(2,1)S(1)}, bf16[256,128]{1,0:T(8,128)(2,1)S(1)}, u32[]{:S(2)}, u32[]{:S(2)}) %collective-permute-start.18) | collective-permute-done | bytes 65568 | tf_op jit(solution)/shard_map/ppermute | solution.py:330
  137.8 1.4 collective-permute-done.19.m3
  139.2 2.7 %project.1 = bf16[8,32,4096]{2,1,0:T(8,128)(2,1)S(1)} custom-call(s32[4]{0:T(128)S(1)} %pad_add_fusion.where_ref, bf16[256,128]{1,0:T(8,128)(2,1)S(1)} %get-tuple-element.50.m0, bf16[256,128]{1,0:T(8,128)(2,1)S(1)} %collective-permute-done.17.m1, bf16[256,128]{1,0:T(8,128)(2,1)S(1)} %collective-permute-done.18.m2, ...), custom_call_target="tpu_custom_call" | custom-call | flops 1073741824 | bytes 6291456 | tf_op jit(solution)/shard_map/project/pallas_call | solution.py:331
  141.9 35.1 %all_to_all.10 = bf16[8,32,4096]{2,1,0:T(8,128)(2,1)S(1)} all-to-all(bf16[8,32,4096]{2,1,0:T(8,128)(2,1)S(1)} %project.1), channel_id=1, replica_groups=mesh['yl'=2,'z2'=2,'z1'=2,'z0'=2,'c'=2,'x'=4,'yh'=2] {'x','yh'}, dimensions={0} | all-to-all | bytes 4194304 | tf_op jit(solution)/shard_map/all_to_all | solution.py:344
  177.0 1.1 reduce_sum.12
  (19 shorter events, 0.1 us)
Async XLA Ops:
  0.1 1.1 copy-start.4
  1.2 0.9 copy-start.5
  2.9 0.9 copy-start.3
  3.8 80.2 %copy-start.1 = (bf16[2,512,512]{2,1,0:T(8,128)(2,1)S(1)}, bf16[2,512,512]{2,1,0:T(8,128)(2,1)}, u32[]{:S(2)}) copy-start(bf16[2,512,512]{2,1,0:T(8,128)(2,1)} %audio_ref.1) | copy-start | bytes 3145732
  3.8 80.3 %copy-start.2 = (bf16[2,512,512]{2,1,0:T(8,128)(2,1)S(1)}, bf16[2,512,512]{2,1,0:T(8,128)(2,1)}, u32[]{:S(2)}) copy-start(bf16[2,512,512]{2,1,0:T(8,128)(2,1)} %video_ref.1) | copy-start | bytes 3145732
  3.8 80.3 %copy-start.6 = (f32[2,4]{1,0:T(2,128)S(1)}, f32[2,4]{1,0:T(2,128)}, u32[]{:S(2)}) copy-start(f32[2,4]{1,0:T(2,128)} %gate_ref.1) | copy-start | bytes 100
  3.8 80.3 %copy-start.7 = (s32[2]{0:T(128)S(1)}, s32[2]{0:T(128)}, u32[]{:S(2)}) copy-start(s32[2]{0:T(128)} %len_ref.1) | copy-start | bytes 28
  3.8 44.4 %all-to-all-start = ((bf16[32,3,32,128]{3,2,1,0:T(8,128)(2,1)}), bf16[32,3,32,128]{3,2,1,0:T(8,128)(2,1)S(1)}, u32[]{:S(2)}, u32[]{:S(2)}) async-start(bf16[32,3,32,128]{3,2,1,0:T(8,128)(2,1)} %copy-done.3), calls=%async_computation | async-start | bytes 1572864 | tf_op jit(solution)/shard_map/all_to_all | solution.py:260
  17.0 22.4 %collective-permute-start.7 = (bf16[2,128,128]{2,1,0:T(8,128)(2,1)S(1)}, bf16[2,128,128]{2,1,0:T(8,128)(2,1)S(1)}, u32[]{:S(2)}, u32[]{:S(2)}) collective-permute-start(bf16[2,128,128]{2,1,0:T(8,128)(2,1)S(1)} %get-tuple-element.54), channel_id=1, source_target_pairs={{0,32},{32,0},{64,96},{96,64},{1,33},{33,1},{65,97},{97,65},{2,34}... | collective-permute-start | bytes 196616 | tf_op jit(solution)/shard_map/ppermute | solution.py:248
  19.8 21.9 %collective-permute-start.8 = (bf16[2,128,128]{2,1,0:T(8,128)(2,1)S(1)}, bf16[2,128,128]{2,1,0:T(8,128)(2,1)S(1)}, u32[]{:S(2)}, u32[]{:S(2)}) collective-permute-start(bf16[2,128,128]{2,1,0:T(8,128)(2,1)S(1)} %get-tuple-element.53), channel_id=1, source_target_pairs={{0,64},{32,96},{64,0},{96,32},{1,65},{33,97},{65,1},{97,33},{2,66}... | collective-permute-start | bytes 196616 | tf_op jit(solution)/shard_map/ppermute | solution.py:248
  23.4 19.5 %collective-permute-start.9 = (bf16[2,128,128]{2,1,0:T(8,128)(2,1)S(1)}, bf16[2,128,128]{2,1,0:T(8,128)(2,1)S(1)}, u32[]{:S(2)}, u32[]{:S(2)}) collective-permute-start(bf16[2,128,128]{2,1,0:T(8,128)(2,1)S(1)} %get-tuple-element.52), channel_id=1, source_target_pairs={{0,96},{32,64},{64,32},{96,0},{1,97},{33,65},{65,33},{97,1},{2,98}... | collective-permute-start | bytes 196616 | tf_op jit(solution)/shard_map/ppermute | solution.py:248
  43.7 10.6 %collective-permute-start.11 = (bf16[4,2,128,128]{3,2,1,0:T(8,128)(2,1)}, bf16[4,2,128,128]{3,2,1,0:T(8,128)(2,1)}, u32[]{:S(2)}, u32[]{:S(2)}) collective-permute-start(bf16[4,2,128,128]{3,2,1,0:T(8,128)(2,1)} %pad_maximum_fusion.refs_0_), channel_id=1, source_target_pairs={{0,16},{16,0},{128,144},{144,128},{1,17},{17,1},{129,145},{145,129... | collective-permute-start | bytes 786440 | tf_op jit(solution)/shard_map/ppermute | solution.py:253
  46.7 11.8 %collective-permute-start.13 = (bf16[4,2,128,128]{3,2,1,0:T(8,128)(2,1)}, bf16[4,2,128,128]{3,2,1,0:T(8,128)(2,1)}, u32[]{:S(2)}, u32[]{:S(2)}) collective-permute-start(bf16[4,2,128,128]{3,2,1,0:T(8,128)(2,1)} %pad_maximum_fusion.refs_0_), channel_id=1, source_target_pairs={{0,128},{16,144},{128,0},{144,16},{1,129},{17,145},{129,1},{145,17... | collective-permute-start | bytes 786440 | tf_op jit(solution)/shard_map/ppermute | solution.py:253
  47.4 12.6 %collective-permute-start.15 = (bf16[4,2,128,128]{3,2,1,0:T(8,128)(2,1)}, bf16[4,2,128,128]{3,2,1,0:T(8,128)(2,1)}, u32[]{:S(2)}, u32[]{:S(2)}) collective-permute-start(bf16[4,2,128,128]{3,2,1,0:T(8,128)(2,1)} %pad_maximum_fusion.refs_0_), channel_id=1, source_target_pairs={{0,144},{16,128},{128,16},{144,0},{1,145},{17,129},{129,17},{145,1... | collective-permute-start | bytes 786440 | tf_op jit(solution)/shard_map/ppermute | solution.py:253
  48.2 11.8 %collective-permute-start.10 = (bf16[4,2,128,128]{3,2,1,0:T(8,128)(2,1)}, bf16[4,2,128,128]{3,2,1,0:T(8,128)(2,1)}, u32[]{:S(2)}, u32[]{:S(2)}) collective-permute-start(bf16[4,2,128,128]{3,2,1,0:T(8,128)(2,1)} %pad_maximum_fusion.refs_0_), channel_id=1, source_target_pairs={{0,8},{8,0},{1,9},{9,1},{2,10},{10,2},{3,11},{11,3},{4,12},{12,4},... | collective-permute-start | bytes 786440 | tf_op jit(solution)/shard_map/ppermute | solution.py:256
  49.0 22.0 %collective-permute-start.4 = (bf16[2,1024,128]{2,1,0:T(8,128)(2,1)}, bf16[2,1024,128]{2,1,0:T(8,128)(2,1)S(1)}, u32[]{:S(2)}, u32[]{:S(2)}) collective-permute-start(bf16[2,1024,128]{2,1,0:T(8,128)(2,1)} %get-tuple-element.28.kv0_ref), channel_id=1, source_target_pairs={{0,16},{16,0},{128,144},{144,128},{1,17},{17,1},{129,145},{145,129... | collective-permute-start | bytes 1572872 | tf_op jit(solution)/shard_map/ppermute | solution.py:253
  54.2 26.5 %collective-permute-start.2 = (bf16[2,1024,128]{2,1,0:T(8,128)(2,1)}, bf16[2,1024,128]{2,1,0:T(8,128)(2,1)S(1)}, u32[]{:S(2)}, u32[]{:S(2)}) collective-permute-start(bf16[2,1024,128]{2,1,0:T(8,128)(2,1)} %get-tuple-element.28.kv0_ref), channel_id=1, source_target_pairs={{0,128},{16,144},{128,0},{144,16},{1,129},{17,145},{129,1},{145,17... | collective-permute-start | bytes 1572872 | tf_op jit(solution)/shard_map/ppermute | solution.py:253
  58.5 22.2 %collective-permute-start = (bf16[2,1024,128]{2,1,0:T(8,128)(2,1)}, bf16[2,1024,128]{2,1,0:T(8,128)(2,1)}, u32[]{:S(2)}, u32[]{:S(2)}) collective-permute-start(bf16[2,1024,128]{2,1,0:T(8,128)(2,1)} %get-tuple-element.28.kv0_ref), channel_id=1, source_target_pairs={{0,144},{16,128},{128,16},{144,0},{1,145},{17,129},{129,17},{145,1... | collective-permute-start | bytes 1572872 | tf_op jit(solution)/shard_map/ppermute | solution.py:253
  60.0 1.7 collective-permute-start.12
  60.0 2.6 %collective-permute-start.14 = (bf16[4,2,128,128]{3,2,1,0:T(8,128)(2,1)}, bf16[4,2,128,128]{3,2,1,0:T(8,128)(2,1)S(1)}, u32[]{:S(2)}, u32[]{:S(2)}) collective-permute-start(bf16[4,2,128,128]{3,2,1,0:T(8,128)(2,1)} %collective-permute-done.13.refs_4_), channel_id=1, source_target_pairs={{0,8},{8,0},{1,9},{9,1},{2,10},{10,2},{3,11},{11,3},{4,12},{12,4},... | collective-permute-start | bytes 786440 | tf_op jit(solution)/shard_map/ppermute | solution.py:256
  61.7 0.7 copy-start.8
  62.4 37.6 %collective-permute-start.6 = (bf16[2,1024,128]{2,1,0:T(8,128)(2,1)}, bf16[2,1024,128]{2,1,0:T(8,128)(2,1)}, u32[]{:S(2)}, u32[]{:S(2)}) collective-permute-start(bf16[2,1024,128]{2,1,0:T(8,128)(2,1)} %get-tuple-element.28.kv0_ref), channel_id=1, source_target_pairs={{0,8},{8,0},{1,9},{9,1},{2,10},{10,2},{3,11},{11,3},{4,12},{12,4},... | collective-permute-start | bytes 1572872 | tf_op jit(solution)/shard_map/ppermute | solution.py:256
  62.5 0.7 copy-start.10
  63.3 24.9 %collective-permute-start.16 = (bf16[4,2,128,128]{3,2,1,0:T(8,128)(2,1)}, bf16[4,2,128,128]{3,2,1,0:T(8,128)(2,1)}, u32[]{:S(2)}, u32[]{:S(2)}) collective-permute-start(bf16[4,2,128,128]{3,2,1,0:T(8,128)(2,1)} %collective-permute-done.15.refs_6_), channel_id=1, source_target_pairs={{0,8},{8,0},{1,9},{9,1},{2,10},{10,2},{3,11},{11,3},{4,12},{12,4},... | collective-permute-start | bytes 786440 | tf_op jit(solution)/shard_map/ppermute | solution.py:256
  71.0 35.6 %collective-permute-start.5 = (bf16[2,1024,128]{2,1,0:T(8,128)(2,1)S(1)}, bf16[2,1024,128]{2,1,0:T(8,128)(2,1)}, u32[]{:S(2)}, u32[]{:S(2)}) collective-permute-start(bf16[2,1024,128]{2,1,0:T(8,128)(2,1)S(1)} %collective-permute-done.4.kv0_ref), channel_id=1, source_target_pairs={{0,8},{8,0},{1,9},{9,1},{2,10},{10,2},{3,11},{11,3},{4,12},{12,4},... | collective-permute-start | bytes 1572872 | tf_op jit(solution)/shard_map/ppermute | solution.py:256
  80.7 32.2 %collective-permute-start.3 = (bf16[2,1024,128]{2,1,0:T(8,128)(2,1)S(1)}, bf16[2,1024,128]{2,1,0:T(8,128)(2,1)}, u32[]{:S(2)}, u32[]{:S(2)}) collective-permute-start(bf16[2,1024,128]{2,1,0:T(8,128)(2,1)S(1)} %collective-permute-done.2.kv0_ref), channel_id=1, source_target_pairs={{0,8},{8,0},{1,9},{9,1},{2,10},{10,2},{3,11},{11,3},{4,12},{12,4},... | collective-permute-start | bytes 1572872 | tf_op jit(solution)/shard_map/ppermute | solution.py:256
  80.7 38.5 %collective-permute-start.1 = (bf16[2,1024,128]{2,1,0:T(8,128)(2,1)}, bf16[2,1024,128]{2,1,0:T(8,128)(2,1)}, u32[]{:S(2)}, u32[]{:S(2)}) collective-permute-start(bf16[2,1024,128]{2,1,0:T(8,128)(2,1)} %collective-permute-done.kv0_ref), channel_id=1, source_target_pairs={{0,8},{8,0},{1,9},{9,1},{2,10},{10,2},{3,11},{11,3},{4,12},{12,4},... | collective-permute-start | bytes 1572872 | tf_op jit(solution)/shard_map/ppermute | solution.py:256
  82.2 6.0 %copy-start.9 = (bf16[4,2,128,128]{3,2,1,0:T(8,128)(2,1)S(1)}, bf16[4,2,128,128]{3,2,1,0:T(8,128)(2,1)}, u32[]{:S(2)}) copy-start(bf16[4,2,128,128]{3,2,1,0:T(8,128)(2,1)} %copy-done.8) | copy-start | bytes 786436
  82.2 6.0 %copy-start.11 = (bf16[4,2,128,128]{3,2,1,0:T(8,128)(2,1)S(1)}, bf16[4,2,128,128]{3,2,1,0:T(8,128)(2,1)}, u32[]{:S(2)}) copy-start(bf16[4,2,128,128]{3,2,1,0:T(8,128)(2,1)} %copy-done.10) | copy-start | bytes 786436
  119.2 20.0 %copy-start = (bf16[512,4096]{1,0:T(8,128)(2,1)S(1)}, bf16[512,4096]{1,0:T(8,128)(2,1)}, u32[]{:S(2)}) copy-start(bf16[512,4096]{1,0:T(8,128)(2,1)} %w_ref.1) | copy-start | bytes 12582916
  126.1 6.6 %collective-permute-start.17 = (bf16[256,128]{1,0:T(8,128)(2,1)S(1)}, bf16[256,128]{1,0:T(8,128)(2,1)S(1)}, u32[]{:S(2)}, u32[]{:S(2)}) collective-permute-start(bf16[256,128]{1,0:T(8,128)(2,1)S(1)} %get-tuple-element.49), channel_id=1, source_target_pairs={{0,32},{32,0},{64,96},{96,64},{1,33},{33,1},{65,97},{97,65},{2,34}... | collective-permute-start | bytes 196616 | tf_op jit(solution)/shard_map/ppermute | solution.py:330
  128.1 9.7 %collective-permute-start.18 = (bf16[256,128]{1,0:T(8,128)(2,1)S(1)}, bf16[256,128]{1,0:T(8,128)(2,1)S(1)}, u32[]{:S(2)}, u32[]{:S(2)}) collective-permute-start(bf16[256,128]{1,0:T(8,128)(2,1)S(1)} %get-tuple-element.48), channel_id=1, source_target_pairs={{0,64},{32,96},{64,0},{96,32},{1,65},{33,97},{65,1},{97,33},{2,66}... | collective-permute-start | bytes 196616 | tf_op jit(solution)/shard_map/ppermute | solution.py:330
  130.4 8.9 %collective-permute-start.19 = (bf16[256,128]{1,0:T(8,128)(2,1)S(1)}, bf16[256,128]{1,0:T(8,128)(2,1)S(1)}, u32[]{:S(2)}, u32[]{:S(2)}) collective-permute-start(bf16[256,128]{1,0:T(8,128)(2,1)S(1)} %get-tuple-element.47), channel_id=1, source_target_pairs={{0,96},{32,64},{64,32},{96,0},{1,97},{33,65},{65,33},{97,1},{2,98}... | collective-permute-start | bytes 196616 | tf_op jit(solution)/shard_map/ppermute | solution.py:330

commit v2 on v1

v2 whole, which is shorter than its diff:
```python
import functools
import math

import jax
import jax.numpy as jnp
from jax import lax
from jax.experimental import pallas as pl
from jax.experimental.pallas import tpu as pltpu
from jax.sharding import Mesh
from jax.sharding import PartitionSpec as P

HD = 128
KEYS = 1536
neg_large = -1e30
score_scale = math.log2(math.e) / math.sqrt(HD)

AXES = ("yl", "z2", "z1", "z0", "c", "x", "yh")
SIZES = (2, 2, 2, 2, 2, 4, 2)
ZZ = ("z2", "z1")
HEADS = ("x", "yh")

VM = pltpu.VMEM
SM = pltpu.SMEM
whole = functools.partial(pl.BlockSpec, memory_space=VM)
anywhere = functools.partial(pl.BlockSpec, memory_space=pl.ANY)
scalars = functools.partial(pl.BlockSpec, memory_space=SM)
params = functools.partial(pltpu.CompilerParams, vmem_limit_bytes=40 * 2**20)


def xor_perm(count, k):
    return [(i, i ^ k) for i in range(count)]


def pack_kernel(where_ref, span_ref, cache_ref, span_out, cache_out, sems):
    j = where_ref[1]
    copies = []
    for k in range(4):
        col = pl.multiple_of((j ^ k) * HD, HD)
        copies.append((cache_ref.at[:, :, pl.ds(col, HD)], cache_out.at[k]))
    for d in range(32):
        col = ((d % 8) * 4 + d // 8) * HD
        copies.append((span_ref.at[:, :, pl.ds(col, HD)], span_out.at[d]))
    copies = [
        pltpu.make_async_copy(src, dst, sems.at[n]) for n, (src, dst) in enumerate(copies)
    ]
    for copy in copies:
        copy.start()
    for copy in copies:
        copy.wait()


def unpack_kernel(got_ref, c0_ref, c1_ref, c2_ref, c3_ref, q_out, kv_out):
    for t in range(8):
        first = (t if t < 4 else 7 - t) * 8 + (t // 4) * 4
        rows = slice(t * 128, (t + 1) * 128)
        q_out[rows, :] = got_ref[first:first + 4, 0].reshape(128, HD)
        kv_out[0, rows, :] = got_ref[first:first + 4, 1].reshape(128, HD)
        kv_out[1, rows, :] = got_ref[first:first + 4, 2].reshape(128, HD)
    for k, c_ref in enumerate((c0_ref, c1_ref, c2_ref, c3_ref)):
        kv_out[:, 1024 + k * 128:1024 + (k + 1) * 128, :] = c_ref[...]


def segment_of(t, yl, z0, c):
    low = t < 4
    s = yl * 16 + jnp.where(low, t, 7 - t) * 4 + z0 * 2 + c
    return jnp.where(low, s, 63 - s)


def bias_kernel(where_ref, mask_ref, own_out, near_out):
    yl, j, z0, c = where_ref[0], where_ref[1], where_ref[2], where_ref[3]
    mask = mask_ref[0].astype(jnp.float32).astype(jnp.bfloat16)
    r = lax.broadcasted_iota(jnp.int32, (32, 128), 0)
    qb = 2 * segment_of((r >> 1) & 7, yl, z0 ^ (r >> 4), c) + (r & 1)
    pick = (lax.broadcasted_iota(jnp.int32, (32, 128), 1) == qb).astype(jnp.float32)
    rows = jnp.dot(pick.astype(jnp.bfloat16), mask, preferred_element_type=jnp.float32)
    rows = rows.astype(jnp.bfloat16)

    def spread(block):
        n = block.shape[1]
        one = lax.broadcasted_iota(jnp.int32, (192, n), 0) == jnp.broadcast_to(block, (192, n))
        one = jnp.where(one, 1.0, 0.0).astype(jnp.bfloat16)
        return jnp.dot(rows, one, preferred_element_type=jnp.float32) > 0.5

    for dy, out in enumerate((own_out, near_out)):
        for dc in range(2):
            first = dc * KEYS
            lane = lax.broadcasted_iota(jnp.int32, (1, 1024), 1)
            b = (lane >> 6) & 1
            kb = 2 * segment_of(lane >> 7, yl ^ dy, z0, c ^ dc) + b
            ok = spread(kb + 64).astype(jnp.int32)
            q_full = jnp.broadcast_to(qb[:, :1], (32, 1024))
            k_full = jnp.broadcast_to(kb, (32, 1024))
            ok = ((k_full < q_full) & (ok != 0)) | (k_full == q_full)
            out[:, first:first + 1024] = jnp.where(ok, 0.0, neg_large)
            lane = lax.broadcasted_iota(jnp.int32, (1, 512), 1)
            b = (lane >> 6) & 1
            s = (yl ^ dy) * 16 + (j ^ (lane >> 7)) * 4 + z0 * 2 + (c ^ dc)
            ok = spread(2 * s + b)
            out[:, first + 1024:first + KEYS] = jnp.where(ok, 0.0, neg_large)


def score_tile(q, keys):
    return lax.dot_general(
        q, keys, (((1,), (1,)), ((), ())), preferred_element_type=jnp.float32
    )


def lane_sums(p):
    total = p[:, :HD]
    for i in range(1, p.shape[1] // HD):
        total = total + p[:, i * HD:(i + 1) * HD]
    return total


def fold(state, q, keys, values, bias_ref, block, lanes, causal=None):
    top, total, acc = state
    raw = score_tile(q, keys) * score_scale
    parts = []
    for i in range(q.shape[0] // 64):
        parts.append(raw[i * 64:(i + 1) * 64] + bias_ref[pl.ds(block + i, 1), lanes])
    s = jnp.concatenate(parts, axis=0)
    if causal is not None:
        s = s + causal
    new_top = jnp.maximum(top, jnp.max(s, axis=1, keepdims=True))
    factor = jnp.exp2(top - new_top)
    p = jnp.exp2(s - new_top[:, :1])
    total = total * factor + lane_sums(p)
    acc = acc * factor + jnp.dot(
        p.astype(jnp.bfloat16), values, preferred_element_type=jnp.float32
    )
    return new_top, total, acc


def fresh(rows):
    return (
        jnp.full((rows, HD), neg_large, jnp.float32),
        jnp.zeros((rows, HD), jnp.float32),
        jnp.zeros((rows, HD), jnp.float32),
    )


def fold_range(state, q, kv_ref, bias_ref, block, dc, first, causal=None):
    keys = slice(first, first + 512)
    lanes = slice(dc * KEYS + first, dc * KEYS + first + 512)
    return fold(
        state, q, kv_ref[0, keys, :], kv_ref[1, keys, :], bias_ref, block, lanes, causal
    )


def own_kernel(q0_ref, q1_ref, kv0_ref, kv1_ref, bias_ref, top_out, total_out, acc_out):
    for tile in range(4):
        q_ref = (q0_ref, q1_ref)[tile // 2]
        high = tile % 2
        q = q_ref[high * 512:(high + 1) * 512, :]
        state = fresh(512)
        for dc, kv_ref in enumerate((kv0_ref, kv1_ref)):
            for first in (0, 512, 1024):
                if first == 512 and not high:
                    continue
                causal = None
                if tile < 2 and dc == 0 and first == high * 512:
                    row = lax.broadcasted_iota(jnp.int32, (512, 512), 0)
                    col = lax.broadcasted_iota(jnp.int32, (512, 512), 1)
                    causal = jnp.where(col <= row, 0.0, neg_large)
                state = fold_range(state, q, kv_ref, bias_ref, tile * 8, dc, first, causal)
        rows = slice(tile * 512, (tile + 1) * 512)
        top_out[rows, :], total_out[rows, :], acc_out[rows, :] = state


def near_fold(where_ref, which, q_ref, kv_refs, bias_ref, refs, top, total, acc):
    yl = where_ref[0]
    for high in range(2):
        rows = slice(high * 512, (high + 1) * 512)
        state_rows = slice(which * 1024 + high * 512, which * 1024 + (high + 1) * 512)
        q = q_ref[rows, :]
        block = which * 16 + high * 8
        state = tuple(ref[state_rows, :] for ref in refs)
        for dc, kv_ref in enumerate(kv_refs):
            for first in (0, 1024) if high else (1024,):
                state = fold_range(state, q, kv_ref, bias_ref, block, dc, first)
        top[rows, :], total[rows, :], acc[rows, :] = state

        @pl.when(yl == 1 - high)
        def _():
            state = top[rows, :], total[rows, :], acc[rows, :]
            for dc, kv_ref in enumerate(kv_refs):
                state = fold_range(state, q, kv_ref, bias_ref, block, dc, high * 512)
            top[rows, :], total[rows, :], acc[rows, :] = state


def to_row(column):
    row = lax.broadcasted_iota(jnp.int32, (128, HD), 0)
    col = lax.broadcasted_iota(jnp.int32, (128, HD), 1)
    return jnp.sum(jnp.where(row == col, column, 0.0), axis=0, keepdims=True)


def to_column(line):
    row = lax.broadcasted_iota(jnp.int32, (128, HD), 0)
    col = lax.broadcasted_iota(jnp.int32, (128, HD), 1)
    return jnp.sum(jnp.where(row == col, line, 0.0), axis=1, keepdims=True)


def near_partner_kernel(
    where_ref, q_ref, kv0_ref, kv1_ref, bias_ref, t_ref, l_ref, a_ref, part_out, stats_out,
    top, total, acc,
):
    near_fold(
        where_ref, 1, q_ref, (kv0_ref, kv1_ref), bias_ref, (t_ref, l_ref, a_ref), top, total, acc
    )
    for t in range(8):
        rows = slice(t * 128, (t + 1) * 128)
        weight = jnp.sum(total[rows, :], axis=1, keepdims=True)
        part_out[rows, :] = (acc[rows, :] / weight).astype(jnp.bfloat16)
        stats_out[t:t + 1, :] = to_row(top[rows, :])
        stats_out[8 + t:9 + t, :] = to_row(jnp.broadcast_to(weight, (128, HD)))


def near_own_kernel(
    where_ref, q_ref, kv0_ref, kv1_ref, bias_ref, t_ref, l_ref, a_ref, top, total, acc
):
    near_fold(
        where_ref, 0, q_ref, (kv0_ref, kv1_ref), bias_ref, (t_ref, l_ref, a_ref), top, total, acc
    )


def combine_kernel(where_ref, top, total, acc, part_ref, stats_ref, extra_ref, out_ref):
    j = where_ref[1]
    for t in range(8):
        rows = slice(t * 128, (t + 1) * 128)
        other_top = to_column(stats_ref[t:t + 1, :])
        other_weight = to_column(stats_ref[8 + t:9 + t, :])
        best = jnp.maximum(top[rows, :], other_top)
        factor = jnp.exp2(top[rows, :] - best)
        other = jnp.exp2(other_top - best) * other_weight
        weight = jnp.sum(total[rows, :], axis=1, keepdims=True) * factor + other
        own = acc[rows, :] * factor + part_ref[rows, :].astype(jnp.float32) * other
        mixed = (own / weight + extra_ref[rows, :]).astype(jnp.bfloat16)
        to = t if t < 4 else 7 - t
        half = t // 4
        out_ref[j ^ to, half * 128:(half + 1) * 128, :] = mixed


def memory_kernel(where_ref, len_ref, gate_ref, q_ref, audio_ref, video_ref, out_ref):
    j = where_ref[1]
    slot = lax.broadcasted_iota(jnp.int32, (1, 512), 1)

    def step(w, _):
        rows = pl.ds(pl.multiple_of(w * 512, 512), 512)
        q = q_ref[rows, :]
        mixed = jnp.zeros((512, HD), jnp.float32)
        for n, mem_ref in enumerate((audio_ref, video_ref)):
            bias = jnp.where(slot < len_ref[n], 0.0, neg_large)
            s = score_tile(q, mem_ref[0]) * score_scale + bias
            p = jnp.exp2(s - jnp.max(s, axis=1, keepdims=True))
            total = jnp.sum(p, axis=1, keepdims=True)
            part = jnp.dot(
                p.astype(jnp.bfloat16), mem_ref[1], preferred_element_type=jnp.float32
            )
            gate = jnp.tanh(jnp.full((1, HD), gate_ref[n, j], jnp.float32))
            mixed = mixed + gate * (part / total)
        out_ref[rows, :] = mixed
        return 0

    lax.fori_loop(0, 2, step, 0)


def project_kernel(where_ref, m0, m1, m2, m3, w_ref, out_ref, mixed):
    j = where_ref[1]

    @pl.when(pl.program_id(0) == 0)
    def _():
        for k, m in enumerate((m0, m1, m2, m3)):
            mixed[:, pl.ds(pl.multiple_of((j ^ k) * HD, HD), HD)] = m[...]

    part = jnp.dot(mixed[...], w_ref[...], preferred_element_type=jnp.float32)
    part = part.astype(jnp.bfloat16)
    for h in range(8):
        out_ref[h] = part[h * 32:(h + 1) * 32]


def cost(us):
    return pl.CostEstimate(flops=int(us * 1.15e9), bytes_accessed=2**20, transcendentals=0)


def f32(*shape):
    return jax.ShapeDtypeStruct(shape, jnp.float32)


def b16(*shape):
    return jax.ShapeDtypeStruct(shape, jnp.bfloat16)


def shards(
    span_qkv, cache_kv, audio_kv, video_kv, block_mask, mem_lengths, cross_gates, out_weight
):
    j = lax.axis_index("z2") * 2 + lax.axis_index("z1")
    where = jnp.stack(
        [lax.axis_index("yl"), j, lax.axis_index("z0"), lax.axis_index("c")]
    ).astype(jnp.int32)

    span_packed, cache_packed = pl.pallas_call(
        pack_kernel,
        out_shape=(b16(32, 3, 32, HD), b16(4, 2, 128, HD)),
        in_specs=[scalars(), anywhere(), anywhere()],
        out_specs=(anywhere(), anywhere()),
        scratch_shapes=[pltpu.SemaphoreType.DMA((36,))],
        compiler_params=params(),
        cost_estimate=cost(2),
        name="pack",
    )(where, span_qkv, cache_kv)

    cache_own = [cache_packed[0]] + [
        lax.ppermute(cache_packed[k], ZZ, xor_perm(4, k)) for k in range(1, 4)
    ]
    got = lax.all_to_all(span_packed, ZZ + HEADS, split_axis=0, concat_axis=0, tiled=True)

    def swap(part, axis):
        return lax.ppermute(part, axis, xor_perm(2, 1))

    queries, kv_own = pl.pallas_call(
        unpack_kernel,
        out_shape=(b16(1024, HD), b16(2, KEYS, HD)),
        in_specs=[whole()] * 5,
        out_specs=(whole(), whole()),
        compiler_params=params(),
        cost_estimate=cost(1),
        name="unpack",
    )(got, *cache_own)
    kv_near = swap(kv_own, "yl")
    partner_queries = swap(queries, "z0")
    kv_sibling = swap(kv_own, "c")
    kv_near_sibling = swap(kv_near, "c")

    own_bias, near_bias = pl.pallas_call(
        bias_kernel,
        out_shape=(f32(32, 2 * KEYS),) * 2,
        in_specs=[scalars(), whole()],
        out_specs=(whole(),) * 2,
        compiler_params=params(),
        cost_estimate=cost(2),
        name="bias",
    )(where, block_mask)

    extra = pl.pallas_call(
        memory_kernel,
        grid_spec=pltpu.PrefetchScalarGridSpec(
            num_scalar_prefetch=1,
            grid=(1,),
            in_specs=[
                scalars(),
                scalars(),
                pl.BlockSpec((1024, HD), lambda i, where: (0, 0)),
                pl.BlockSpec((2, 512, HD), lambda i, where: (0, 0, where[1])),
                pl.BlockSpec((2, 512, HD), lambda i, where: (0, 0, where[1])),
            ],
            out_specs=pl.BlockSpec((1024, HD), lambda i, where: (0, 0)),
        ),
        out_shape=f32(1024, HD),
        compiler_params=params(),
        cost_estimate=cost(3),
        name="memories",
    )(where, mem_lengths, cross_gates, queries, audio_kv, video_kv)

    state = pl.pallas_call(
        own_kernel,
        out_shape=(f32(2048, HD),) * 3,
        in_specs=[whole()] * 5,
        out_specs=(whole(),) * 3,
        compiler_params=params(),
        cost_estimate=cost(8),
        name="own_keys",
    )(queries, partner_queries, kv_own, kv_sibling, own_bias)

    part, stats = pl.pallas_call(
        near_partner_kernel,
        out_shape=(b16(1024, HD), f32(16, HD)),
        in_specs=[scalars()] + [whole()] * 7,
        out_specs=(whole(),) * 2,
        scratch_shapes=[pltpu.VMEM((1024, HD), jnp.float32)] * 3,
        compiler_params=params(),
        cost_estimate=cost(4),
        name="near_keys_partner",
    )(where, partner_queries, kv_near, kv_near_sibling, near_bias, *state)
    part = swap(part, "z0")
    stats = swap(stats, "z0")
    state = pl.pallas_call(
        near_own_kernel,
        out_shape=(f32(1024, HD),) * 3,
        in_specs=[scalars()] + [whole()] * 7,
        out_specs=(whole(),) * 3,
        compiler_params=params(),
        cost_estimate=cost(4),
        name="near_keys_own",
    )(where, queries, kv_near, kv_near_sibling, near_bias, *state)
    state = pl.pallas_call(
        combine_kernel,
        out_shape=b16(4, 256, HD),
        in_specs=[scalars()] + [whole()] * 6,
        out_specs=whole(),
        compiler_params=params(),
        cost_estimate=cost(1),
        name="combine",
    )(where, *state, part, stats, extra)

    mixed = [state[0]] + [lax.ppermute(state[k], ZZ, xor_perm(4, k)) for k in range(1, 4)]
    partial_sums = pl.pallas_call(
        project_kernel,
        grid=(4,),
        out_shape=b16(8, 32, 4096),
        in_specs=[scalars()]
        + [pl.BlockSpec((256, HD), lambda i: (0, 0))] * 4
        + [pl.BlockSpec((512, 1024), lambda i: (0, i))],
        out_specs=pl.BlockSpec((8, 32, 1024), lambda i: (0, 0, i)),
        scratch_shapes=[pltpu.VMEM((256, 512), jnp.bfloat16)],
        compiler_params=params(),
        cost_estimate=cost(3),
        name="project",
    )(where, *mixed, out_weight)
    gathered = lax.all_to_all(partial_sums, HEADS, split_axis=0, concat_axis=0, tiled=True)
    return jnp.sum(gathered.astype(jnp.float32), axis=0).astype(jnp.bfloat16)


def solution(mesh):
    fine = Mesh(mesh.devices.reshape(SIZES), AXES)
    seq = ("yl", "z2", "z1", "z0", "c")
    placed = (
        P(None, seq + HEADS, None),
        P(None, seq, HEADS),
        P(None, None, HEADS),
        P(None, None, HEADS),
        P(HEADS, None, None),
        P(),
        P(None, HEADS),
        P(HEADS, None),
    )
    return jax.shard_map(
        shards, mesh=fine, in_specs=placed, out_specs=P(seq + HEADS, None), check_vma=False
    )
```

time: 179 us -> 138 us (0.77)
  Pallas kernels: 48 us -> 31.9 us
  waiting for transfers between devices: 51.6 us -> 38.4 us
  starting transfers between devices: 35.8 us -> 29.2 us
  local copies, waits for them, and re-layouts: 5.44 us -> 2.3 us
    pallas_call x7 -> x6, Pallas kernels: 40.5 us -> 24.1 us  [the longest x1 8.51 us: shards(): pl.pallas_call(own_kernel, out_shape=(f32(2048, HD),) * 3, in_specs=[whol...]
    ppermute x14 -> x6, waiting for transfers between devices: 25.8 us -> 10.2 us  [swap(): return lax.ppermute(part, axis, xor_perm(2, 1))]
    ppermute x14 -> x6, starting transfers between devices: 9.42 us -> 2.97 us  [swap(): return lax.ppermute(part, axis, xor_perm(2, 1))]
    all_to_all x1, waiting for transfers between devices: 0.01 us -> 3.62 us  [shards(): lax.all_to_all(span_packed, ZZ + HEADS, split_axis=0, concat_axis=0, tile...]
    unnamed x25 -> x17, local copies, waits for them, and re-layouts: 5.4 us -> 2.26 us
  transfers between devices with their start and end apart: 21 -> 13, of which waited for: 11 -> 8; matrix products, arithmetic and copies ran while one was open for 1% -> 0% of each run, Pallas kernels for 21% -> 14%
where the time goes in v2:
time: 138 us; the launch traced here: 137 us
  waiting for transfers between devices  38.4 us (28%)
  blocking collectives  34 us (25%)
  Pallas kernels  31.9 us (23%)
  starting transfers between devices  29.2 us (21%)
  local copies, waits for them, and re-layouts  2.3 us (2%)
    all_to_all x1, blocking collectives, shards(): lax.all_to_all(partial_sums, HEADS, split_axis=0, concat_axis=0, tiled=True)  34 us
    ppermute x3, waiting for transfers between devices, shards(): lax.ppermute(cache_packed[k], ZZ, xor_perm(4, k))  19.3 us
    all_to_all x1, starting transfers between devices, shards(): lax.all_to_all(span_packed, ZZ + HEADS, split_axis=0, concat_axis=0, tile...  13.1 us
    ppermute x6, waiting for transfers between devices, swap(): return lax.ppermute(part, axis, xor_perm(2, 1))  10.2 us
    pallas_call x1, Pallas kernels, shards(): pl.pallas_call(own_kernel, out_shape=(f32(2048, HD),) * 3, in_specs=[whol...  8.51 us
    pallas_call x1, Pallas kernels, shards(): pl.pallas_call(near_partner_kernel, out_shape=(b16(1024, HD), f32(16, HD)...  6.67 us
    ppermute x3, starting transfers between devices, shards(): lax.ppermute(state[k], ZZ, xor_perm(4, k))  6.58 us
    ppermute x3, starting transfers between devices, shards(): lax.ppermute(cache_packed[k], ZZ, xor_perm(4, k))  6.58 us
  transfers between devices with their start and end apart: 13, of which 8 were waited for; matrix products, arithmetic and copies ran while one was open for 0% of the time, Pallas kernels for 14%

profile of v2, /device:TPU:32, one launch (start us, length us, event | category | flops | bytes accessed | tf_op | source)
XLA Modules:
  0.0 137.1 jit_solution(9470644223251069254)
XLA Ops:
  0.0 0.1 pad_add_fusion.where_ref
  0.1 0.0 copy-start.3
  0.1 1.1 copy-done.3
  1.2 0.0 copy-start.4
  1.2 0.9 copy-done.4
  2.2 1.8 %pack.1 = (bf16[32,3,32,128]{3,2,1,0:T(8,128)(2,1)}, bf16[4,2,128,128]{3,2,1,0:T(8,128)(2,1)S(1)}) custom-call(s32[4]{0:T(128)S(1)} %pad_add_fusion.where_ref, bf16[3,32,4096]{2,1,0:T(8,128)(2,1)S(1)} %copy-done.3, bf16[2,128,512]{2,1,0:T(8,128)(2,1)S(1)} %copy-done.4), custom_call_target="tpu_custom_call" | custom-call | flops 2300000000 | bytes 1048576 | tf_op jit(solution)/shard_map/pack/pallas_call | solution.py:301
  4.0 13.1 %all-to-all-start = ((bf16[32,3,32,128]{3,2,1,0:T(8,128)(2,1)}), bf16[32,3,32,128]{3,2,1,0:T(8,128)(2,1)S(1)}, u32[]{:S(2)}, u32[]{:S(2)}) async-start(bf16[32,3,32,128]{3,2,1,0:T(8,128)(2,1)} %get-tuple-element.19), calls=%async_computation | async-start | bytes 1572864 | tf_op jit(solution)/shard_map/all_to_all | solution.py:315
  17.1 2.8 %collective-permute-start = (bf16[2,128,128]{2,1,0:T(8,128)(2,1)S(1)}, bf16[2,128,128]{2,1,0:T(8,128)(2,1)S(1)}, u32[]{:S(2)}, u32[]{:S(2)}) collective-permute-start(bf16[2,128,128]{2,1,0:T(8,128)(2,1)S(1)} %get-tuple-element.39), channel_id=1, source_target_pairs={{0,32},{32,0},{64,96},{96,64},{1,33},{33,1},{65,97},{97,65},{2,34}... | collective-permute-start | bytes 196616 | tf_op jit(solution)/shard_map/ppermute | solution.py:313
  19.8 3.6 %collective-permute-start.1 = (bf16[2,128,128]{2,1,0:T(8,128)(2,1)S(1)}, bf16[2,128,128]{2,1,0:T(8,128)(2,1)S(1)}, u32[]{:S(2)}, u32[]{:S(2)}) collective-permute-start(bf16[2,128,128]{2,1,0:T(8,128)(2,1)S(1)} %get-tuple-element.38), channel_id=1, source_target_pairs={{0,64},{32,96},{64,0},{96,32},{1,65},{33,97},{65,1},{97,33},{2,66}... | collective-permute-start | bytes 196616 | tf_op jit(solution)/shard_map/ppermute | solution.py:313
  23.5 0.2 collective-permute-start.2
  23.7 15.8 %collective-permute-done.c1_ref = bf16[2,128,128]{2,1,0:T(8,128)(2,1)S(1)} collective-permute-done((bf16[2,128,128]{2,1,0:T(8,128)(2,1)S(1)}, bf16[2,128,128]{2,1,0:T(8,128)(2,1)S(1)}, u32[]{:S(2)}, u32[]{:S(2)}) %collective-permute-start) | collective-permute-done | bytes 65568 | tf_op jit(solution)/shard_map/ppermute | solution.py:313
  39.5 2.2 %collective-permute-done.1.c2_ref = bf16[2,128,128]{2,1,0:T(8,128)(2,1)S(1)} collective-permute-done((bf16[2,128,128]{2,1,0:T(8,128)(2,1)S(1)}, bf16[2,128,128]{2,1,0:T(8,128)(2,1)S(1)}, u32[]{:S(2)}, u32[]{:S(2)}) %collective-permute-start.1) | collective-permute-done | bytes 65568 | tf_op jit(solution)/shard_map/ppermute | solution.py:313
  41.7 1.3 collective-permute-done.2.c3_ref
  43.0 3.6 %all-to-all-done.got_ref = bf16[32,3,32,128]{3,2,1,0:T(8,128)(2,1)S(1)} async-done(((bf16[32,3,32,128]{3,2,1,0:T(8,128)(2,1)}), bf16[32,3,32,128]{3,2,1,0:T(8,128)(2,1)S(1)}, u32[]{:S(2)}, u32[]{:S(2)}) %all-to-all-start) | async-done | bytes 786464 | tf_op jit(solution)/shard_map/all_to_all | solution.py:315
  46.6 0.0 copy-start.7
  46.6 0.1 unpack.1
  46.7 0.8 collective-permute-start.3
  47.4 0.0 collective-permute-start.6
  47.4 0.1 copy-done.7
  47.5 0.1 copy.9.mask_ref
  47.6 0.0 copy-start.1
  47.6 0.0 copy-start.2
  47.6 0.0 copy-start.5
  47.6 0.0 copy-start.6
  47.6 1.5 %bias.1 = (f32[32,3072]{1,0:T(8,128)S(1)}, f32[32,3072]{1,0:T(8,128)S(1)}) custom-call(s32[4]{0:T(128)S(1)} %pad_add_fusion.where_ref, s32[1,128,192]{2,1,0:T(8,128)S(1)} %copy.9.mask_ref), custom_call_target="tpu_custom_call" | custom-call | flops 2300000000 | bytes 1048576 | tf_op jit(solution)/shard_map/bias/pallas_call | solution.py:334
  49.2 0.1 collective-permute-start.5
  49.3 0.0 copy-done.1
  49.3 0.0 copy-done.2
  49.3 0.0 copy-done.5
  49.3 0.0 copy-done.6
  49.3 3.2 %memories.1.extra_ref = f32[1024,128]{1,0:T(8,128)S(1)} custom-call(s32[4]{0:T(128)S(1)} %pad_add_fusion.where_ref, s32[2]{0:T(128)S(1)} %copy-done.6, f32[2,4]{1,0:T(2,128)S(1)} %copy-done.5, bf16[1024,128]{1,0:T(8,128)(2,1)S(1)} %get-tuple-element.21.q0_ref.q_ref, bf16[2,512,512]{2,1,0:T(8,128)(2,1)S(1)} %copy-done.1, bf16[2,512,512]{2,1,0:T(8,128)(2,1)S(1)} %copy-done.2), custom_call_target="tpu_custom_call" | custom-call | flops 3449999872 | bytes 1048576 | tf_op jit(solution)/shard_map/memories/pallas_call | solution.py:344
  52.6 9.6 %collective-permute-done.3.kv0_ref = bf16[2,1536,128]{2,1,0:T(8,128)(2,1)S(1)} collective-permute-done((bf16[2,1536,128]{2,1,0:T(8,128)(2,1)S(1)}, bf16[2,1536,128]{2,1,0:T(8,128)(2,1)S(1)}, u32[]{:S(2)}, u32[]{:S(2)}) %collective-permute-start.3) | collective-permute-done | bytes 786464 | tf_op jit(solution)/shard_map/ppermute | solution.py:318
  62.1 0.0 collective-permute-start.4
  62.2 0.0 collective-permute-done.5.q1_ref.q_ref
  62.2 0.0 collective-permute-done.6.kv1_ref
  62.2 8.5 %own_keys.1 = (f32[2048,128]{1,0:T(8,128)S(1)}, f32[2048,128]{1,0:T(8,128)S(1)}, f32[2048,128]{1,0:T(8,128)S(1)}) custom-call(bf16[1024,128]{1,0:T(8,128)(2,1)S(1)} %get-tuple-element.21.q0_ref.q_ref, bf16[1024,128]{1,0:T(8,128)(2,1)S(1)} %collective-permute-done.5.q1_ref.q_ref, bf16[2,1536,128]{2,1,0:T(8,128)(2,1)S(1)} %get-tuple-element.22.kv0_ref, ...), custom_call_target="tpu_custom_call" | custom-call | flops 9200000000 | bytes 1048576 | tf_op jit(solution)/shard_map/own_keys/pallas_call | solution.py:364
  70.7 0.0 collective-permute-done.4.kv1_ref
  70.7 6.7 %near_keys_partner.1 = (bf16[1024,128]{1,0:T(8,128)(2,1)S(1)}, f32[16,128]{1,0:T(8,128)S(1)}) custom-call(s32[4]{0:T(128)S(1)} %pad_add_fusion.where_ref, bf16[1024,128]{1,0:T(8,128)(2,1)S(1)} %collective-permute-done.5.q1_ref.q_ref, bf16[2,1536,128]{2,1,0:T(8,128)(2,1)S(1)} %collective-permute-done.3.kv0_ref, ...), custom_call_target="tpu_custom_call" | custom-call | flops 4600000000 | bytes 1048576 | tf_op jit(solution)/shard_map/near_keys_partner/pallas_call | solution.py:374
  77.4 0.6 collective-permute-start.7
  77.9 1.5 %collective-permute-start.8 = (f32[16,128]{1,0:T(8,128)S(1)}, f32[16,128]{1,0:T(8,128)S(1)}, u32[]{:S(2)}, u32[]{:S(2)}) collective-permute-start(f32[16,128]{1,0:T(8,128)S(1)} %get-tuple-element.32), channel_id=1, source_target_pairs={{0,16},{16,0},{1,17},{17,1},{2,18},{18,2},{3,19},{19,3},{4,20},{20... | collective-permute-start | bytes 24584 | tf_op jit(solution)/shard_map/ppermute | solution.py:318
  79.5 6.3 %near_keys_own.1 = (f32[1024,128]{1,0:T(8,128)S(1)}, f32[1024,128]{1,0:T(8,128)S(1)}, f32[1024,128]{1,0:T(8,128)S(1)}) custom-call(s32[4]{0:T(128)S(1)} %pad_add_fusion.where_ref, bf16[1024,128]{1,0:T(8,128)(2,1)S(1)} %get-tuple-element.21.q0_ref.q_ref, bf16[2,1536,128]{2,1,0:T(8,128)(2,1)S(1)} %collective-permute-done.3.kv0_ref, ...), custom_call_target="tpu_custom_call" | custom-call | flops 4600000000 | bytes 1048576 | tf_op jit(solution)/shard_map/near_keys_own/pallas_call | solution.py:386
  85.7 0.6 collective-permute-done.8.stats_ref
  86.3 0.0 collective-permute-done.7.part_ref
  86.3 0.0 copy-start
  86.3 1.1 combine.1
  87.4 3.1 %collective-permute-start.10 = (bf16[256,128]{1,0:T(8,128)(2,1)S(1)}, bf16[256,128]{1,0:T(8,128)(2,1)S(1)}, u32[]{:S(2)}, u32[]{:S(2)}) collective-permute-start(bf16[256,128]{1,0:T(8,128)(2,1)S(1)} %get-tuple-element.34), channel_id=1, source_target_pairs={{0,64},{32,96},{64,0},{96,32},{1,65},{33,97},{65,1},{97,33},{2,66}... | collective-permute-start | bytes 196616 | tf_op jit(solution)/shard_map/ppermute | solution.py:405
  90.5 2.0 %collective-permute-start.11 = (bf16[256,128]{1,0:T(8,128)(2,1)S(1)}, bf16[256,128]{1,0:T(8,128)(2,1)S(1)}, u32[]{:S(2)}, u32[]{:S(2)}) collective-permute-start(bf16[256,128]{1,0:T(8,128)(2,1)S(1)} %get-tuple-element.33), channel_id=1, source_target_pairs={{0,96},{32,64},{64,32},{96,0},{1,97},{33,65},{65,33},{97,1},{2,98}... | collective-permute-start | bytes 196616 | tf_op jit(solution)/shard_map/ppermute | solution.py:405
  92.5 1.5 %collective-permute-start.9 = (bf16[256,128]{1,0:T(8,128)(2,1)S(1)}, bf16[256,128]{1,0:T(8,128)(2,1)S(1)}, u32[]{:S(2)}, u32[]{:S(2)}) collective-permute-start(bf16[256,128]{1,0:T(8,128)(2,1)S(1)} %get-tuple-element.35), channel_id=1, source_target_pairs={{0,32},{32,0},{64,96},{96,64},{1,33},{33,1},{65,97},{97,65},{2,34}... | collective-permute-start | bytes 196616 | tf_op jit(solution)/shard_map/ppermute | solution.py:405
  94.0 2.6 %collective-permute-done.10.m2 = bf16[256,128]{1,0:T(8,128)(2,1)S(1)} collective-permute-done((bf16[256,128]{1,0:T(8,128)(2,1)S(1)}, bf16[256,128]{1,0:T(8,128)(2,1)S(1)}, u32[]{:S(2)}, u32[]{:S(2)}) %collective-permute-start.10) | collective-permute-done | bytes 65568 | tf_op jit(solution)/shard_map/ppermute | solution.py:405
  96.6 2.6 %collective-permute-done.11.m3 = bf16[256,128]{1,0:T(8,128)(2,1)S(1)} collective-permute-done((bf16[256,128]{1,0:T(8,128)(2,1)S(1)}, bf16[256,128]{1,0:T(8,128)(2,1)S(1)}, u32[]{:S(2)}, u32[]{:S(2)}) %collective-permute-start.11) | collective-permute-done | bytes 65568 | tf_op jit(solution)/shard_map/ppermute | solution.py:405
  99.3 0.0 collective-permute-done.9.m1
  99.3 0.0 copy-done
  99.3 2.7 %project.1 = bf16[8,32,4096]{2,1,0:T(8,128)(2,1)S(1)} custom-call(s32[4]{0:T(128)S(1)} %pad_add_fusion.where_ref, bf16[256,128]{1,0:T(8,128)(2,1)S(1)} %get-tuple-element.36.m0, bf16[256,128]{1,0:T(8,128)(2,1)S(1)} %collective-permute-done.9.m1, bf16[256,128]{1,0:T(8,128)(2,1)S(1)} %collective-permute-done.10.m2, ...), custom_call_target="tpu_custom_call" | custom-call | flops 3449999872 | bytes 1048576 | tf_op jit(solution)/shard_map/project/pallas_call | solution.py:406
  102.0 34.0 %all_to_all.10 = bf16[8,32,4096]{2,1,0:T(8,128)(2,1)S(1)} all-to-all(bf16[8,32,4096]{2,1,0:T(8,128)(2,1)S(1)} %project.1), channel_id=1, replica_groups=mesh['yl'=2,'z2'=2,'z1'=2,'z0'=2,'c'=2,'x'=4,'yh'=2] {'x','yh'}, dimensions={0} | all-to-all | bytes 4194304 | tf_op jit(solution)/shard_map/all_to_all | solution.py:419
  136.0 1.1 reduce_sum.12
  (2 shorter events, 0.0 us)
Async XLA Ops:
  0.1 1.1 copy-start.3
  1.2 0.9 copy-start.4
  4.0 42.6 %all-to-all-start = ((bf16[32,3,32,128]{3,2,1,0:T(8,128)(2,1)}), bf16[32,3,32,128]{3,2,1,0:T(8,128)(2,1)S(1)}, u32[]{:S(2)}, u32[]{:S(2)}) async-start(bf16[32,3,32,128]{3,2,1,0:T(8,128)(2,1)} %get-tuple-element.19), calls=%async_computation | async-start | bytes 1572864 | tf_op jit(solution)/shard_map/all_to_all | solution.py:315
  17.1 22.4 %collective-permute-start = (bf16[2,128,128]{2,1,0:T(8,128)(2,1)S(1)}, bf16[2,128,128]{2,1,0:T(8,128)(2,1)S(1)}, u32[]{:S(2)}, u32[]{:S(2)}) collective-permute-start(bf16[2,128,128]{2,1,0:T(8,128)(2,1)S(1)} %get-tuple-element.39), channel_id=1, source_target_pairs={{0,32},{32,0},{64,96},{96,64},{1,33},{33,1},{65,97},{97,65},{2,34}... | collective-permute-start | bytes 196616 | tf_op jit(solution)/shard_map/ppermute | solution.py:313
  19.8 21.9 %collective-permute-start.1 = (bf16[2,128,128]{2,1,0:T(8,128)(2,1)S(1)}, bf16[2,128,128]{2,1,0:T(8,128)(2,1)S(1)}, u32[]{:S(2)}, u32[]{:S(2)}) collective-permute-start(bf16[2,128,128]{2,1,0:T(8,128)(2,1)S(1)} %get-tuple-element.38), channel_id=1, source_target_pairs={{0,64},{32,96},{64,0},{96,32},{1,65},{33,97},{65,1},{97,33},{2,66}... | collective-permute-start | bytes 196616 | tf_op jit(solution)/shard_map/ppermute | solution.py:313
  23.5 19.5 %collective-permute-start.2 = (bf16[2,128,128]{2,1,0:T(8,128)(2,1)S(1)}, bf16[2,128,128]{2,1,0:T(8,128)(2,1)S(1)}, u32[]{:S(2)}, u32[]{:S(2)}) collective-permute-start(bf16[2,128,128]{2,1,0:T(8,128)(2,1)S(1)} %get-tuple-element.37), channel_id=1, source_target_pairs={{0,96},{32,64},{64,32},{96,0},{1,97},{33,65},{65,33},{97,1},{2,98}... | collective-permute-start | bytes 196616 | tf_op jit(solution)/shard_map/ppermute | solution.py:313
  46.6 0.9 copy-start.7
  46.7 15.5 %collective-permute-start.3 = (bf16[2,1536,128]{2,1,0:T(8,128)(2,1)S(1)}, bf16[2,1536,128]{2,1,0:T(8,128)(2,1)S(1)}, u32[]{:S(2)}, u32[]{:S(2)}) collective-permute-start(bf16[2,1536,128]{2,1,0:T(8,128)(2,1)S(1)} %get-tuple-element.22.kv0_ref), channel_id=1, source_target_pairs={{0,128},{128,0},{1,129},{129,1},{2,130},{130,2},{3,131},{131,3},{4... | collective-permute-start | bytes 2359304 | tf_op jit(solution)/shard_map/ppermute | solution.py:318
  47.4 14.7 %collective-permute-start.6 = (bf16[2,1536,128]{2,1,0:T(8,128)(2,1)S(1)}, bf16[2,1536,128]{2,1,0:T(8,128)(2,1)S(1)}, u32[]{:S(2)}, u32[]{:S(2)}) collective-permute-start(bf16[2,1536,128]{2,1,0:T(8,128)(2,1)S(1)} %get-tuple-element.22.kv0_ref), channel_id=1, source_target_pairs={{0,8},{8,0},{1,9},{9,1},{2,10},{10,2},{3,11},{11,3},{4,12},{12,4},... | collective-permute-start | bytes 2359304 | tf_op jit(solution)/shard_map/ppermute | solution.py:318
  47.6 1.7 %copy-start.1 = (bf16[2,512,512]{2,1,0:T(8,128)(2,1)S(1)}, bf16[2,512,512]{2,1,0:T(8,128)(2,1)}, u32[]{:S(2)}) copy-start(bf16[2,512,512]{2,1,0:T(8,128)(2,1)} %audio_ref.1) | copy-start | bytes 3145732
  47.6 1.7 %copy-start.2 = (bf16[2,512,512]{2,1,0:T(8,128)(2,1)S(1)}, bf16[2,512,512]{2,1,0:T(8,128)(2,1)}, u32[]{:S(2)}) copy-start(bf16[2,512,512]{2,1,0:T(8,128)(2,1)} %video_ref.1) | copy-start | bytes 3145732
  47.6 1.7 %copy-start.5 = (f32[2,4]{1,0:T(2,128)S(1)}, f32[2,4]{1,0:T(2,128)}, u32[]{:S(2)}) copy-start(f32[2,4]{1,0:T(2,128)} %gate_ref.1) | copy-start | bytes 100
  47.6 1.7 %copy-start.6 = (s32[2]{0:T(128)S(1)}, s32[2]{0:T(128)}, u32[]{:S(2)}) copy-start(s32[2]{0:T(128)} %len_ref.1) | copy-start | bytes 28
  49.2 13.0 %collective-permute-start.5 = (bf16[1024,128]{1,0:T(8,128)(2,1)S(1)}, bf16[1024,128]{1,0:T(8,128)(2,1)S(1)}, u32[]{:S(2)}, u32[]{:S(2)}) collective-permute-start(bf16[1024,128]{1,0:T(8,128)(2,1)S(1)} %get-tuple-element.21.q0_ref.q_ref), channel_id=1, source_target_pairs={{0,16},{16,0},{1,17},{17,1},{2,18},{18,2},{3,19},{19,3},{4,20},{20... | collective-permute-start | bytes 786440 | tf_op jit(solution)/shard_map/ppermute | solution.py:318
  62.1 8.5 %collective-permute-start.4 = (bf16[2,1536,128]{2,1,0:T(8,128)(2,1)S(1)}, bf16[2,1536,128]{2,1,0:T(8,128)(2,1)S(1)}, u32[]{:S(2)}, u32[]{:S(2)}) collective-permute-start(bf16[2,1536,128]{2,1,0:T(8,128)(2,1)S(1)} %collective-permute-done.3.kv0_ref), channel_id=1, source_target_pairs={{0,8},{8,0},{1,9},{9,1},{2,10},{10,2},{3,11},{11,3},{4,12},{12,4},... | collective-permute-start | bytes 2359304 | tf_op jit(solution)/shard_map/ppermute | solution.py:318
  77.4 9.0 %collective-permute-start.7 = (bf16[1024,128]{1,0:T(8,128)(2,1)S(1)}, bf16[1024,128]{1,0:T(8,128)(2,1)S(1)}, u32[]{:S(2)}, u32[]{:S(2)}) collective-permute-start(bf16[1024,128]{1,0:T(8,128)(2,1)S(1)} %get-tuple-element.31), channel_id=1, source_target_pairs={{0,16},{16,0},{1,17},{17,1},{2,18},{18,2},{3,19},{19,3},{4,20},{20... | collective-permute-start | bytes 786440 | tf_op jit(solution)/shard_map/ppermute | solution.py:318
  77.9 8.4 %collective-permute-start.8 = (f32[16,128]{1,0:T(8,128)S(1)}, f32[16,128]{1,0:T(8,128)S(1)}, u32[]{:S(2)}, u32[]{:S(2)}) collective-permute-start(f32[16,128]{1,0:T(8,128)S(1)} %get-tuple-element.32), channel_id=1, source_target_pairs={{0,16},{16,0},{1,17},{17,1},{2,18},{18,2},{3,19},{19,3},{4,20},{20... | collective-permute-start | bytes 24584 | tf_op jit(solution)/shard_map/ppermute | solution.py:318
  86.3 12.9 %copy-start = (bf16[512,4096]{1,0:T(8,128)(2,1)S(1)}, bf16[512,4096]{1,0:T(8,128)(2,1)}, u32[]{:S(2)}) copy-start(bf16[512,4096]{1,0:T(8,128)(2,1)} %w_ref.1) | copy-start | bytes 12582916
  87.4 9.2 %collective-permute-start.10 = (bf16[256,128]{1,0:T(8,128)(2,1)S(1)}, bf16[256,128]{1,0:T(8,128)(2,1)S(1)}, u32[]{:S(2)}, u32[]{:S(2)}) collective-permute-start(bf16[256,128]{1,0:T(8,128)(2,1)S(1)} %get-tuple-element.34), channel_id=1, source_target_pairs={{0,64},{32,96},{64,0},{96,32},{1,65},{33,97},{65,1},{97,33},{2,66}... | collective-permute-start | bytes 196616 | tf_op jit(solution)/shard_map/ppermute | solution.py:405
  90.5 8.8 %collective-permute-start.11 = (bf16[256,128]{1,0:T(8,128)(2,1)S(1)}, bf16[256,128]{1,0:T(8,128)(2,1)S(1)}, u32[]{:S(2)}, u32[]{:S(2)}) collective-permute-start(bf16[256,128]{1,0:T(8,128)(2,1)S(1)} %get-tuple-element.33), channel_id=1, source_target_pairs={{0,96},{32,64},{64,32},{96,0},{1,97},{33,65},{65,33},{97,1},{2,98}... | collective-permute-start | bytes 196616 | tf_op jit(solution)/shard_map/ppermute | solution.py:405
  92.5 6.8 %collective-permute-start.9 = (bf16[256,128]{1,0:T(8,128)(2,1)S(1)}, bf16[256,128]{1,0:T(8,128)(2,1)S(1)}, u32[]{:S(2)}, u32[]{:S(2)}) collective-permute-start(bf16[256,128]{1,0:T(8,128)(2,1)S(1)} %get-tuple-element.35), channel_id=1, source_target_pairs={{0,32},{32,0},{64,96},{96,64},{1,33},{33,1},{65,97},{97,65},{2,34}... | collective-permute-start | bytes 196616 | tf_op jit(solution)/shard_map/ppermute | solution.py:405

commit v3 on v2

v3 whole, which is shorter than its diff:
```python
import functools
import math

import jax
import jax.numpy as jnp
from jax import lax
from jax.experimental import pallas as pl
from jax.experimental.pallas import tpu as pltpu
from jax.sharding import Mesh
from jax.sharding import PartitionSpec as P

HD = 128
KEYS = 1536
neg_large = -1e30
score_scale = math.log2(math.e) / math.sqrt(HD)

AXES = ("yl", "z2", "z1", "z0", "c", "x", "yh")
SIZES = (2, 2, 2, 2, 2, 4, 2)
ZZ = ("z2", "z1")
HEADS = ("x", "yh")

VM = pltpu.VMEM
SM = pltpu.SMEM
whole = functools.partial(pl.BlockSpec, memory_space=VM)
anywhere = functools.partial(pl.BlockSpec, memory_space=pl.ANY)
scalars = functools.partial(pl.BlockSpec, memory_space=SM)


def params(vmem_limit_bytes=24 * 2**20):
    return pltpu.CompilerParams(vmem_limit_bytes=vmem_limit_bytes)


def xor_perm(count, k):
    return [(i, i ^ k) for i in range(count)]


def pack_kernel(where_ref, span_ref, cache_ref, span_out, cache_out):
    j = where_ref[1]
    for k in range(4):
        cache_out[k] = cache_ref[:, :, pl.ds(pl.multiple_of((j ^ k) * HD, HD), HD)]
    for d in range(32):
        col = ((d % 8) * 4 + d // 8) * HD
        span_out[d] = span_ref[:, :, col:col + HD]


def copy_keys(got_ref, cache_refs, kv_out):
    for t in range(8):
        first = (7 - t) * 8 + 4 if t > 3 else t * 8
        rows = slice(t * 128, (t + 1) * 128)
        for n in range(2):
            kv_out[n, rows, :] = got_ref[first:first + 4, 1 + n].reshape(128, HD)
    for k, c_ref in enumerate(cache_refs):
        kv_out[:, 1024 + k * 128:1024 + (k + 1) * 128, :] = c_ref[...]


def unpack_keys_kernel(got_ref, c0_ref, c1_ref, c2_ref, c3_ref, token_ref, kv_out):
    copy_keys(got_ref, (c0_ref, c1_ref, c2_ref, c3_ref), kv_out)


def unpack_rest_kernel(
    got_ref, c0_ref, c1_ref, c2_ref, c3_ref, token_ref, q_out, kv_out
):
    for t in range(8):
        first = (7 - t) * 8 + 4 if t > 3 else t * 8
        q_out[t * 128:(t + 1) * 128, :] = got_ref[first:first + 4, 0].reshape(128, HD)
    copy_keys(got_ref, (c0_ref, c1_ref, c2_ref, c3_ref), kv_out)


def segment_of(t, yl, z0, c):
    low = t < 4
    s = yl * 16 + jnp.where(low, t, 7 - t) * 4 + z0 * 2 + c
    return jnp.where(low, s, 63 - s)


def bias_kernel(where_ref, mask_ref, own_out, near_out):
    yl, j, z0, c = where_ref[0], where_ref[1], where_ref[2], where_ref[3]
    mask = mask_ref[0].astype(jnp.float32).astype(jnp.bfloat16)
    r = lax.broadcasted_iota(jnp.int32, (32, 128), 0)
    qb = 2 * segment_of((r >> 1) & 7, yl, z0 ^ (r >> 4), c) + (r & 1)
    pick = (lax.broadcasted_iota(jnp.int32, (32, 128), 1) == qb).astype(jnp.float32)
    rows = jnp.dot(pick.astype(jnp.bfloat16), mask, preferred_element_type=jnp.float32)
    rows = rows.astype(jnp.bfloat16)

    def spread(block):
        n = block.shape[1]
        one = lax.broadcasted_iota(jnp.int32, (192, n), 0) == jnp.broadcast_to(block, (192, n))
        one = jnp.where(one, 1.0, 0.0).astype(jnp.bfloat16)
        return jnp.dot(rows, one, preferred_element_type=jnp.float32) > 0.5

    def span_bias(dy, dc):
        lane = lax.broadcasted_iota(jnp.int32, (1, 1024), 1)
        kb = 2 * segment_of(lane >> 7, yl ^ dy, z0, c ^ dc) + ((lane >> 6) & 1)
        ok = spread(kb + 64).astype(jnp.int32)
        q_full = jnp.broadcast_to(qb[:, :1], (32, 1024))
        k_full = jnp.broadcast_to(kb, (32, 1024))
        ok = ((k_full < q_full) & (ok != 0)) | (k_full == q_full)
        return jnp.where(ok, 0.0, neg_large)

    def cache_bias(dy, dc):
        lane = lax.broadcasted_iota(jnp.int32, (1, 512), 1)
        s = (yl ^ dy) * 16 + (j ^ (lane >> 7)) * 4 + z0 * 2 + (c ^ dc)
        return jnp.where(spread(2 * s + ((lane >> 6) & 1)), 0.0, neg_large)

    for dy, out in enumerate((own_out, near_out)):
        for dc in range(2):
            out[:, dc * KEYS:dc * KEYS + 1024] = span_bias(dy, dc)
            out[:, dc * KEYS + 1024:(dc + 1) * KEYS] = cache_bias(dy, dc)


def score_tile(q, keys):
    return lax.dot_general(
        q, keys, (((1,), (1,)), ((), ())), preferred_element_type=jnp.float32
    )


def lane_sums(p):
    total = p[:, :HD]
    for i in range(1, p.shape[1] // HD):
        total = total + p[:, i * HD:(i + 1) * HD]
    return total


def attend(state, q, jobs, bias_ref, block):
    def scores(job):
        kv_ref, first = job[:2]
        return score_tile(q, kv_ref[0, first:first + 512, :])

    raws = [scores(jobs[0])]
    for n, (kv_ref, first, lanes, causal) in enumerate(jobs):
        if n + 1 < len(jobs):
            raws.append(scores(jobs[n + 1]))
        raw = raws[n] * score_scale
        parts = []
        for i in range(q.shape[0] // 64):
            bias = bias_ref[block + i:block + i + 1, lanes:lanes + 512]
            parts.append(raw[i * 64:(i + 1) * 64] + bias)
        s = jnp.concatenate(parts, axis=0)
        if causal:
            row = lax.broadcasted_iota(jnp.int32, s.shape, 0)
            col = lax.broadcasted_iota(jnp.int32, s.shape, 1)
            s = jnp.where(col <= row, s, neg_large)
        top, total, acc = state
        new_top = jnp.maximum(top, jnp.max(s, axis=1, keepdims=True))
        factor = jnp.exp2(top - new_top)
        p = jnp.exp2(s - new_top[:, :1])
        total = total * factor + lane_sums(p)
        acc = acc * factor + jnp.dot(
            p.astype(jnp.bfloat16),
            kv_ref[1, first:first + 512, :],
            preferred_element_type=jnp.float32,
        )
        state = new_top, total, acc
    return state


def fresh(rows):
    return (
        jnp.full((rows, HD), neg_large, jnp.float32),
        jnp.zeros((rows, HD), jnp.float32),
        jnp.zeros((rows, HD), jnp.float32),
    )


def own_kernel(which, q_ref, kv0, kv1, bias_ref, top, total, acc):
    for high in range(2):
        jobs = []
        for dc, kv_ref in enumerate((kv0, kv1)):
            lanes = dc * KEYS
            causal = which == 0 and dc == 0
            jobs.append((kv_ref, 1024, lanes + 1024, False))
            jobs.append((kv_ref, 0, lanes, causal and not high))
            if high:
                jobs.append((kv_ref, 512, lanes + 512, causal))
        rows = slice(high * 512, (high + 1) * 512)
        top[rows, :], total[rows, :], acc[rows, :] = attend(
            fresh(512), q_ref[rows, :], jobs, bias_ref, which * 16 + high * 8
        )


def near_fold(yl, which, q_ref, kv_refs, bias_ref, refs, done):
    def variant(firsts):
        for high in range(2):
            rows = slice(high * 512, (high + 1) * 512)
            jobs = [
                (kv_ref, first, dc * KEYS + first, False)
                for dc, kv_ref in kv_refs for first in firsts[high]
            ]
            state = attend(
                tuple(ref[rows, :] for ref in refs), q_ref[rows, :], jobs, bias_ref,
                which * 16 + high * 8,
            )
            done(high, *state)

    @pl.when(yl == 1)
    def _():
        variant(((0, 1024), (0, 1024)))

    @pl.when(yl == 0)
    def _():
        variant(((1024,), (0, 512, 1024)))


def to_row(column):
    row = lax.broadcasted_iota(jnp.int32, (128, HD), 0)
    col = lax.broadcasted_iota(jnp.int32, (128, HD), 1)
    return jnp.sum(jnp.where(row == col, column, 0.0), axis=0, keepdims=True)


def to_column(line):
    row = lax.broadcasted_iota(jnp.int32, (128, HD), 0)
    col = lax.broadcasted_iota(jnp.int32, (128, HD), 1)
    return jnp.sum(jnp.where(row == col, line, 0.0), axis=1, keepdims=True)


def near_partner_kernel(where_ref, q_ref, kv_ref, bias_ref, t_ref, l_ref, a_ref, part_out, levels):
    def done(high, top, total, acc):
        weight = jnp.sum(total, axis=1, keepdims=True)
        part_out[high * 512:(high + 1) * 512, :] = (acc / weight).astype(jnp.bfloat16)
        level = top + jnp.log2(jnp.broadcast_to(weight, (512, HD)))
        for i in range(4):
            t = high * 4 + i
            levels[t:t + 1, :] = to_row(level[i * 128:(i + 1) * 128])

    near_fold(
        where_ref[0], 1, q_ref, ((1, kv_ref),), bias_ref, (t_ref, l_ref, a_ref), done
    )
    rest = levels[...]
    pieces = []
    for _ in range(4):
        piece = rest.astype(jnp.bfloat16).astype(jnp.float32)
        rest = rest - piece
        pieces.append(piece)
    part_out[1024:, :] = jnp.concatenate(pieces, axis=0).astype(jnp.bfloat16)


def near_kernel(which, cores, where_ref, q_ref, *refs):
    def done(high, *state):
        rows = slice(high * 512, (high + 1) * 512)
        for ref, value in zip(refs[-3:], state):
            ref[rows, :] = value

    kv_refs = tuple(zip(cores, refs))
    refs = refs[len(cores):]
    near_fold(where_ref[0], which, q_ref, kv_refs, refs[0], refs[1:4], done)


def combine_kernel(where_ref, top, total, acc, part_ref, extra_ref, out_ref):
    j = where_ref[1]
    pieces = part_ref[1024:, :].astype(jnp.float32)
    levels = pieces[0:8] + (pieces[8:16] + (pieces[16:24] + pieces[24:32]))
    for t in range(8):
        rows = slice(t * 128, (t + 1) * 128)
        level = to_column(levels[t:t + 1])
        best = jnp.maximum(top[rows, :], level)
        factor = jnp.exp2(top[rows, :] - best)
        other = jnp.exp2(level - best)
        weight = jnp.sum(total[rows, :], axis=1, keepdims=True) * factor + other
        own = acc[rows, :] * factor + part_ref[rows, :].astype(jnp.float32) * other
        mixed = (own / weight + extra_ref[rows, :]).astype(jnp.bfloat16)
        to = t if t < 4 else 7 - t
        half = t // 4
        out_ref[j ^ to, half * 128:(half + 1) * 128, :] = mixed


def memory_kernel(where_ref, len_ref, gate_ref, q_ref, audio_ref, video_ref, out_ref):
    j = where_ref[1]
    slot = lax.broadcasted_iota(jnp.int32, (1, 512), 1)
    for high in range(2):
        q = q_ref[high * 512:(high + 1) * 512, :]
        mixed = jnp.zeros((512, HD), jnp.float32)
        raws = [score_tile(q, mem_ref[0]) for mem_ref in (audio_ref, video_ref)]
        for n, mem_ref in enumerate((audio_ref, video_ref)):
            bias = jnp.where(slot < len_ref[n], 0.0, neg_large)
            s = raws[n] * score_scale + bias
            p = jnp.exp2(s - jnp.max(s, axis=1, keepdims=True))
            total = jnp.sum(lane_sums(p), axis=1, keepdims=True)
            part = jnp.dot(
                p.astype(jnp.bfloat16), mem_ref[1], preferred_element_type=jnp.float32
            )
            gate = jnp.tanh(jnp.full((1, HD), gate_ref[n, j], jnp.float32))
            mixed = mixed + gate * (part / total)
        out_ref[high * 512:(high + 1) * 512, :] = mixed


def project_kernel(where_ref, m0, m1, m2, m3, w_ref, out_ref, mixed):
    j = where_ref[1]

    @pl.when(pl.program_id(0) == 0)
    def _():
        for k, m in enumerate((m0, m1, m2, m3)):
            mixed[:, pl.ds(pl.multiple_of((j ^ k) * HD, HD), HD)] = m[...]

    part = jnp.dot(mixed[...], w_ref[...], preferred_element_type=jnp.float32)
    part = part.astype(jnp.bfloat16)
    for h in range(8):
        out_ref[h] = part[h * 32:(h + 1) * 32]


def cost(us):
    return pl.CostEstimate(flops=int(us * 1.15e9), bytes_accessed=2**20, transcendentals=0)


def after(array, token):
    def kernel(array_ref, token_ref, out_ref):
        pass

    return pl.pallas_call(
        kernel,
        out_shape=jax.ShapeDtypeStruct(array.shape, array.dtype),
        in_specs=[anywhere(), anywhere()],
        out_specs=anywhere(),
        input_output_aliases={0: 0},
        compiler_params=params(),
        name="after",
    )(array, token)


def f32(*shape):
    return jax.ShapeDtypeStruct(shape, jnp.float32)


def b16(*shape):
    return jax.ShapeDtypeStruct(shape, jnp.bfloat16)


def shards(
    span_qkv, cache_kv, audio_kv, video_kv, block_mask, mem_lengths, cross_gates, out_weight
):
    j = lax.axis_index("z2") * 2 + lax.axis_index("z1")
    where = jnp.stack(
        [lax.axis_index("yl"), j, lax.axis_index("z0"), lax.axis_index("c")]
    ).astype(jnp.int32)

    span_packed, cache_packed = pl.pallas_call(
        pack_kernel,
        out_shape=(b16(32, 3, 32, HD), b16(4, 2, 128, HD)),
        in_specs=[scalars(), whole(), whole()],
        out_specs=(whole(),) * 2,
        compiler_params=params(),
        cost_estimate=cost(2),
        name="pack",
    )(where, span_qkv, cache_kv)

    def swap(part, axis):
        return lax.ppermute(part, axis, xor_perm(2, 1))

    def swap_z(parts):
        return [parts[0]] + [lax.ppermute(parts[k], ZZ, xor_perm(4, k)) for k in range(1, 4)]

    own_bias, near_bias = pl.pallas_call(
        bias_kernel,
        out_shape=(f32(32, 2 * KEYS),) * 2,
        in_specs=[scalars(), whole()],
        out_specs=(whole(),) * 2,
        compiler_params=params(),
        cost_estimate=cost(2),
        name="bias",
    )(where, block_mask)

    got = lax.all_to_all(span_packed, ZZ + HEADS, split_axis=0, concat_axis=0, tiled=True)
    cache_own = swap_z([cache_packed[k] for k in range(4)])
    def unpack(kernel, token, name, *outs):
        return pl.pallas_call(
            kernel,
            out_shape=outs,
            in_specs=[whole()] * 5 + [anywhere()],
            out_specs=(whole(),) * len(outs),
            compiler_params=params(),
            cost_estimate=cost(0.1),
            name=name,
        )(got, *cache_own, token)

    (kv_sent,) = unpack(unpack_keys_kernel, own_bias, "unpack_keys", b16(2, KEYS, HD))
    kv_near = swap(kv_sent, "yl")
    queries, kv_own = unpack(
        unpack_rest_kernel, kv_sent, "unpack_rest", b16(1024, HD), b16(2, KEYS, HD)
    )
    partner_queries = swap(queries, "z0")
    sibling_keys = swap(kv_own, "c")

    extra = pl.pallas_call(
        memory_kernel,
        grid_spec=pltpu.PrefetchScalarGridSpec(
            num_scalar_prefetch=1,
            grid=(1,),
            in_specs=[
                scalars(),
                scalars(),
                pl.BlockSpec((1024, HD), lambda i, where: (0, 0)),
                pl.BlockSpec((2, 512, HD), lambda i, where: (0, 0, where[1])),
                pl.BlockSpec((2, 512, HD), lambda i, where: (0, 0, where[1])),
            ],
            out_specs=pl.BlockSpec((1024, HD), lambda i, where: (0, 0)),
        ),
        out_shape=f32(1024, HD),
        compiler_params=params(),
        cost_estimate=cost(0.1),
        name="memories",
    )(where, mem_lengths, cross_gates, queries, audio_kv, video_kv)

    def own(which, q):
        return pl.pallas_call(
            functools.partial(own_kernel, which),
            out_shape=(f32(1024, HD),) * 3,
            in_specs=[whole()] * 4,
            out_specs=(whole(),) * 3,
            compiler_params=params(),
            cost_estimate=cost(0.1),
            name="own_keys",
        )(q, kv_own, sibling_keys, own_bias)

    sibling_keys = after(sibling_keys, extra)
    states = [own(0, queries)]
    partner_queries = after(partner_queries, states[0][0])
    states.append(own(1, partner_queries))
    kv_near = after(kv_near, states[1][0])
    near_sibling = swap(kv_near, "c")

    def near(which, cores, q, keys, state):
        return pl.pallas_call(
            functools.partial(near_kernel, which, cores),
            out_shape=(f32(1024, HD),) * 3,
            in_specs=[scalars()] + [whole()] * (5 + len(cores)),
            out_specs=(whole(),) * 3,
            compiler_params=params(),
            cost_estimate=cost(2.5 * len(cores)),
            name="near_keys",
        )(where, q, *keys, near_bias, *state)

    state = near(1, (0,), partner_queries, (kv_near,), states[1])
    part = pl.pallas_call(
        near_partner_kernel,
        out_shape=b16(1056, HD),
        in_specs=[scalars()] + [whole()] * 6,
        out_specs=whole(),
        scratch_shapes=[pltpu.VMEM((8, HD), jnp.float32)],
        compiler_params=params(),
        cost_estimate=cost(3),
        name="near_keys_partner",
    )(where, partner_queries, near_sibling, near_bias, *state)
    part = swap(part, "z0")
    state = near(0, (0, 1), queries, (kv_near, near_sibling), states[0])
    state = pl.pallas_call(
        combine_kernel,
        out_shape=b16(4, 256, HD),
        in_specs=[scalars()] + [whole()] * 5,
        out_specs=whole(),
        compiler_params=params(),
        cost_estimate=cost(1),
        name="combine",
    )(where, *state, part, extra)

    mixed = [state[0]] + [lax.ppermute(state[k], ZZ, xor_perm(4, k)) for k in range(1, 4)]
    partial_sums = pl.pallas_call(
        project_kernel,
        grid=(4,),
        out_shape=b16(8, 32, 4096),
        in_specs=[scalars()]
        + [pl.BlockSpec((256, HD), lambda i: (0, 0))] * 4
        + [pl.BlockSpec((512, 1024), lambda i: (0, i))],
        out_specs=pl.BlockSpec((8, 32, 1024), lambda i: (0, 0, i)),
        scratch_shapes=[pltpu.VMEM((256, 512), jnp.bfloat16)],
        compiler_params=params(),
        cost_estimate=cost(3),
        name="project",
    )(where, *mixed, out_weight)
    gathered = lax.all_to_all(partial_sums, HEADS, split_axis=0, concat_axis=0, tiled=True)
    return jnp.sum(gathered.astype(jnp.float32), axis=0).astype(jnp.bfloat16)


def solution(mesh):
    fine = Mesh(mesh.devices.reshape(SIZES), AXES)
    seq = ("yl", "z2", "z1", "z0", "c")
    placed = (
        P(None, seq + HEADS, None),
        P(None, seq, HEADS),
        P(None, None, HEADS),
        P(None, None, HEADS),
        P(HEADS, None, None),
        P(),
        P(None, HEADS),
        P(HEADS, None),
    )
    return jax.shard_map(
        shards, mesh=fine, in_specs=placed, out_specs=P(seq + HEADS, None), check_vma=False
    )
```

time: 138 us -> 132 us (0.957)
  Pallas kernels: 31.9 us -> 27.8 us
  blocking collectives: 34 us -> 31.9 us
  starting transfers between devices: 29.2 us -> 27.2 us
    pallas_call x4 -> x10, Pallas kernels: 21.5 us -> 18.2 us  [the longest x2 7.95 us: near(): pl.pallas_call(functools.partial(near_kernel, which, cores), out_shape=(f...]
    ppermute x6 -> x5, waiting for transfers between devices: 10.2 us -> 13.2 us  [swap(): return lax.ppermute(part, axis, xor_perm(2, 1))]
    all_to_all x1, blocking collectives: 34 us -> 31.9 us  [shards(): lax.all_to_all(partial_sums, HEADS, split_axis=0, concat_axis=0, tiled=True)]
    ppermute x6 -> x5, starting transfers between devices: 2.97 us -> 0.95 us  [swap(): return lax.ppermute(part, axis, xor_perm(2, 1))]
    unnamed x17 -> x21, local copies, waits for them, and re-layouts: 2.26 us -> 2.96 us
  transfers between devices with their start and end apart: 13 -> 12, of which waited for: 8 -> 8; matrix products, arithmetic and copies ran while one was open for 0% -> 1% of each run, Pallas kernels for 14% -> 15%
where the time goes in v3:
time: 132 us; the launch traced here: 130 us
  waiting for transfers between devices  38.3 us (29%)
  blocking collectives  31.9 us (24%)
  Pallas kernels  27.8 us (21%)
  starting transfers between devices  27.2 us (21%)
  local copies, waits for them, and re-layouts  3.65 us (3%)
    all_to_all x1, blocking collectives, shards(): lax.all_to_all(partial_sums, HEADS, split_axis=0, concat_axis=0, tiled=True)  31.9 us
    ppermute x3, waiting for transfers between devices, swap_z(): lax.ppermute(parts[k], ZZ, xor_perm(4, k))  18.4 us
    ppermute x5, waiting for transfers between devices, swap(): return lax.ppermute(part, axis, xor_perm(2, 1))  13.2 us
    all_to_all x1, starting transfers between devices, shards(): lax.all_to_all(span_packed, ZZ + HEADS, split_axis=0, concat_axis=0, tile...  13.2 us
    pallas_call x2, Pallas kernels, near(): pl.pallas_call(functools.partial(near_kernel, which, cores), out_shape=(f...  7.95 us
    pallas_call x2, Pallas kernels, own(): pl.pallas_call(functools.partial(own_kernel, which), out_shape=(f32(1024,...  7.09 us
    ppermute x3, starting transfers between devices, shards(): lax.ppermute(state[k], ZZ, xor_perm(4, k))  6.58 us
    ppermute x3, starting transfers between devices, swap_z(): lax.ppermute(parts[k], ZZ, xor_perm(4, k))  6.5 us
  transfers between devices with their start and end apart: 12, of which 8 were waited for; matrix products, arithmetic and copies ran while one was open for 1% of the time, Pallas kernels for 15%

profile of v3, /device:TPU:32, one launch (start us, length us, event | category | flops | bytes accessed | tf_op | source)
XLA Modules:
  0.0 130.1 jit_solution(236394050546465881)
XLA Ops:
  0.0 0.1 pad_add_fusion.where_ref
  0.1 0.0 copy-start.5
  0.1 1.1 copy-done.5
  1.2 0.0 copy-start.6
  1.2 0.9 copy-done.6
  2.2 1.6 %pack.1 = (bf16[32,3,32,128]{3,2,1,0:T(8,128)(2,1)}, bf16[4,2,128,128]{3,2,1,0:T(8,128)(2,1)S(1)}) custom-call(s32[4]{0:T(128)S(1)} %pad_add_fusion.where_ref, bf16[3,32,4096]{2,1,0:T(8,128)(2,1)S(1)} %copy-done.5, bf16[2,128,512]{2,1,0:T(8,128)(2,1)S(1)} %copy-done.6), custom_call_target="tpu_custom_call" | custom-call | flops 2300000000 | bytes 1048576 | tf_op jit(solution)/shard_map/pack/pallas_call | solution.py:334
  3.7 0.0 copy-start.9
  3.7 13.2 %all-to-all-start = ((bf16[32,3,32,128]{3,2,1,0:T(8,128)(2,1)}), bf16[32,3,32,128]{3,2,1,0:T(8,128)(2,1)S(1)}, u32[]{:S(2)}, u32[]{:S(2)}) async-start(bf16[32,3,32,128]{3,2,1,0:T(8,128)(2,1)} %get-tuple-element.23), calls=%async_computation | async-start | bytes 1572864 | tf_op jit(solution)/shard_map/all_to_all | solution.py:360
  16.9 0.7 slice_bitcast_fusion.4
  17.6 3.9 %collective-permute-start.2 = (bf16[2,128,128]{2,1,0:T(8,128)(2,1)}, bf16[2,128,128]{2,1,0:T(8,128)(2,1)S(1)}, u32[]{:S(2)}, u32[]{:S(2)}) collective-permute-start(bf16[2,128,128]{2,1,0:T(8,128)(2,1)} %get-tuple-element.45), channel_id=1, source_target_pairs={{0,96},{32,64},{64,32},{96,0},{1,97},{33,65},{65,33},{97,1},{2,98}... | collective-permute-start | bytes 196616 | tf_op jit(solution)/shard_map/ppermute | solution.py:348
  21.5 2.3 %collective-permute-start.1 = (bf16[2,128,128]{2,1,0:T(8,128)(2,1)}, bf16[2,128,128]{2,1,0:T(8,128)(2,1)S(1)}, u32[]{:S(2)}, u32[]{:S(2)}) collective-permute-start(bf16[2,128,128]{2,1,0:T(8,128)(2,1)} %get-tuple-element.46), channel_id=1, source_target_pairs={{0,64},{32,96},{64,0},{96,32},{1,65},{33,97},{65,1},{97,33},{2,66}... | collective-permute-start | bytes 196616 | tf_op jit(solution)/shard_map/ppermute | solution.py:348
  23.9 0.2 collective-permute-start
  24.1 0.0 copy-done.9
  24.1 0.1 copy.12.mask_ref
  24.2 1.5 %bias.1 = (f32[32,3072]{1,0:T(8,128)S(1)}, f32[32,3072]{1,0:T(8,128)S(1)}) custom-call(s32[4]{0:T(128)S(1)} %pad_add_fusion.where_ref, s32[1,128,192]{2,1,0:T(8,128)S(1)} %copy.12.mask_ref), custom_call_target="tpu_custom_call" | custom-call | flops 2300000000 | bytes 1048576 | tf_op jit(solution)/shard_map/bias/pallas_call | solution.py:350
  25.7 0.0 copy-start.7
  25.8 0.8 copy-done.7
  26.5 0.0 copy-start
  26.5 0.0 copy-start.1
  26.5 0.0 copy-start.2
  26.5 0.0 copy-start.3
  26.5 16.9 %collective-permute-done.2.c3_ref = bf16[2,128,128]{2,1,0:T(8,128)(2,1)S(1)} collective-permute-done((bf16[2,128,128]{2,1,0:T(8,128)(2,1)}, bf16[2,128,128]{2,1,0:T(8,128)(2,1)S(1)}, u32[]{:S(2)}, u32[]{:S(2)}) %collective-permute-start.2) | collective-permute-done | bytes 65568 | tf_op jit(solution)/shard_map/ppermute | solution.py:348
  43.5 1.4 %collective-permute-done.1.c2_ref = bf16[2,128,128]{2,1,0:T(8,128)(2,1)S(1)} collective-permute-done((bf16[2,128,128]{2,1,0:T(8,128)(2,1)}, bf16[2,128,128]{2,1,0:T(8,128)(2,1)S(1)}, u32[]{:S(2)}, u32[]{:S(2)}) %collective-permute-start.1) | collective-permute-done | bytes 65568 | tf_op jit(solution)/shard_map/ppermute | solution.py:348
  44.9 0.0 collective-permute-done.c1_ref
  44.9 2.4 %all-to-all-done.got_ref = bf16[32,3,32,128]{3,2,1,0:T(8,128)(2,1)S(1)} async-done(((bf16[32,3,32,128]{3,2,1,0:T(8,128)(2,1)}), bf16[32,3,32,128]{3,2,1,0:T(8,128)(2,1)S(1)}, u32[]{:S(2)}, u32[]{:S(2)}) %all-to-all-start) | async-done | bytes 786464 | tf_op jit(solution)/shard_map/all_to_all | solution.py:360
  47.3 0.1 unpack_keys.1.token_ref
  47.3 0.1 unpack_rest.1
  47.4 0.1 collective-permute-start.5
  47.5 0.8 collective-permute-start.3
  48.3 0.0 collective-permute-start.4
  48.3 0.0 copy-done
  48.3 0.0 copy-done.1
  48.3 0.0 copy-done.2
  48.3 0.0 copy-done.3
  48.3 2.8 %memories.1.token_ref.extra_ref = f32[1024,128]{1,0:T(8,128)S(1)} custom-call(s32[4]{0:T(128)S(1)} %pad_add_fusion.where_ref, s32[2]{0:T(128)S(1)} %copy-done.3, f32[2,4]{1,0:T(2,128)S(1)} %copy-done.2, bf16[1024,128]{1,0:T(8,128)(2,1)S(1)} %get-tuple-element.26.q_ref, bf16[2,512,512]{2,1,0:T(8,128)(2,1)S(1)} %copy-done, bf16[2,512,512]{2,1,0:T(8,128)(2,1)S(1)} %copy-done.1), custom_call_target="tpu_custom_call" | custom-call | flops 115000000 | bytes 1048576 | tf_op jit(solution)/shard_map/memories/pallas_call | solution.py:381
  51.1 0.0 collective-permute-done.5.array_ref
  51.1 3.5 %own_keys.2 = (f32[1024,128]{1,0:T(8,128)S(1)}, f32[1024,128]{1,0:T(8,128)S(1)}, f32[1024,128]{1,0:T(8,128)S(1)}) custom-call(bf16[1024,128]{1,0:T(8,128)(2,1)S(1)} %get-tuple-element.26.q_ref, bf16[2,1536,128]{2,1,0:T(8,128)(2,1)S(1)} %get-tuple-element.27.kv0, bf16[2,1536,128]{2,1,0:T(8,128)(2,1)S(1)} %after.3.kv1, ...), custom_call_target="tpu_custom_call" | custom-call | flops 115000000 | bytes 1048576 | tf_op jit(solution)/shard_map/own_keys/pallas_call | solution.py:402
  54.6 2.0 %collective-permute-done.4.array_ref = bf16[1024,128]{1,0:T(8,128)(2,1)S(1)} collective-permute-done((bf16[1024,128]{1,0:T(8,128)(2,1)S(1)}, bf16[1024,128]{1,0:T(8,128)(2,1)S(1)}, u32[]{:S(2)}, u32[]{:S(2)}) %collective-permute-start.4) | collective-permute-done | bytes 262176 | tf_op jit(solution)/shard_map/ppermute | solution.py:345
  56.6 0.0 copy-start.8
  56.6 3.6 %own_keys.3 = (f32[1024,128]{1,0:T(8,128)S(1)}, f32[1024,128]{1,0:T(8,128)S(1)}, f32[1024,128]{1,0:T(8,128)S(1)}) custom-call(bf16[1024,128]{1,0:T(8,128)(2,1)S(1)} %after.4.q_ref, bf16[2,1536,128]{2,1,0:T(8,128)(2,1)S(1)} %get-tuple-element.27.kv0, bf16[2,1536,128]{2,1,0:T(8,128)(2,1)S(1)} %after.3.kv1, f32[32,3072]{1,0:T(8,128)S(1)} %get-tuple-element.25.token_ref.bias_ref), custom_call_target="tpu_custom_call" | custom-call | flops 115000000 | bytes 1048576 | tf_op jit(solution)/shard_map/own_keys/pallas_call | solution.py:402
  60.2 7.2 %collective-permute-done.3.array_ref = bf16[2,1536,128]{2,1,0:T(8,128)(2,1)S(1)} collective-permute-done((bf16[2,1536,128]{2,1,0:T(8,128)(2,1)S(1)}, bf16[2,1536,128]{2,1,0:T(8,128)(2,1)S(1)}, u32[]{:S(2)}, u32[]{:S(2)}) %collective-permute-start.3) | collective-permute-done | bytes 786464 | tf_op jit(solution)/shard_map/ppermute | solution.py:345
  67.5 0.0 collective-permute-start.6
  67.5 0.0 copy-done.8
  67.5 3.1 %near_keys.3 = (f32[1024,128]{1,0:T(8,128)S(1)}, f32[1024,128]{1,0:T(8,128)S(1)}, f32[1024,128]{1,0:T(8,128)S(1)}) custom-call(s32[4]{0:T(128)S(1)} %pad_add_fusion.where_ref, bf16[1024,128]{1,0:T(8,128)(2,1)S(1)} %after.4.q_ref, bf16[2,1536,128]{2,1,0:T(8,128)(2,1)S(1)} %after.5.refs_0_, f32[32,3072]{1,0:T(8,128)S(1)} %copy-done.8, ...), custom_call_target="tpu_custom_call" | custom-call | flops 2875000064 | bytes 1048576 | tf_op jit(solution)/shard_map/near_keys/pallas_call | solution.py:420
  70.6 0.0 collective-permute-done.6.refs_1_.kv_ref
  70.6 3.0 %near_keys_partner.1 = bf16[1056,128]{1,0:T(8,128)(2,1)S(1)} custom-call(s32[4]{0:T(128)S(1)} %pad_add_fusion.where_ref, bf16[1024,128]{1,0:T(8,128)(2,1)S(1)} %after.4.q_ref, bf16[2,1536,128]{2,1,0:T(8,128)(2,1)S(1)} %collective-permute-done.6.refs_1_.kv_ref, f32[32,3072]{1,0:T(8,128)S(1)} %copy-done.8, f32[1024,128]{1,0:T(8,128)S(1)} %get-tuple-element.38.t_ref, ...), custom_call_target="tpu_custom_call" | custom-call | flops 3449999872 | bytes 1048576 | tf_op jit(solution)/shard_map/near_keys_partner/pallas_call | solution.py:431
  73.6 0.1 collective-permute-start.7
  73.7 4.8 %near_keys.2 = (f32[1024,128]{1,0:T(8,128)S(1)}, f32[1024,128]{1,0:T(8,128)S(1)}, f32[1024,128]{1,0:T(8,128)S(1)}) custom-call(s32[4]{0:T(128)S(1)} %pad_add_fusion.where_ref, bf16[1024,128]{1,0:T(8,128)(2,1)S(1)} %get-tuple-element.26.q_ref, bf16[2,1536,128]{2,1,0:T(8,128)(2,1)S(1)} %after.5.refs_0_, ...), custom_call_target="tpu_custom_call" | custom-call | flops 5750000128 | bytes 1048576 | tf_op jit(solution)/shard_map/near_keys/pallas_call | solution.py:420
  78.6 4.0 %collective-permute-done.7.part_ref = bf16[1056,128]{1,0:T(8,128)(2,1)S(1)} collective-permute-done((bf16[1056,128]{1,0:T(8,128)(2,1)S(1)}, bf16[1056,128]{1,0:T(8,128)(2,1)S(1)}, u32[]{:S(2)}, u32[]{:S(2)}) %collective-permute-start.7) | collective-permute-done | bytes 270368 | tf_op jit(solution)/shard_map/ppermute | solution.py:345
  82.6 0.0 copy-start.4
  82.6 0.9 combine.1
  83.5 1.3 collective-permute-start.10
  84.8 1.4 %collective-permute-start.9 = (bf16[256,128]{1,0:T(8,128)(2,1)S(1)}, bf16[256,128]{1,0:T(8,128)(2,1)S(1)}, u32[]{:S(2)}, u32[]{:S(2)}) collective-permute-start(bf16[256,128]{1,0:T(8,128)(2,1)S(1)} %get-tuple-element.42), channel_id=1, source_target_pairs={{0,64},{32,96},{64,0},{96,32},{1,65},{33,97},{65,1},{97,33},{2,66}... | collective-permute-start | bytes 196616 | tf_op jit(solution)/shard_map/ppermute | solution.py:453
  86.2 4.0 %collective-permute-start.8 = (bf16[256,128]{1,0:T(8,128)(2,1)S(1)}, bf16[256,128]{1,0:T(8,128)(2,1)S(1)}, u32[]{:S(2)}, u32[]{:S(2)}) collective-permute-start(bf16[256,128]{1,0:T(8,128)(2,1)S(1)} %get-tuple-element.43), channel_id=1, source_target_pairs={{0,32},{32,0},{64,96},{96,64},{1,33},{33,1},{65,97},{97,65},{2,34}... | collective-permute-start | bytes 196616 | tf_op jit(solution)/shard_map/ppermute | solution.py:453
  90.1 3.5 %collective-permute-done.10.m3 = bf16[256,128]{1,0:T(8,128)(2,1)S(1)} collective-permute-done((bf16[256,128]{1,0:T(8,128)(2,1)S(1)}, bf16[256,128]{1,0:T(8,128)(2,1)S(1)}, u32[]{:S(2)}, u32[]{:S(2)}) %collective-permute-start.10) | collective-permute-done | bytes 65568 | tf_op jit(solution)/shard_map/ppermute | solution.py:453
  93.6 0.0 collective-permute-done.9.m2
  93.6 0.8 collective-permute-done.8.m1
  94.5 0.0 copy-done.4
  94.5 2.7 %project.1 = bf16[8,32,4096]{2,1,0:T(8,128)(2,1)S(1)} custom-call(s32[4]{0:T(128)S(1)} %pad_add_fusion.where_ref, bf16[256,128]{1,0:T(8,128)(2,1)S(1)} %get-tuple-element.44.m0, bf16[256,128]{1,0:T(8,128)(2,1)S(1)} %collective-permute-done.8.m1, bf16[256,128]{1,0:T(8,128)(2,1)S(1)} %collective-permute-done.9.m2, ...), custom_call_target="tpu_custom_call" | custom-call | flops 3449999872 | bytes 1048576 | tf_op jit(solution)/shard_map/project/pallas_call | solution.py:454
  97.2 31.9 %all_to_all.10 = bf16[8,32,4096]{2,1,0:T(8,128)(2,1)S(1)} all-to-all(bf16[8,32,4096]{2,1,0:T(8,128)(2,1)S(1)} %project.1), channel_id=1, replica_groups=mesh['yl'=2,'z2'=2,'z1'=2,'z0'=2,'c'=2,'x'=4,'yh'=2] {'x','yh'}, dimensions={0} | all-to-all | bytes 4194304 | tf_op jit(solution)/shard_map/all_to_all | solution.py:467
  129.1 1.1 reduce_sum.12
  (4 shorter events, 0.0 us)
Async XLA Ops:
  0.1 1.1 copy-start.5
  1.2 0.9 copy-start.6
  3.7 20.4 %copy-start.9 = (s32[1,128,192]{1,2,0:T(8,128)S(1)}, s32[1,128,192]{1,2,0:T(8,128)}, u32[]{:S(2)}) copy-start(s32[1,128,192]{1,2,0:T(8,128)} %param.12) | copy-start | bytes 294916
  3.7 43.5 %all-to-all-start = ((bf16[32,3,32,128]{3,2,1,0:T(8,128)(2,1)}), bf16[32,3,32,128]{3,2,1,0:T(8,128)(2,1)S(1)}, u32[]{:S(2)}, u32[]{:S(2)}) async-start(bf16[32,3,32,128]{3,2,1,0:T(8,128)(2,1)} %get-tuple-element.23), calls=%async_computation | async-start | bytes 1572864 | tf_op jit(solution)/shard_map/all_to_all | solution.py:360
  17.6 25.9 %collective-permute-start.2 = (bf16[2,128,128]{2,1,0:T(8,128)(2,1)}, bf16[2,128,128]{2,1,0:T(8,128)(2,1)S(1)}, u32[]{:S(2)}, u32[]{:S(2)}) collective-permute-start(bf16[2,128,128]{2,1,0:T(8,128)(2,1)} %get-tuple-element.45), channel_id=1, source_target_pairs={{0,96},{32,64},{64,32},{96,0},{1,97},{33,65},{65,33},{97,1},{2,98}... | collective-permute-start | bytes 196616 | tf_op jit(solution)/shard_map/ppermute | solution.py:348
  21.5 23.4 %collective-permute-start.1 = (bf16[2,128,128]{2,1,0:T(8,128)(2,1)}, bf16[2,128,128]{2,1,0:T(8,128)(2,1)S(1)}, u32[]{:S(2)}, u32[]{:S(2)}) collective-permute-start(bf16[2,128,128]{2,1,0:T(8,128)(2,1)} %get-tuple-element.46), channel_id=1, source_target_pairs={{0,64},{32,96},{64,0},{96,32},{1,65},{33,97},{65,1},{97,33},{2,66}... | collective-permute-start | bytes 196616 | tf_op jit(solution)/shard_map/ppermute | solution.py:348
  23.9 21.0 %collective-permute-start = (bf16[2,128,128]{2,1,0:T(8,128)(2,1)}, bf16[2,128,128]{2,1,0:T(8,128)(2,1)S(1)}, u32[]{:S(2)}, u32[]{:S(2)}) collective-permute-start(bf16[2,128,128]{2,1,0:T(8,128)(2,1)} %get-tuple-element.47), channel_id=1, source_target_pairs={{0,32},{32,0},{64,96},{96,64},{1,33},{33,1},{65,97},{97,65},{2,34}... | collective-permute-start | bytes 196616 | tf_op jit(solution)/shard_map/ppermute | solution.py:348
  25.7 0.8 copy-start.7
  26.5 21.8 %copy-start = (bf16[2,512,512]{2,1,0:T(8,128)(2,1)S(1)}, bf16[2,512,512]{2,1,0:T(8,128)(2,1)}, u32[]{:S(2)}) copy-start(bf16[2,512,512]{2,1,0:T(8,128)(2,1)} %audio_ref.1) | copy-start | bytes 3145732
  26.5 21.8 %copy-start.1 = (bf16[2,512,512]{2,1,0:T(8,128)(2,1)S(1)}, bf16[2,512,512]{2,1,0:T(8,128)(2,1)}, u32[]{:S(2)}) copy-start(bf16[2,512,512]{2,1,0:T(8,128)(2,1)} %video_ref.1) | copy-start | bytes 3145732
  26.5 21.8 %copy-start.2 = (f32[2,4]{1,0:T(2,128)S(1)}, f32[2,4]{1,0:T(2,128)}, u32[]{:S(2)}) copy-start(f32[2,4]{1,0:T(2,128)} %gate_ref.1) | copy-start | bytes 100
  26.5 21.8 %copy-start.3 = (s32[2]{0:T(128)S(1)}, s32[2]{0:T(128)}, u32[]{:S(2)}) copy-start(s32[2]{0:T(128)} %len_ref.1) | copy-start | bytes 28
  47.4 3.7 %collective-permute-start.5 = (bf16[2,1536,128]{2,1,0:T(8,128)(2,1)S(1)}, bf16[2,1536,128]{2,1,0:T(8,128)(2,1)S(1)}, u32[]{:S(2)}, u32[]{:S(2)}) collective-permute-start(bf16[2,1536,128]{2,1,0:T(8,128)(2,1)S(1)} %get-tuple-element.27.kv0), channel_id=1, source_target_pairs={{0,8},{8,0},{1,9},{9,1},{2,10},{10,2},{3,11},{11,3},{4,12},{12,4},... | collective-permute-start | bytes 2359304 | tf_op jit(solution)/shard_map/ppermute | solution.py:345
  47.5 20.0 %collective-permute-start.3 = (bf16[2,1536,128]{2,1,0:T(8,128)(2,1)S(1)}, bf16[2,1536,128]{2,1,0:T(8,128)(2,1)S(1)}, u32[]{:S(2)}, u32[]{:S(2)}) collective-permute-start(bf16[2,1536,128]{2,1,0:T(8,128)(2,1)S(1)} %unpack_keys.1.token_ref), channel_id=1, source_target_pairs={{0,128},{128,0},{1,129},{129,1},{2,130},{130,2},{3,131},{131,3},{4... | collective-permute-start | bytes 2359304 | tf_op jit(solution)/shard_map/ppermute | solution.py:345
  48.3 8.4 %collective-permute-start.4 = (bf16[1024,128]{1,0:T(8,128)(2,1)S(1)}, bf16[1024,128]{1,0:T(8,128)(2,1)S(1)}, u32[]{:S(2)}, u32[]{:S(2)}) collective-permute-start(bf16[1024,128]{1,0:T(8,128)(2,1)S(1)} %get-tuple-element.26.q_ref), channel_id=1, source_target_pairs={{0,16},{16,0},{1,17},{17,1},{2,18},{18,2},{3,19},{19,3},{4,20},{20... | collective-permute-start | bytes 786440 | tf_op jit(solution)/shard_map/ppermute | solution.py:345
  56.6 10.8 %copy-start.8 = (f32[32,3072]{1,0:T(8,128)S(1)}, f32[32,3072]{1,0:T(8,128)}, u32[]{:S(2)}) copy-start(f32[32,3072]{1,0:T(8,128)} %copy-done.7) | copy-start | bytes 1179652
  67.5 3.1 %collective-permute-start.6 = (bf16[2,1536,128]{2,1,0:T(8,128)(2,1)S(1)}, bf16[2,1536,128]{2,1,0:T(8,128)(2,1)S(1)}, u32[]{:S(2)}, u32[]{:S(2)}) collective-permute-start(bf16[2,1536,128]{2,1,0:T(8,128)(2,1)S(1)} %after.5.refs_0_), channel_id=1, source_target_pairs={{0,8},{8,0},{1,9},{9,1},{2,10},{10,2},{3,11},{11,3},{4,12},{12,4},... | collective-permute-start | bytes 2359304 | tf_op jit(solution)/shard_map/ppermute | solution.py:345
  73.6 9.0 %collective-permute-start.7 = (bf16[1056,128]{1,0:T(8,128)(2,1)S(1)}, bf16[1056,128]{1,0:T(8,128)(2,1)S(1)}, u32[]{:S(2)}, u32[]{:S(2)}) collective-permute-start(bf16[1056,128]{1,0:T(8,128)(2,1)S(1)} %near_keys_partner.1), channel_id=1, source_target_pairs={{0,16},{16,0},{1,17},{17,1},{2,18},{18,2},{3,19},{19,3},{4,20},{20... | collective-permute-start | bytes 811016 | tf_op jit(solution)/shard_map/ppermute | solution.py:345
  82.6 11.9 %copy-start.4 = (bf16[512,4096]{1,0:T(8,128)(2,1)S(1)}, bf16[512,4096]{1,0:T(8,128)(2,1)}, u32[]{:S(2)}) copy-start(bf16[512,4096]{1,0:T(8,128)(2,1)} %w_ref.1) | copy-start | bytes 12582916
  83.5 10.1 %collective-permute-start.10 = (bf16[256,128]{1,0:T(8,128)(2,1)S(1)}, bf16[256,128]{1,0:T(8,128)(2,1)S(1)}, u32[]{:S(2)}, u32[]{:S(2)}) collective-permute-start(bf16[256,128]{1,0:T(8,128)(2,1)S(1)} %get-tuple-element.41), channel_id=1, source_target_pairs={{0,96},{32,64},{64,32},{96,0},{1,97},{33,65},{65,33},{97,1},{2,98}... | collective-permute-start | bytes 196616 | tf_op jit(solution)/shard_map/ppermute | solution.py:453
  84.8 8.8 %collective-permute-start.9 = (bf16[256,128]{1,0:T(8,128)(2,1)S(1)}, bf16[256,128]{1,0:T(8,128)(2,1)S(1)}, u32[]{:S(2)}, u32[]{:S(2)}) collective-permute-start(bf16[256,128]{1,0:T(8,128)(2,1)S(1)} %get-tuple-element.42), channel_id=1, source_target_pairs={{0,64},{32,96},{64,0},{96,32},{1,65},{33,97},{65,1},{97,33},{2,66}... | collective-permute-start | bytes 196616 | tf_op jit(solution)/shard_map/ppermute | solution.py:453
  86.2 8.3 %collective-permute-start.8 = (bf16[256,128]{1,0:T(8,128)(2,1)S(1)}, bf16[256,128]{1,0:T(8,128)(2,1)S(1)}, u32[]{:S(2)}, u32[]{:S(2)}) collective-permute-start(bf16[256,128]{1,0:T(8,128)(2,1)S(1)} %get-tuple-element.43), channel_id=1, source_target_pairs={{0,32},{32,0},{64,96},{96,64},{1,33},{33,1},{65,97},{97,65},{2,34}... | collective-permute-start | bytes 196616 | tf_op jit(solution)/shard_map/ppermute | solution.py:453

commit v4 on v3

--- a/solution.py
+++ b/solution.py
@@ -34,13 +34,20 @@
     return [(i, i ^ k) for i in range(count)]
 
 
-def pack_kernel(where_ref, span_ref, cache_ref, span_out, cache_out):
+def turn_perm(count, k):
+    return [(i, (i + k) % count) for i in range(count)]
+
+
+def pack_kernel(span_ref, span_out):
+    for d in range(32):
+        col = ((d % 8) * 4 + d // 8) * HD
+        span_out[d, 0] = span_ref[0, :, col:col + HD]
+
+
+def pack_cache_kernel(where_ref, cache_ref, token_ref, cache_out):
     j = where_ref[1]
     for k in range(4):
-        cache_out[k] = cache_ref[:, :, pl.ds(pl.multiple_of((j ^ k) * HD, HD), HD)]
-    for d in range(32):
-        col = ((d % 8) * 4 + d // 8) * HD
-        span_out[d] = span_ref[:, :, col:col + HD]
+        cache_out[k] = cache_ref[:, :, pl.ds(pl.multiple_of(((j + k) & 3) * HD, HD), HD)]
 
 
 def copy_keys(got_ref, cache_refs, kv_out):
@@ -98,7 +105,7 @@
 
     def cache_bias(dy, dc):
         lane = lax.broadcasted_iota(jnp.int32, (1, 512), 1)
-        s = (yl ^ dy) * 16 + (j ^ (lane >> 7)) * 4 + z0 * 2 + (c ^ dc)
+        s = (yl ^ dy) * 16 + ((j - (lane >> 7)) & 3) * 4 + z0 * 2 + (c ^ dc)
         return jnp.where(spread(2 * s + ((lane >> 6) & 1)), 0.0, neg_large)
 
     for dy, out in enumerate((own_out, near_out)):
@@ -244,8 +251,7 @@
     near_fold(where_ref[0], which, q_ref, kv_refs, refs[0], refs[1:4], done)
 
 
-def combine_kernel(where_ref, top, total, acc, part_ref, extra_ref, out_ref):
-    j = where_ref[1]
+def combine_kernel(top, total, acc, part_ref, extra_ref, out_ref):
     pieces = part_ref[1024:, :].astype(jnp.float32)
     levels = pieces[0:8] + (pieces[8:16] + (pieces[16:24] + pieces[24:32]))
     for t in range(8):
@@ -259,7 +265,7 @@
         mixed = (own / weight + extra_ref[rows, :]).astype(jnp.bfloat16)
         to = t if t < 4 else 7 - t
         half = t // 4
-        out_ref[j ^ to, half * 128:(half + 1) * 128, :] = mixed
+        out_ref[to, half * 128:(half + 1) * 128, :] = mixed
 
 
 def memory_kernel(where_ref, len_ref, gate_ref, q_ref, audio_ref, video_ref, out_ref):
@@ -282,13 +288,11 @@
         out_ref[high * 512:(high + 1) * 512, :] = mixed
 
 
-def project_kernel(where_ref, m0, m1, m2, m3, w_ref, out_ref, mixed):
-    j = where_ref[1]
-
+def project_kernel(got_ref, w_ref, out_ref, mixed):
     @pl.when(pl.program_id(0) == 0)
     def _():
-        for k, m in enumerate((m0, m1, m2, m3)):
-            mixed[:, pl.ds(pl.multiple_of((j ^ k) * HD, HD), HD)] = m[...]
+        for j in range(4):
+            mixed[:, j * HD:(j + 1) * HD] = got_ref[j]
 
     part = jnp.dot(mixed[...], w_ref[...], preferred_element_type=jnp.float32)
     part = part.astype(jnp.bfloat16)
@@ -297,7 +301,7 @@
 
 
 def cost(us):
-    return pl.CostEstimate(flops=int(us * 1.15e9), bytes_accessed=2**20, transcendentals=0)
+    return pl.CostEstimate(flops=int(us * 1.15e9), bytes_accessed=1024, transcendentals=0)
 
 
 def after(array, token):
@@ -311,6 +315,7 @@
         out_specs=anywhere(),
         input_output_aliases={0: 0},
         compiler_params=params(),
+        cost_estimate=cost(0.001),
         name="after",
     )(array, token)
 
@@ -331,21 +336,31 @@
         [lax.axis_index("yl"), j, lax.axis_index("z0"), lax.axis_index("c")]
     ).astype(jnp.int32)
 
-    span_packed, cache_packed = pl.pallas_call(
+    span_packed = pl.pallas_call(
         pack_kernel,
-        out_shape=(b16(32, 3, 32, HD), b16(4, 2, 128, HD)),
-        in_specs=[scalars(), whole(), whole()],
-        out_specs=(whole(),) * 2,
-        compiler_params=params(),
+        grid=(3,),
+        out_shape=b16(32, 3, 32, HD),
+        in_specs=[pl.BlockSpec((1, 32, 4096), lambda n: (n, 0, 0))],
+        out_specs=pl.BlockSpec((32, 1, 32, HD), lambda n: (0, n, 0, 0)),
+        compiler_params=params(60 * 2**20),
         cost_estimate=cost(2),
         name="pack",
-    )(where, span_qkv, cache_kv)
+    )(span_qkv)
+    cache_packed = pl.pallas_call(
+        pack_cache_kernel,
+        out_shape=b16(4, 2, 128, HD),
+        in_specs=[scalars(), whole(), anywhere()],
+        out_specs=whole(),
+        compiler_params=params(),
+        cost_estimate=cost(1),
+        name="pack_cache",
+    )(where, cache_kv, span_packed)
 
     def swap(part, axis):
         return lax.ppermute(part, axis, xor_perm(2, 1))
 
     def swap_z(parts):
-        return [parts[0]] + [lax.ppermute(parts[k], ZZ, xor_perm(4, k)) for k in range(1, 4)]
+        return [parts[0]] + [lax.ppermute(parts[k], ZZ, turn_perm(4, k)) for k in range(1, 4)]
 
     own_bias, near_bias = pl.pallas_call(
         bias_kernel,
@@ -366,7 +381,7 @@
             in_specs=[whole()] * 5 + [anywhere()],
             out_specs=(whole(),) * len(outs),
             compiler_params=params(),
-            cost_estimate=cost(0.1),
+            cost_estimate=cost(0.001),
             name=name,
         )(got, *cache_own, token)
 
@@ -394,7 +409,7 @@
         ),
         out_shape=f32(1024, HD),
         compiler_params=params(),
-        cost_estimate=cost(0.1),
+        cost_estimate=cost(0.001),
         name="memories",
     )(where, mem_lengths, cross_gates, queries, audio_kv, video_kv)
 
@@ -405,7 +420,7 @@
             in_specs=[whole()] * 4,
             out_specs=(whole(),) * 3,
             compiler_params=params(),
-            cost_estimate=cost(0.1),
+            cost_estimate=cost(0.001),
             name="own_keys",
         )(q, kv_own, sibling_keys, own_bias)
 
@@ -443,27 +458,28 @@
     state = pl.pallas_call(
         combine_kernel,
         out_shape=b16(4, 256, HD),
-        in_specs=[scalars()] + [whole()] * 5,
+        in_specs=[whole()] * 5,
         out_specs=whole(),
         compiler_params=params(),
         cost_estimate=cost(1),
         name="combine",
-    )(where, *state, part, extra)
-
-    mixed = [state[0]] + [lax.ppermute(state[k], ZZ, xor_perm(4, k)) for k in range(1, 4)]
+    )(*state, part, extra)
+
+    mixed = lax.all_to_all(state, ZZ, split_axis=0, concat_axis=0, tiled=True)
     partial_sums = pl.pallas_call(
         project_kernel,
         grid=(4,),
         out_shape=b16(8, 32, 4096),
-        in_specs=[scalars()]
-        + [pl.BlockSpec((256, HD), lambda i: (0, 0))] * 4
-        + [pl.BlockSpec((512, 1024), lambda i: (0, i))],
+        in_specs=[
+            pl.BlockSpec((4, 256, HD), lambda i: (0, 0, 0)),
+            pl.BlockSpec((512, 1024), lambda i: (0, i)),
+        ],
         out_specs=pl.BlockSpec((8, 32, 1024), lambda i: (0, 0, i)),
         scratch_shapes=[pltpu.VMEM((256, 512), jnp.bfloat16)],
         compiler_params=params(),
         cost_estimate=cost(3),
         name="project",
-    )(where, *mixed, out_weight)
+    )(mixed, out_weight)
     gathered = lax.all_to_all(partial_sums, HEADS, split_axis=0, concat_axis=0, tiled=True)
     return jnp.sum(gathered.astype(jnp.float32), axis=0).astype(jnp.bfloat16)
 

time: 132 us -> 130 us (0.985); the launches traced: 130 us -> 130 us
  blocking collectives: 31.9 us -> 44.4 us
  waiting for transfers between devices: 38.3 us -> 29.9 us
  starting transfers between devices: 27.2 us -> 22.6 us
    all_to_all x0 -> x1, blocking collectives: none -> 14 us  [shards(): mixed = lax.all_to_all(state, ZZ, split_axis=0, concat_axis=0, tiled=True)]
    ppermute x6 -> x3, waiting for transfers between devices: 22.7 us -> 13.6 us  [swap_z(): lax.ppermute(parts[k], ZZ, turn_perm(4, k))]
    ppermute x6 -> x3, starting transfers between devices: 13.1 us -> 8.63 us  [swap_z(): lax.ppermute(parts[k], ZZ, turn_perm(4, k))]
    all_to_all x1, blocking collectives: 31.9 us -> 30.4 us  [shards(): lax.all_to_all(partial_sums, HEADS, split_axis=0, concat_axis=0, tiled=True)]
    pallas_call x2 -> x3, Pallas kernels: 2.48 us -> 3.96 us  [the longest x1 2.98 us: shards(): pl.pallas_call(pack_kernel, grid=(3,), out_shape=b16(32, 3, 32, HD), in_s...]
  transfers between devices with their start and end apart: 12 -> 9, of which waited for: 8 -> 6; matrix products, arithmetic and copies ran while one was open for 1% -> 1% of each run, Pallas kernels for 15% -> 16%
where the time goes in v4:
time: 130 us
  blocking collectives  44.4 us (34%)
  waiting for transfers between devices  29.9 us (23%)
  Pallas kernels  29 us (22%)
  starting transfers between devices  22.6 us (17%)
  local copies, waits for them, and re-layouts  2.69 us (2%)
    all_to_all x1, blocking collectives, shards(): lax.all_to_all(partial_sums, HEADS, split_axis=0, concat_axis=0, tiled=True)  30.4 us
    all_to_all x1, blocking collectives, shards(): mixed = lax.all_to_all(state, ZZ, split_axis=0, concat_axis=0, tiled=True)  14 us
    ppermute x3, waiting for transfers between devices, swap_z(): lax.ppermute(parts[k], ZZ, turn_perm(4, k))  13.6 us
    all_to_all x1, starting transfers between devices, shards(): lax.all_to_all(span_packed, ZZ + HEADS, split_axis=0, concat_axis=0, tile...  13 us
    ppermute x5, waiting for transfers between devices, swap(): return lax.ppermute(part, axis, xor_perm(2, 1))  13 us
    ppermute x3, starting transfers between devices, swap_z(): lax.ppermute(parts[k], ZZ, turn_perm(4, k))  8.63 us
    pallas_call x2, Pallas kernels, near(): pl.pallas_call(functools.partial(near_kernel, which, cores), out_shape=(f...  8.04 us
    pallas_call x2, Pallas kernels, own(): pl.pallas_call(functools.partial(own_kernel, which), out_shape=(f32(1024,...  7.24 us
  transfers between devices with their start and end apart: 9, of which 6 were waited for; matrix products, arithmetic and copies ran while one was open for 1% of the time, Pallas kernels for 16%

profile of v4, /device:TPU:32, one launch (start us, length us, event | category | flops | bytes accessed | tf_op | source)
XLA Modules:
  0.0 129.9 jit_solution(16386891348419557432)
XLA Ops:
  0.0 0.0 copy-start.6
  0.0 3.0 %pack.1.token_ref = bf16[32,3,32,128]{3,2,1,0:T(8,128)(2,1)} custom-call(bf16[3,32,4096]{2,1,0:T(8,128)(2,1)} %span_ref.1), custom_call_target="tpu_custom_call" | custom-call | flops 2300000000 | bytes 1024 | tf_op jit(solution)/shard_map/pack/pallas_call | solution.py:339
  3.0 13.0 %all-to-all-start = ((bf16[32,3,32,128]{3,2,1,0:T(8,128)(2,1)}), bf16[32,3,32,128]{3,2,1,0:T(8,128)(2,1)S(1)}, u32[]{:S(2)}, u32[]{:S(2)}) async-start(bf16[32,3,32,128]{3,2,1,0:T(8,128)(2,1)} %pack.1.token_ref), calls=%async_computation | async-start | bytes 1572864 | tf_op jit(solution)/shard_map/all_to_all | solution.py:375
  16.0 0.1 pad_add_fusion.where_ref
  16.1 0.0 copy-done.6
  16.1 0.0 copy-start.2
  16.1 1.1 copy-done.2
  17.3 0.0 copy-start.9
  17.3 0.6 pack_cache.1
  17.9 0.7 slice_bitcast_fusion
  18.5 3.9 %collective-permute-start.2 = (bf16[2,128,128]{2,1,0:T(8,128)(2,1)}, bf16[2,128,128]{2,1,0:T(8,128)(2,1)S(1)}, u32[]{:S(2)}, u32[]{:S(2)}) collective-permute-start(bf16[2,128,128]{2,1,0:T(8,128)(2,1)} %get-tuple-element.37), channel_id=1, source_target_pairs={{0,96},{32,0},{64,32},{96,64},{1,97},{33,1},{65,33},{97,65},{2,98}... | collective-permute-start | bytes 196616 | tf_op jit(solution)/shard_map/ppermute | solution.py:363
  22.5 2.3 %collective-permute-start.1 = (bf16[2,128,128]{2,1,0:T(8,128)(2,1)}, bf16[2,128,128]{2,1,0:T(8,128)(2,1)S(1)}, u32[]{:S(2)}, u32[]{:S(2)}) collective-permute-start(bf16[2,128,128]{2,1,0:T(8,128)(2,1)} %get-tuple-element.38), channel_id=1, source_target_pairs={{0,64},{32,96},{64,0},{96,32},{1,65},{33,97},{65,1},{97,33},{2,66}... | collective-permute-start | bytes 196616 | tf_op jit(solution)/shard_map/ppermute | solution.py:363
  24.8 2.4 %collective-permute-start = (bf16[2,128,128]{2,1,0:T(8,128)(2,1)}, bf16[2,128,128]{2,1,0:T(8,128)(2,1)S(1)}, u32[]{:S(2)}, u32[]{:S(2)}) collective-permute-start(bf16[2,128,128]{2,1,0:T(8,128)(2,1)} %get-tuple-element.39), channel_id=1, source_target_pairs={{0,32},{32,64},{64,96},{96,0},{1,33},{33,65},{65,97},{97,1},{2,34}... | collective-permute-start | bytes 196616 | tf_op jit(solution)/shard_map/ppermute | solution.py:363
  27.2 0.0 copy-done.9
  27.2 0.1 copy.12.mask_ref
  27.3 1.5 %bias.1 = (f32[32,3072]{1,0:T(8,128)S(1)}, f32[32,3072]{1,0:T(8,128)S(1)}) custom-call(s32[4]{0:T(128)S(1)} %pad_add_fusion.where_ref, s32[1,128,192]{2,1,0:T(8,128)S(1)} %copy.12.mask_ref), custom_call_target="tpu_custom_call" | custom-call | flops 2300000000 | bytes 1024 | tf_op jit(solution)/shard_map/bias/pallas_call | solution.py:365
  28.8 0.0 copy-start.7
  28.8 0.8 copy-done.7
  29.6 0.0 copy-start
  29.6 0.0 copy-start.1
  29.6 0.0 copy-start.3
  29.6 0.0 copy-start.4
  29.6 7.4 %collective-permute-done.2.c3_ref = bf16[2,128,128]{2,1,0:T(8,128)(2,1)S(1)} collective-permute-done((bf16[2,128,128]{2,1,0:T(8,128)(2,1)}, bf16[2,128,128]{2,1,0:T(8,128)(2,1)S(1)}, u32[]{:S(2)}, u32[]{:S(2)}) %collective-permute-start.2) | collective-permute-done | bytes 65568 | tf_op jit(solution)/shard_map/ppermute | solution.py:363
  37.0 6.2 %collective-permute-done.1.c2_ref = bf16[2,128,128]{2,1,0:T(8,128)(2,1)S(1)} collective-permute-done((bf16[2,128,128]{2,1,0:T(8,128)(2,1)}, bf16[2,128,128]{2,1,0:T(8,128)(2,1)S(1)}, u32[]{:S(2)}, u32[]{:S(2)}) %collective-permute-start.1) | collective-permute-done | bytes 65568 | tf_op jit(solution)/shard_map/ppermute | solution.py:363
  43.2 0.0 collective-permute-done.c1_ref
  43.2 3.3 %all-to-all-done.got_ref = bf16[32,3,32,128]{3,2,1,0:T(8,128)(2,1)S(1)} async-done(((bf16[32,3,32,128]{3,2,1,0:T(8,128)(2,1)}), bf16[32,3,32,128]{3,2,1,0:T(8,128)(2,1)S(1)}, u32[]{:S(2)}, u32[]{:S(2)}) %all-to-all-start) | async-done | bytes 786464 | tf_op jit(solution)/shard_map/all_to_all | solution.py:375
  46.5 0.1 unpack_keys.1.token_ref
  46.6 0.1 unpack_rest.1
  46.7 0.1 collective-permute-start.5
  46.8 0.8 collective-permute-start.3
  47.5 0.0 collective-permute-start.4
  47.5 0.0 copy-done
  47.5 0.0 copy-done.1
  47.5 0.0 copy-done.3
  47.5 0.0 copy-done.4
  47.5 2.8 %memories.1.token_ref.extra_ref = f32[1024,128]{1,0:T(8,128)S(1)} custom-call(s32[4]{0:T(128)S(1)} %pad_add_fusion.where_ref, s32[2]{0:T(128)S(1)} %copy-done.4, f32[2,4]{1,0:T(2,128)S(1)} %copy-done.3, bf16[1024,128]{1,0:T(8,128)(2,1)S(1)} %get-tuple-element.22.q_ref, bf16[2,512,512]{2,1,0:T(8,128)(2,1)S(1)} %copy-done, bf16[2,512,512]{2,1,0:T(8,128)(2,1)S(1)} %copy-done.1), custom_call_target="tpu_custom_call" | custom-call | flops 1150000 | bytes 1024 | tf_op jit(solution)/shard_map/memories/pallas_call | solution.py:396
  50.4 0.0 collective-permute-done.5.array_ref
  50.4 3.6 %own_keys.2 = (f32[1024,128]{1,0:T(8,128)S(1)}, f32[1024,128]{1,0:T(8,128)S(1)}, f32[1024,128]{1,0:T(8,128)S(1)}) custom-call(bf16[1024,128]{1,0:T(8,128)(2,1)S(1)} %get-tuple-element.22.q_ref, bf16[2,1536,128]{2,1,0:T(8,128)(2,1)S(1)} %get-tuple-element.23.kv0, bf16[2,1536,128]{2,1,0:T(8,128)(2,1)S(1)} %after.3.kv1, ...), custom_call_target="tpu_custom_call" | custom-call | flops 1150000 | bytes 1024 | tf_op jit(solution)/shard_map/own_keys/pallas_call | solution.py:417
  54.0 1.9 %collective-permute-done.4.array_ref = bf16[1024,128]{1,0:T(8,128)(2,1)S(1)} collective-permute-done((bf16[1024,128]{1,0:T(8,128)(2,1)S(1)}, bf16[1024,128]{1,0:T(8,128)(2,1)S(1)}, u32[]{:S(2)}, u32[]{:S(2)}) %collective-permute-start.4) | collective-permute-done | bytes 262176 | tf_op jit(solution)/shard_map/ppermute | solution.py:360
  55.9 0.0 copy-start.8
  55.9 3.7 %own_keys.3 = (f32[1024,128]{1,0:T(8,128)S(1)}, f32[1024,128]{1,0:T(8,128)S(1)}, f32[1024,128]{1,0:T(8,128)S(1)}) custom-call(bf16[1024,128]{1,0:T(8,128)(2,1)S(1)} %after.4.q_ref, bf16[2,1536,128]{2,1,0:T(8,128)(2,1)S(1)} %get-tuple-element.23.kv0, bf16[2,1536,128]{2,1,0:T(8,128)(2,1)S(1)} %after.3.kv1, f32[32,3072]{1,0:T(8,128)S(1)} %get-tuple-element.21.token_ref.bias_ref), custom_call_target="tpu_custom_call" | custom-call | flops 1150000 | bytes 1024 | tf_op jit(solution)/shard_map/own_keys/pallas_call | solution.py:417
  59.6 7.2 %collective-permute-done.3.array_ref = bf16[2,1536,128]{2,1,0:T(8,128)(2,1)S(1)} collective-permute-done((bf16[2,1536,128]{2,1,0:T(8,128)(2,1)S(1)}, bf16[2,1536,128]{2,1,0:T(8,128)(2,1)S(1)}, u32[]{:S(2)}, u32[]{:S(2)}) %collective-permute-start.3) | collective-permute-done | bytes 786464 | tf_op jit(solution)/shard_map/ppermute | solution.py:360
  66.7 0.0 collective-permute-start.6
  66.7 0.0 copy-done.8
  66.7 3.1 %near_keys.3 = (f32[1024,128]{1,0:T(8,128)S(1)}, f32[1024,128]{1,0:T(8,128)S(1)}, f32[1024,128]{1,0:T(8,128)S(1)}) custom-call(s32[4]{0:T(128)S(1)} %pad_add_fusion.where_ref, bf16[1024,128]{1,0:T(8,128)(2,1)S(1)} %after.4.q_ref, bf16[2,1536,128]{2,1,0:T(8,128)(2,1)S(1)} %after.5.refs_0_, f32[32,3072]{1,0:T(8,128)S(1)} %copy-done.8, ...), custom_call_target="tpu_custom_call" | custom-call | flops 2875000064 | bytes 1024 | tf_op jit(solution)/shard_map/near_keys/pallas_call | solution.py:435
  69.8 0.0 collective-permute-done.6.refs_1_.kv_ref
  69.8 3.0 %near_keys_partner.1 = bf16[1056,128]{1,0:T(8,128)(2,1)S(1)} custom-call(s32[4]{0:T(128)S(1)} %pad_add_fusion.where_ref, bf16[1024,128]{1,0:T(8,128)(2,1)S(1)} %after.4.q_ref, bf16[2,1536,128]{2,1,0:T(8,128)(2,1)S(1)} %collective-permute-done.6.refs_1_.kv_ref, f32[32,3072]{1,0:T(8,128)S(1)} %copy-done.8, f32[1024,128]{1,0:T(8,128)S(1)} %get-tuple-element.34.t_ref, ...), custom_call_target="tpu_custom_call" | custom-call | flops 3449999872 | bytes 1024 | tf_op jit(solution)/shard_map/near_keys_partner/pallas_call | solution.py:446
  72.9 0.1 collective-permute-start.7
  73.0 4.9 %near_keys.2 = (f32[1024,128]{1,0:T(8,128)S(1)}, f32[1024,128]{1,0:T(8,128)S(1)}, f32[1024,128]{1,0:T(8,128)S(1)}) custom-call(s32[4]{0:T(128)S(1)} %pad_add_fusion.where_ref, bf16[1024,128]{1,0:T(8,128)(2,1)S(1)} %get-tuple-element.22.q_ref, bf16[2,1536,128]{2,1,0:T(8,128)(2,1)S(1)} %after.5.refs_0_, ...), custom_call_target="tpu_custom_call" | custom-call | flops 5750000128 | bytes 1024 | tf_op jit(solution)/shard_map/near_keys/pallas_call | solution.py:435
  77.9 4.0 %collective-permute-done.7.part_ref = bf16[1056,128]{1,0:T(8,128)(2,1)S(1)} collective-permute-done((bf16[1056,128]{1,0:T(8,128)(2,1)S(1)}, bf16[1056,128]{1,0:T(8,128)(2,1)S(1)}, u32[]{:S(2)}, u32[]{:S(2)}) %collective-permute-start.7) | collective-permute-done | bytes 270368 | tf_op jit(solution)/shard_map/ppermute | solution.py:360
  81.9 0.0 copy-start.5
  81.9 0.4 combine.1
  82.3 14.0 %all_to_all.15.got_ref = bf16[4,256,128]{2,1,0:T(8,128)(2,1)S(1)} all-to-all(bf16[4,256,128]{2,1,0:T(8,128)(2,1)S(1)} %combine.1), channel_id=1, replica_groups=mesh['yl'=2,'z2'=2,'z1'=2,'z0'=2,'c'=2,'x'=4,'yh'=2] {'z2','z1'}, dimensions={0} | all-to-all | bytes 524288 | tf_op jit(solution)/shard_map/all_to_all | solution.py:468
  96.3 0.0 copy-done.5
  96.3 2.2 %project.1 = bf16[8,32,4096]{2,1,0:T(8,128)(2,1)S(1)} custom-call(bf16[4,256,128]{2,1,0:T(8,128)(2,1)S(1)} %all_to_all.15.got_ref, bf16[512,4096]{1,0:T(8,128)(2,1)S(1)} %copy-done.5), custom_call_target="tpu_custom_call" | custom-call | flops 3449999872 | bytes 1024 | tf_op jit(solution)/shard_map/project/pallas_call | solution.py:469
  98.5 30.4 %all_to_all.16 = bf16[8,32,4096]{2,1,0:T(8,128)(2,1)S(1)} all-to-all(bf16[8,32,4096]{2,1,0:T(8,128)(2,1)S(1)} %project.1), channel_id=1, replica_groups=mesh['yl'=2,'z2'=2,'z1'=2,'z0'=2,'c'=2,'x'=4,'yh'=2] {'x','yh'}, dimensions={0} | all-to-all | bytes 4194304 | tf_op jit(solution)/shard_map/all_to_all | solution.py:483
  128.9 1.1 reduce_sum.12
  (3 shorter events, 0.0 us)
Async XLA Ops:
  0.0 16.1 %copy-start.6 = (bf16[2,128,512]{2,1,0:T(8,128)(2,1)S(1)}, bf16[2,128,512]{2,1,0:T(8,128)(2,1)}, u32[]{:S(2)}) copy-start(bf16[2,128,512]{2,1,0:T(8,128)(2,1)} %cache_ref.1) | copy-start | bytes 786436
  3.0 43.5 %all-to-all-start = ((bf16[32,3,32,128]{3,2,1,0:T(8,128)(2,1)}), bf16[32,3,32,128]{3,2,1,0:T(8,128)(2,1)S(1)}, u32[]{:S(2)}, u32[]{:S(2)}) async-start(bf16[32,3,32,128]{3,2,1,0:T(8,128)(2,1)} %pack.1.token_ref), calls=%async_computation | async-start | bytes 1572864 | tf_op jit(solution)/shard_map/all_to_all | solution.py:375
  16.1 1.1 copy-start.2
  17.3 9.9 %copy-start.9 = (s32[1,128,192]{1,2,0:T(8,128)S(1)}, s32[1,128,192]{1,2,0:T(8,128)}, u32[]{:S(2)}) copy-start(s32[1,128,192]{1,2,0:T(8,128)} %param.12) | copy-start | bytes 294916
  18.5 18.5 %collective-permute-start.2 = (bf16[2,128,128]{2,1,0:T(8,128)(2,1)}, bf16[2,128,128]{2,1,0:T(8,128)(2,1)S(1)}, u32[]{:S(2)}, u32[]{:S(2)}) collective-permute-start(bf16[2,128,128]{2,1,0:T(8,128)(2,1)} %get-tuple-element.37), channel_id=1, source_target_pairs={{0,96},{32,0},{64,32},{96,64},{1,97},{33,1},{65,33},{97,65},{2,98}... | collective-permute-start | bytes 196616 | tf_op jit(solution)/shard_map/ppermute | solution.py:363
  22.5 20.7 %collective-permute-start.1 = (bf16[2,128,128]{2,1,0:T(8,128)(2,1)}, bf16[2,128,128]{2,1,0:T(8,128)(2,1)S(1)}, u32[]{:S(2)}, u32[]{:S(2)}) collective-permute-start(bf16[2,128,128]{2,1,0:T(8,128)(2,1)} %get-tuple-element.38), channel_id=1, source_target_pairs={{0,64},{32,96},{64,0},{96,32},{1,65},{33,97},{65,1},{97,33},{2,66}... | collective-permute-start | bytes 196616 | tf_op jit(solution)/shard_map/ppermute | solution.py:363
  24.8 18.4 %collective-permute-start = (bf16[2,128,128]{2,1,0:T(8,128)(2,1)}, bf16[2,128,128]{2,1,0:T(8,128)(2,1)S(1)}, u32[]{:S(2)}, u32[]{:S(2)}) collective-permute-start(bf16[2,128,128]{2,1,0:T(8,128)(2,1)} %get-tuple-element.39), channel_id=1, source_target_pairs={{0,32},{32,64},{64,96},{96,0},{1,33},{33,65},{65,97},{97,1},{2,34}... | collective-permute-start | bytes 196616 | tf_op jit(solution)/shard_map/ppermute | solution.py:363
  28.8 0.8 copy-start.7
  29.6 17.9 %copy-start = (bf16[2,512,512]{2,1,0:T(8,128)(2,1)S(1)}, bf16[2,512,512]{2,1,0:T(8,128)(2,1)}, u32[]{:S(2)}) copy-start(bf16[2,512,512]{2,1,0:T(8,128)(2,1)} %audio_ref.1) | copy-start | bytes 3145732
  29.6 17.9 %copy-start.1 = (bf16[2,512,512]{2,1,0:T(8,128)(2,1)S(1)}, bf16[2,512,512]{2,1,0:T(8,128)(2,1)}, u32[]{:S(2)}) copy-start(bf16[2,512,512]{2,1,0:T(8,128)(2,1)} %video_ref.1) | copy-start | bytes 3145732
  29.6 17.9 %copy-start.3 = (f32[2,4]{1,0:T(2,128)S(1)}, f32[2,4]{1,0:T(2,128)}, u32[]{:S(2)}) copy-start(f32[2,4]{1,0:T(2,128)} %gate_ref.1) | copy-start | bytes 100
  29.6 17.9 %copy-start.4 = (s32[2]{0:T(128)S(1)}, s32[2]{0:T(128)}, u32[]{:S(2)}) copy-start(s32[2]{0:T(128)} %len_ref.1) | copy-start | bytes 28
  46.7 3.7 %collective-permute-start.5 = (bf16[2,1536,128]{2,1,0:T(8,128)(2,1)S(1)}, bf16[2,1536,128]{2,1,0:T(8,128)(2,1)S(1)}, u32[]{:S(2)}, u32[]{:S(2)}) collective-permute-start(bf16[2,1536,128]{2,1,0:T(8,128)(2,1)S(1)} %get-tuple-element.23.kv0), channel_id=1, source_target_pairs={{0,8},{8,0},{1,9},{9,1},{2,10},{10,2},{3,11},{11,3},{4,12},{12,4},... | collective-permute-start | bytes 2359304 | tf_op jit(solution)/shard_map/ppermute | solution.py:360
  46.8 20.0 %collective-permute-start.3 = (bf16[2,1536,128]{2,1,0:T(8,128)(2,1)S(1)}, bf16[2,1536,128]{2,1,0:T(8,128)(2,1)S(1)}, u32[]{:S(2)}, u32[]{:S(2)}) collective-permute-start(bf16[2,1536,128]{2,1,0:T(8,128)(2,1)S(1)} %unpack_keys.1.token_ref), channel_id=1, source_target_pairs={{0,128},{128,0},{1,129},{129,1},{2,130},{130,2},{3,131},{131,3},{4... | collective-permute-start | bytes 2359304 | tf_op jit(solution)/shard_map/ppermute | solution.py:360
  47.5 8.4 %collective-permute-start.4 = (bf16[1024,128]{1,0:T(8,128)(2,1)S(1)}, bf16[1024,128]{1,0:T(8,128)(2,1)S(1)}, u32[]{:S(2)}, u32[]{:S(2)}) collective-permute-start(bf16[1024,128]{1,0:T(8,128)(2,1)S(1)} %get-tuple-element.22.q_ref), channel_id=1, source_target_pairs={{0,16},{16,0},{1,17},{17,1},{2,18},{18,2},{3,19},{19,3},{4,20},{20... | collective-permute-start | bytes 786440 | tf_op jit(solution)/shard_map/ppermute | solution.py:360
  55.9 10.8 %copy-start.8 = (f32[32,3072]{1,0:T(8,128)S(1)}, f32[32,3072]{1,0:T(8,128)}, u32[]{:S(2)}) copy-start(f32[32,3072]{1,0:T(8,128)} %copy-done.7) | copy-start | bytes 1179652
  66.7 3.1 %collective-permute-start.6 = (bf16[2,1536,128]{2,1,0:T(8,128)(2,1)S(1)}, bf16[2,1536,128]{2,1,0:T(8,128)(2,1)S(1)}, u32[]{:S(2)}, u32[]{:S(2)}) collective-permute-start(bf16[2,1536,128]{2,1,0:T(8,128)(2,1)S(1)} %after.5.refs_0_), channel_id=1, source_target_pairs={{0,8},{8,0},{1,9},{9,1},{2,10},{10,2},{3,11},{11,3},{4,12},{12,4},... | collective-permute-start | bytes 2359304 | tf_op jit(solution)/shard_map/ppermute | solution.py:360
  72.9 9.0 %collective-permute-start.7 = (bf16[1056,128]{1,0:T(8,128)(2,1)S(1)}, bf16[1056,128]{1,0:T(8,128)(2,1)S(1)}, u32[]{:S(2)}, u32[]{:S(2)}) collective-permute-start(bf16[1056,128]{1,0:T(8,128)(2,1)S(1)} %near_keys_partner.1), channel_id=1, source_target_pairs={{0,16},{16,0},{1,17},{17,1},{2,18},{18,2},{3,19},{19,3},{4,20},{20... | collective-permute-start | bytes 811016 | tf_op jit(solution)/shard_map/ppermute | solution.py:360
  81.9 14.4 %copy-start.5 = (bf16[512,4096]{1,0:T(8,128)(2,1)S(1)}, bf16[512,4096]{1,0:T(8,128)(2,1)}, u32[]{:S(2)}) copy-start(bf16[512,4096]{1,0:T(8,128)(2,1)} %w_ref.1) | copy-start | bytes 12582916

commit v5 on v4

--- a/solution.py
+++ b/solution.py
@@ -38,10 +38,20 @@
     return [(i, (i + k) % count) for i in range(count)]
 
 
-def pack_kernel(span_ref, span_out):
-    for d in range(32):
-        col = ((d % 8) * 4 + d // 8) * HD
-        span_out[d, 0] = span_ref[0, :, col:col + HD]
+def pack_kernel(span_ref, span_out, span_in, packed, sems):
+    reads = [
+        pltpu.make_async_copy(span_ref.at[n], span_in.at[n], sems.at[n]) for n in range(3)
+    ]
+    for copy in reads:
+        copy.start()
+    for n in range(3):
+        reads[n].wait()
+        for d in range(32):
+            col = ((d % 8) * 4 + d // 8) * HD
+            packed[d, n] = span_in[n, :, col:col + HD]
+    write = pltpu.make_async_copy(packed, span_out, sems.at[3])
+    write.start()
+    write.wait()
 
 
 def pack_cache_kernel(where_ref, cache_ref, token_ref, cache_out):
@@ -288,16 +298,14 @@
         out_ref[high * 512:(high + 1) * 512, :] = mixed
 
 
-def project_kernel(got_ref, w_ref, out_ref, mixed):
-    @pl.when(pl.program_id(0) == 0)
-    def _():
-        for j in range(4):
-            mixed[:, j * HD:(j + 1) * HD] = got_ref[j]
-
-    part = jnp.dot(mixed[...], w_ref[...], preferred_element_type=jnp.float32)
-    part = part.astype(jnp.bfloat16)
-    for h in range(8):
-        out_ref[h] = part[h * 32:(h + 1) * 32]
+def project_kernel(got_ref, w_ref, out_ref):
+    mixed = jnp.concatenate([got_ref[j] for j in range(4)], axis=1)
+    for n in range(4):
+        cols = slice(n * 1024, (n + 1) * 1024)
+        part = jnp.dot(mixed, w_ref[:, cols], preferred_element_type=jnp.float32)
+        part = part.astype(jnp.bfloat16)
+        for h in range(8):
+            out_ref[h, :, cols] = part[h * 32:(h + 1) * 32]
 
 
 def cost(us):
@@ -338,10 +346,14 @@
 
     span_packed = pl.pallas_call(
         pack_kernel,
-        grid=(3,),
         out_shape=b16(32, 3, 32, HD),
-        in_specs=[pl.BlockSpec((1, 32, 4096), lambda n: (n, 0, 0))],
-        out_specs=pl.BlockSpec((32, 1, 32, HD), lambda n: (0, n, 0, 0)),
+        in_specs=[anywhere()],
+        out_specs=anywhere(),
+        scratch_shapes=[
+            pltpu.VMEM((3, 32, 4096), jnp.bfloat16),
+            pltpu.VMEM((32, 3, 32, HD), jnp.bfloat16),
+            pltpu.SemaphoreType.DMA((4,)),
+        ],
         compiler_params=params(60 * 2**20),
         cost_estimate=cost(2),
         name="pack",
@@ -468,14 +480,9 @@
     mixed = lax.all_to_all(state, ZZ, split_axis=0, concat_axis=0, tiled=True)
     partial_sums = pl.pallas_call(
         project_kernel,
-        grid=(4,),
         out_shape=b16(8, 32, 4096),
-        in_specs=[
-            pl.BlockSpec((4, 256, HD), lambda i: (0, 0, 0)),
-            pl.BlockSpec((512, 1024), lambda i: (0, i)),
-        ],
-        out_specs=pl.BlockSpec((8, 32, 1024), lambda i: (0, 0, i)),
-        scratch_shapes=[pltpu.VMEM((256, 512), jnp.bfloat16)],
+        in_specs=[whole()] * 2,
+        out_specs=whole(),
         compiler_params=params(),
         cost_estimate=cost(3),
         name="project",

time: 130 us -> 128 us (0.985)
  Pallas kernels: 29 us -> 27.1 us
    pallas_call x2, Pallas kernels: 5.21 us -> 3.36 us  [the longest x1 2.11 us: shards(): pl.pallas_call(pack_kernel, out_shape=b16(32, 3, 32, HD), in_specs=[anywh...]
where the time goes in v5:
time: 128 us
  blocking collectives  44.3 us (35%)
  waiting for transfers between devices  30 us (23%)
  Pallas kernels  27.1 us (21%)
  starting transfers between devices  22.6 us (18%)
  local copies, waits for them, and re-layouts  2.69 us (2%)
    all_to_all x1, blocking collectives, shards(): lax.all_to_all(partial_sums, HEADS, split_axis=0, concat_axis=0, tiled=True)  30.3 us
    all_to_all x1, blocking collectives, shards(): mixed = lax.all_to_all(state, ZZ, split_axis=0, concat_axis=0, tiled=True)  14 us
    ppermute x3, waiting for transfers between devices, swap_z(): lax.ppermute(parts[k], ZZ, turn_perm(4, k))  13.6 us
    all_to_all x1, starting transfers between devices, shards(): lax.all_to_all(span_packed, ZZ + HEADS, split_axis=0, concat_axis=0, tile...  13.1 us
    ppermute x5, waiting for transfers between devices, swap(): return lax.ppermute(part, axis, xor_perm(2, 1))  13 us
    ppermute x3, starting transfers between devices, swap_z(): lax.ppermute(parts[k], ZZ, turn_perm(4, k))  8.63 us
    pallas_call x2, Pallas kernels, near(): pl.pallas_call(functools.partial(near_kernel, which, cores), out_shape=(f...  8.04 us
    pallas_call x2, Pallas kernels, own(): pl.pallas_call(functools.partial(own_kernel, which), out_shape=(f32(1024,...  7.24 us
  transfers between devices with their start and end apart: 9, of which 6 were waited for; matrix products, arithmetic and copies ran while one was open for 1% of the time, Pallas kernels for 16%

profile of v5, /device:TPU:32, one launch (start us, length us, event | category | flops | bytes accessed | tf_op | source)
XLA Modules:
  0.0 128.0 jit_solution(5296659754788008404)
XLA Ops:
  0.0 0.0 copy-start.6
  0.0 2.1 %pack.1.token_ref = bf16[32,3,32,128]{3,2,1,0:T(8,128)(2,1)} custom-call(bf16[3,32,4096]{2,1,0:T(8,128)(2,1)} %span_ref.1), custom_call_target="tpu_custom_call" | custom-call | flops 2300000000 | bytes 1024 | tf_op jit(solution)/shard_map/pack/pallas_call | solution.py:347
  2.1 13.1 %all-to-all-start = ((bf16[32,3,32,128]{3,2,1,0:T(8,128)(2,1)}), bf16[32,3,32,128]{3,2,1,0:T(8,128)(2,1)S(1)}, u32[]{:S(2)}, u32[]{:S(2)}) async-start(bf16[32,3,32,128]{3,2,1,0:T(8,128)(2,1)} %pack.1.token_ref), calls=%async_computation | async-start | bytes 1572864 | tf_op jit(solution)/shard_map/all_to_all | solution.py:387
  15.2 0.1 pad_add_fusion.where_ref
  15.3 0.0 copy-done.6
  15.3 0.0 copy-start.2
  15.3 1.1 copy-done.2
  16.4 0.0 copy-start.9
  16.4 0.6 pack_cache.1
  17.0 0.7 slice_bitcast_fusion
  17.7 3.9 %collective-permute-start.2 = (bf16[2,128,128]{2,1,0:T(8,128)(2,1)}, bf16[2,128,128]{2,1,0:T(8,128)(2,1)S(1)}, u32[]{:S(2)}, u32[]{:S(2)}) collective-permute-start(bf16[2,128,128]{2,1,0:T(8,128)(2,1)} %get-tuple-element.37), channel_id=1, source_target_pairs={{0,96},{32,0},{64,32},{96,64},{1,97},{33,1},{65,33},{97,65},{2,98}... | collective-permute-start | bytes 196616 | tf_op jit(solution)/shard_map/ppermute | solution.py:375
  21.6 2.3 %collective-permute-start.1 = (bf16[2,128,128]{2,1,0:T(8,128)(2,1)}, bf16[2,128,128]{2,1,0:T(8,128)(2,1)S(1)}, u32[]{:S(2)}, u32[]{:S(2)}) collective-permute-start(bf16[2,128,128]{2,1,0:T(8,128)(2,1)} %get-tuple-element.38), channel_id=1, source_target_pairs={{0,64},{32,96},{64,0},{96,32},{1,65},{33,97},{65,1},{97,33},{2,66}... | collective-permute-start | bytes 196616 | tf_op jit(solution)/shard_map/ppermute | solution.py:375
  23.9 2.4 %collective-permute-start = (bf16[2,128,128]{2,1,0:T(8,128)(2,1)}, bf16[2,128,128]{2,1,0:T(8,128)(2,1)S(1)}, u32[]{:S(2)}, u32[]{:S(2)}) collective-permute-start(bf16[2,128,128]{2,1,0:T(8,128)(2,1)} %get-tuple-element.39), channel_id=1, source_target_pairs={{0,32},{32,64},{64,96},{96,0},{1,33},{33,65},{65,97},{97,1},{2,34}... | collective-permute-start | bytes 196616 | tf_op jit(solution)/shard_map/ppermute | solution.py:375
  26.3 0.0 copy-done.9
  26.3 0.1 copy.12.mask_ref
  26.4 1.5 %bias.1 = (f32[32,3072]{1,0:T(8,128)S(1)}, f32[32,3072]{1,0:T(8,128)S(1)}) custom-call(s32[4]{0:T(128)S(1)} %pad_add_fusion.where_ref, s32[1,128,192]{2,1,0:T(8,128)S(1)} %copy.12.mask_ref), custom_call_target="tpu_custom_call" | custom-call | flops 2300000000 | bytes 1024 | tf_op jit(solution)/shard_map/bias/pallas_call | solution.py:377
  28.0 0.0 copy-start.7
  28.0 0.8 copy-done.7
  28.7 0.0 copy-start
  28.7 0.0 copy-start.1
  28.7 0.0 copy-start.3
  28.7 0.0 copy-start.4
  28.8 7.4 %collective-permute-done.2.c3_ref = bf16[2,128,128]{2,1,0:T(8,128)(2,1)S(1)} collective-permute-done((bf16[2,128,128]{2,1,0:T(8,128)(2,1)}, bf16[2,128,128]{2,1,0:T(8,128)(2,1)S(1)}, u32[]{:S(2)}, u32[]{:S(2)}) %collective-permute-start.2) | collective-permute-done | bytes 65568 | tf_op jit(solution)/shard_map/ppermute | solution.py:375
  36.2 6.2 %collective-permute-done.1.c2_ref = bf16[2,128,128]{2,1,0:T(8,128)(2,1)S(1)} collective-permute-done((bf16[2,128,128]{2,1,0:T(8,128)(2,1)}, bf16[2,128,128]{2,1,0:T(8,128)(2,1)S(1)}, u32[]{:S(2)}, u32[]{:S(2)}) %collective-permute-start.1) | collective-permute-done | bytes 65568 | tf_op jit(solution)/shard_map/ppermute | solution.py:375
  42.4 0.0 collective-permute-done.c1_ref
  42.4 3.3 %all-to-all-done.got_ref = bf16[32,3,32,128]{3,2,1,0:T(8,128)(2,1)S(1)} async-done(((bf16[32,3,32,128]{3,2,1,0:T(8,128)(2,1)}), bf16[32,3,32,128]{3,2,1,0:T(8,128)(2,1)S(1)}, u32[]{:S(2)}, u32[]{:S(2)}) %all-to-all-start) | async-done | bytes 786464 | tf_op jit(solution)/shard_map/all_to_all | solution.py:387
  45.7 0.1 unpack_keys.1.token_ref
  45.7 0.1 unpack_rest.1
  45.8 0.1 collective-permute-start.5
  45.9 0.8 collective-permute-start.3
  46.7 0.0 collective-permute-start.4
  46.7 0.0 copy-done
  46.7 0.0 copy-done.1
  46.7 0.0 copy-done.3
  46.7 0.0 copy-done.4
  46.7 2.8 %memories.1.token_ref.extra_ref = f32[1024,128]{1,0:T(8,128)S(1)} custom-call(s32[4]{0:T(128)S(1)} %pad_add_fusion.where_ref, s32[2]{0:T(128)S(1)} %copy-done.4, f32[2,4]{1,0:T(2,128)S(1)} %copy-done.3, bf16[1024,128]{1,0:T(8,128)(2,1)S(1)} %get-tuple-element.22.q_ref, bf16[2,512,512]{2,1,0:T(8,128)(2,1)S(1)} %copy-done, bf16[2,512,512]{2,1,0:T(8,128)(2,1)S(1)} %copy-done.1), custom_call_target="tpu_custom_call" | custom-call | flops 1150000 | bytes 1024 | tf_op jit(solution)/shard_map/memories/pallas_call | solution.py:408
  49.5 0.0 collective-permute-done.5.array_ref
  49.5 3.6 %own_keys.2 = (f32[1024,128]{1,0:T(8,128)S(1)}, f32[1024,128]{1,0:T(8,128)S(1)}, f32[1024,128]{1,0:T(8,128)S(1)}) custom-call(bf16[1024,128]{1,0:T(8,128)(2,1)S(1)} %get-tuple-element.22.q_ref, bf16[2,1536,128]{2,1,0:T(8,128)(2,1)S(1)} %get-tuple-element.23.kv0, bf16[2,1536,128]{2,1,0:T(8,128)(2,1)S(1)} %after.3.kv1, ...), custom_call_target="tpu_custom_call" | custom-call | flops 1150000 | bytes 1024 | tf_op jit(solution)/shard_map/own_keys/pallas_call | solution.py:429
  53.1 1.9 %collective-permute-done.4.array_ref = bf16[1024,128]{1,0:T(8,128)(2,1)S(1)} collective-permute-done((bf16[1024,128]{1,0:T(8,128)(2,1)S(1)}, bf16[1024,128]{1,0:T(8,128)(2,1)S(1)}, u32[]{:S(2)}, u32[]{:S(2)}) %collective-permute-start.4) | collective-permute-done | bytes 262176 | tf_op jit(solution)/shard_map/ppermute | solution.py:372
  55.0 0.0 copy-start.8
  55.0 3.7 %own_keys.3 = (f32[1024,128]{1,0:T(8,128)S(1)}, f32[1024,128]{1,0:T(8,128)S(1)}, f32[1024,128]{1,0:T(8,128)S(1)}) custom-call(bf16[1024,128]{1,0:T(8,128)(2,1)S(1)} %after.4.q_ref, bf16[2,1536,128]{2,1,0:T(8,128)(2,1)S(1)} %get-tuple-element.23.kv0, bf16[2,1536,128]{2,1,0:T(8,128)(2,1)S(1)} %after.3.kv1, f32[32,3072]{1,0:T(8,128)S(1)} %get-tuple-element.21.token_ref.bias_ref), custom_call_target="tpu_custom_call" | custom-call | flops 1150000 | bytes 1024 | tf_op jit(solution)/shard_map/own_keys/pallas_call | solution.py:429
  58.7 7.2 %collective-permute-done.3.array_ref = bf16[2,1536,128]{2,1,0:T(8,128)(2,1)S(1)} collective-permute-done((bf16[2,1536,128]{2,1,0:T(8,128)(2,1)S(1)}, bf16[2,1536,128]{2,1,0:T(8,128)(2,1)S(1)}, u32[]{:S(2)}, u32[]{:S(2)}) %collective-permute-start.3) | collective-permute-done | bytes 786464 | tf_op jit(solution)/shard_map/ppermute | solution.py:372
  65.9 0.0 collective-permute-start.6
  65.9 0.0 copy-done.8
  65.9 3.1 %near_keys.3 = (f32[1024,128]{1,0:T(8,128)S(1)}, f32[1024,128]{1,0:T(8,128)S(1)}, f32[1024,128]{1,0:T(8,128)S(1)}) custom-call(s32[4]{0:T(128)S(1)} %pad_add_fusion.where_ref, bf16[1024,128]{1,0:T(8,128)(2,1)S(1)} %after.4.q_ref, bf16[2,1536,128]{2,1,0:T(8,128)(2,1)S(1)} %after.5.refs_0_, f32[32,3072]{1,0:T(8,128)S(1)} %copy-done.8, ...), custom_call_target="tpu_custom_call" | custom-call | flops 2875000064 | bytes 1024 | tf_op jit(solution)/shard_map/near_keys/pallas_call | solution.py:447
  69.0 0.0 collective-permute-done.6.refs_1_.kv_ref
  69.0 3.0 %near_keys_partner.1 = bf16[1056,128]{1,0:T(8,128)(2,1)S(1)} custom-call(s32[4]{0:T(128)S(1)} %pad_add_fusion.where_ref, bf16[1024,128]{1,0:T(8,128)(2,1)S(1)} %after.4.q_ref, bf16[2,1536,128]{2,1,0:T(8,128)(2,1)S(1)} %collective-permute-done.6.refs_1_.kv_ref, f32[32,3072]{1,0:T(8,128)S(1)} %copy-done.8, f32[1024,128]{1,0:T(8,128)S(1)} %get-tuple-element.34.t_ref, ...), custom_call_target="tpu_custom_call" | custom-call | flops 3449999872 | bytes 1024 | tf_op jit(solution)/shard_map/near_keys_partner/pallas_call | solution.py:458
  72.0 0.1 collective-permute-start.7
  72.1 4.9 %near_keys.2 = (f32[1024,128]{1,0:T(8,128)S(1)}, f32[1024,128]{1,0:T(8,128)S(1)}, f32[1024,128]{1,0:T(8,128)S(1)}) custom-call(s32[4]{0:T(128)S(1)} %pad_add_fusion.where_ref, bf16[1024,128]{1,0:T(8,128)(2,1)S(1)} %get-tuple-element.22.q_ref, bf16[2,1536,128]{2,1,0:T(8,128)(2,1)S(1)} %after.5.refs_0_, ...), custom_call_target="tpu_custom_call" | custom-call | flops 5750000128 | bytes 1024 | tf_op jit(solution)/shard_map/near_keys/pallas_call | solution.py:447
  77.0 4.0 %collective-permute-done.7.part_ref = bf16[1056,128]{1,0:T(8,128)(2,1)S(1)} collective-permute-done((bf16[1056,128]{1,0:T(8,128)(2,1)S(1)}, bf16[1056,128]{1,0:T(8,128)(2,1)S(1)}, u32[]{:S(2)}, u32[]{:S(2)}) %collective-permute-start.7) | collective-permute-done | bytes 270368 | tf_op jit(solution)/shard_map/ppermute | solution.py:372
  81.0 0.0 copy-start.5
  81.0 0.4 combine.1
  81.4 14.0 %all_to_all.15.got_ref = bf16[4,256,128]{2,1,0:T(8,128)(2,1)S(1)} all-to-all(bf16[4,256,128]{2,1,0:T(8,128)(2,1)S(1)} %combine.1), channel_id=1, replica_groups=mesh['yl'=2,'z2'=2,'z1'=2,'z0'=2,'c'=2,'x'=4,'yh'=2] {'z2','z1'}, dimensions={0} | all-to-all | bytes 524288 | tf_op jit(solution)/shard_map/all_to_all | solution.py:480
  95.4 0.0 copy-done.5
  95.4 1.3 project.1
  96.7 30.3 %all_to_all.16 = bf16[8,32,4096]{2,1,0:T(8,128)(2,1)S(1)} all-to-all(bf16[8,32,4096]{2,1,0:T(8,128)(2,1)S(1)} %project.1), channel_id=1, replica_groups=mesh['yl'=2,'z2'=2,'z1'=2,'z0'=2,'c'=2,'x'=4,'yh'=2] {'x','yh'}, dimensions={0} | all-to-all | bytes 4194304 | tf_op jit(solution)/shard_map/all_to_all | solution.py:490
  127.0 1.1 reduce_sum.12
  (3 shorter events, 0.0 us)
Async XLA Ops:
  0.0 15.3 %copy-start.6 = (bf16[2,128,512]{2,1,0:T(8,128)(2,1)S(1)}, bf16[2,128,512]{2,1,0:T(8,128)(2,1)}, u32[]{:S(2)}) copy-start(bf16[2,128,512]{2,1,0:T(8,128)(2,1)} %cache_ref.1) | copy-start | bytes 786436
  2.1 43.5 %all-to-all-start = ((bf16[32,3,32,128]{3,2,1,0:T(8,128)(2,1)}), bf16[32,3,32,128]{3,2,1,0:T(8,128)(2,1)S(1)}, u32[]{:S(2)}, u32[]{:S(2)}) async-start(bf16[32,3,32,128]{3,2,1,0:T(8,128)(2,1)} %pack.1.token_ref), calls=%async_computation | async-start | bytes 1572864 | tf_op jit(solution)/shard_map/all_to_all | solution.py:387
  15.3 1.1 copy-start.2
  16.4 9.9 %copy-start.9 = (s32[1,128,192]{1,2,0:T(8,128)S(1)}, s32[1,128,192]{1,2,0:T(8,128)}, u32[]{:S(2)}) copy-start(s32[1,128,192]{1,2,0:T(8,128)} %param.12) | copy-start | bytes 294916
  17.7 18.5 %collective-permute-start.2 = (bf16[2,128,128]{2,1,0:T(8,128)(2,1)}, bf16[2,128,128]{2,1,0:T(8,128)(2,1)S(1)}, u32[]{:S(2)}, u32[]{:S(2)}) collective-permute-start(bf16[2,128,128]{2,1,0:T(8,128)(2,1)} %get-tuple-element.37), channel_id=1, source_target_pairs={{0,96},{32,0},{64,32},{96,64},{1,97},{33,1},{65,33},{97,65},{2,98}... | collective-permute-start | bytes 196616 | tf_op jit(solution)/shard_map/ppermute | solution.py:375
  21.6 20.7 %collective-permute-start.1 = (bf16[2,128,128]{2,1,0:T(8,128)(2,1)}, bf16[2,128,128]{2,1,0:T(8,128)(2,1)S(1)}, u32[]{:S(2)}, u32[]{:S(2)}) collective-permute-start(bf16[2,128,128]{2,1,0:T(8,128)(2,1)} %get-tuple-element.38), channel_id=1, source_target_pairs={{0,64},{32,96},{64,0},{96,32},{1,65},{33,97},{65,1},{97,33},{2,66}... | collective-permute-start | bytes 196616 | tf_op jit(solution)/shard_map/ppermute | solution.py:375
  23.9 18.4 %collective-permute-start = (bf16[2,128,128]{2,1,0:T(8,128)(2,1)}, bf16[2,128,128]{2,1,0:T(8,128)(2,1)S(1)}, u32[]{:S(2)}, u32[]{:S(2)}) collective-permute-start(bf16[2,128,128]{2,1,0:T(8,128)(2,1)} %get-tuple-element.39), channel_id=1, source_target_pairs={{0,32},{32,64},{64,96},{96,0},{1,33},{33,65},{65,97},{97,1},{2,34}... | collective-permute-start | bytes 196616 | tf_op jit(solution)/shard_map/ppermute | solution.py:375
  28.0 0.8 copy-start.7
  28.7 17.9 %copy-start = (bf16[2,512,512]{2,1,0:T(8,128)(2,1)S(1)}, bf16[2,512,512]{2,1,0:T(8,128)(2,1)}, u32[]{:S(2)}) copy-start(bf16[2,512,512]{2,1,0:T(8,128)(2,1)} %audio_ref.1) | copy-start | bytes 3145732
  28.7 17.9 %copy-start.1 = (bf16[2,512,512]{2,1,0:T(8,128)(2,1)S(1)}, bf16[2,512,512]{2,1,0:T(8,128)(2,1)}, u32[]{:S(2)}) copy-start(bf16[2,512,512]{2,1,0:T(8,128)(2,1)} %video_ref.1) | copy-start | bytes 3145732
  28.7 17.9 %copy-start.3 = (f32[2,4]{1,0:T(2,128)S(1)}, f32[2,4]{1,0:T(2,128)}, u32[]{:S(2)}) copy-start(f32[2,4]{1,0:T(2,128)} %gate_ref.1) | copy-start | bytes 100
  28.7 17.9 %copy-start.4 = (s32[2]{0:T(128)S(1)}, s32[2]{0:T(128)}, u32[]{:S(2)}) copy-start(s32[2]{0:T(128)} %len_ref.1) | copy-start | bytes 28
  45.8 3.7 %collective-permute-start.5 = (bf16[2,1536,128]{2,1,0:T(8,128)(2,1)S(1)}, bf16[2,1536,128]{2,1,0:T(8,128)(2,1)S(1)}, u32[]{:S(2)}, u32[]{:S(2)}) collective-permute-start(bf16[2,1536,128]{2,1,0:T(8,128)(2,1)S(1)} %get-tuple-element.23.kv0), channel_id=1, source_target_pairs={{0,8},{8,0},{1,9},{9,1},{2,10},{10,2},{3,11},{11,3},{4,12},{12,4},... | collective-permute-start | bytes 2359304 | tf_op jit(solution)/shard_map/ppermute | solution.py:372
  45.9 20.0 %collective-permute-start.3 = (bf16[2,1536,128]{2,1,0:T(8,128)(2,1)S(1)}, bf16[2,1536,128]{2,1,0:T(8,128)(2,1)S(1)}, u32[]{:S(2)}, u32[]{:S(2)}) collective-permute-start(bf16[2,1536,128]{2,1,0:T(8,128)(2,1)S(1)} %unpack_keys.1.token_ref), channel_id=1, source_target_pairs={{0,128},{128,0},{1,129},{129,1},{2,130},{130,2},{3,131},{131,3},{4... | collective-permute-start | bytes 2359304 | tf_op jit(solution)/shard_map/ppermute | solution.py:372
  46.7 8.4 %collective-permute-start.4 = (bf16[1024,128]{1,0:T(8,128)(2,1)S(1)}, bf16[1024,128]{1,0:T(8,128)(2,1)S(1)}, u32[]{:S(2)}, u32[]{:S(2)}) collective-permute-start(bf16[1024,128]{1,0:T(8,128)(2,1)S(1)} %get-tuple-element.22.q_ref), channel_id=1, source_target_pairs={{0,16},{16,0},{1,17},{17,1},{2,18},{18,2},{3,19},{19,3},{4,20},{20... | collective-permute-start | bytes 786440 | tf_op jit(solution)/shard_map/ppermute | solution.py:372
  55.0 10.8 %copy-start.8 = (f32[32,3072]{1,0:T(8,128)S(1)}, f32[32,3072]{1,0:T(8,128)}, u32[]{:S(2)}) copy-start(f32[32,3072]{1,0:T(8,128)} %copy-done.7) | copy-start | bytes 1179652
  65.9 3.1 %collective-permute-start.6 = (bf16[2,1536,128]{2,1,0:T(8,128)(2,1)S(1)}, bf16[2,1536,128]{2,1,0:T(8,128)(2,1)S(1)}, u32[]{:S(2)}, u32[]{:S(2)}) collective-permute-start(bf16[2,1536,128]{2,1,0:T(8,128)(2,1)S(1)} %after.5.refs_0_), channel_id=1, source_target_pairs={{0,8},{8,0},{1,9},{9,1},{2,10},{10,2},{3,11},{11,3},{4,12},{12,4},... | collective-permute-start | bytes 2359304 | tf_op jit(solution)/shard_map/ppermute | solution.py:372
  72.0 9.0 %collective-permute-start.7 = (bf16[1056,128]{1,0:T(8,128)(2,1)S(1)}, bf16[1056,128]{1,0:T(8,128)(2,1)S(1)}, u32[]{:S(2)}, u32[]{:S(2)}) collective-permute-start(bf16[1056,128]{1,0:T(8,128)(2,1)S(1)} %near_keys_partner.1), channel_id=1, source_target_pairs={{0,16},{16,0},{1,17},{17,1},{2,18},{18,2},{3,19},{19,3},{4,20},{20... | collective-permute-start | bytes 811016 | tf_op jit(solution)/shard_map/ppermute | solution.py:372
  81.0 14.4 %copy-start.5 = (bf16[512,4096]{1,0:T(8,128)(2,1)S(1)}, bf16[512,4096]{1,0:T(8,128)(2,1)}, u32[]{:S(2)}) copy-start(bf16[512,4096]{1,0:T(8,128)(2,1)} %w_ref.1) | copy-start | bytes 12582916

commit v6 on v5

--- a/solution.py
+++ b/solution.py
@@ -38,10 +38,13 @@
     return [(i, (i + k) % count) for i in range(count)]
 
 
-def pack_kernel(span_ref, span_out, span_in, packed, sems):
+def pack_kernel(span_ref, cache_ref, span_out, *refs):
+    cache_outs, (span_in, cache_in, packed, sems) = refs[:4], refs[4:]
+    j = lax.axis_index("z2") * 2 + lax.axis_index("z1")
     reads = [
         pltpu.make_async_copy(span_ref.at[n], span_in.at[n], sems.at[n]) for n in range(3)
     ]
+    reads.append(pltpu.make_async_copy(cache_ref, cache_in, sems.at[3]))
     for copy in reads:
         copy.start()
     for n in range(3):
@@ -49,15 +52,15 @@
         for d in range(32):
             col = ((d % 8) * 4 + d // 8) * HD
             packed[d, n] = span_in[n, :, col:col + HD]
-    write = pltpu.make_async_copy(packed, span_out, sems.at[3])
-    write.start()
-    write.wait()
-
-
-def pack_cache_kernel(where_ref, cache_ref, token_ref, cache_out):
-    j = where_ref[1]
-    for k in range(4):
-        cache_out[k] = cache_ref[:, :, pl.ds(pl.multiple_of(((j + k) & 3) * HD, HD), HD)]
+    writes = [pltpu.make_async_copy(packed, span_out, sems.at[4])]
+    writes[0].start()
+    reads[3].wait()
+    for k, cache_out in enumerate(cache_outs):
+        piece = cache_in.at[:, :, pl.ds(pl.multiple_of(((j + k) & 3) * HD, HD), HD)]
+        writes.append(pltpu.make_async_copy(piece, cache_out, sems.at[5 + k]))
+        writes[1 + k].start()
+    for copy in writes:
+        copy.wait()
 
 
 def copy_keys(got_ref, cache_refs, kv_out):
@@ -308,6 +311,22 @@
             out_ref[h, :, cols] = part[h * 32:(h + 1) * 32]
 
 
+def sum_kernel(got_ref, out_ref, sums, sems):
+    writes = []
+    for n in range(4):
+        cols = slice(n * 1024, (n + 1) * 1024)
+        total = got_ref[0, :, cols].astype(jnp.float32)
+        for h in range(1, 8):
+            total = total + got_ref[h, :, cols].astype(jnp.float32)
+        sums[:, cols] = total.astype(jnp.bfloat16)
+        writes.append(
+            pltpu.make_async_copy(sums.at[:, cols], out_ref.at[:, cols], sems.at[n])
+        )
+        writes[n].start()
+    for copy in writes:
+        copy.wait()
+
+
 def cost(us):
     return pl.CostEstimate(flops=int(us * 1.15e9), bytes_accessed=1024, transcendentals=0)
 
@@ -344,29 +363,21 @@
         [lax.axis_index("yl"), j, lax.axis_index("z0"), lax.axis_index("c")]
     ).astype(jnp.int32)
 
-    span_packed = pl.pallas_call(
+    span_packed, *cache_packed = pl.pallas_call(
         pack_kernel,
-        out_shape=b16(32, 3, 32, HD),
-        in_specs=[anywhere()],
-        out_specs=anywhere(),
+        out_shape=(b16(32, 3, 32, HD),) + (b16(2, 128, HD),) * 4,
+        in_specs=[anywhere()] * 2,
+        out_specs=(anywhere(),) * 5,
         scratch_shapes=[
             pltpu.VMEM((3, 32, 4096), jnp.bfloat16),
+            pltpu.VMEM((2, 128, 512), jnp.bfloat16),
             pltpu.VMEM((32, 3, 32, HD), jnp.bfloat16),
-            pltpu.SemaphoreType.DMA((4,)),
+            pltpu.SemaphoreType.DMA((9,)),
         ],
         compiler_params=params(60 * 2**20),
         cost_estimate=cost(2),
         name="pack",
-    )(span_qkv)
-    cache_packed = pl.pallas_call(
-        pack_cache_kernel,
-        out_shape=b16(4, 2, 128, HD),
-        in_specs=[scalars(), whole(), anywhere()],
-        out_specs=whole(),
-        compiler_params=params(),
-        cost_estimate=cost(1),
-        name="pack_cache",
-    )(where, cache_kv, span_packed)
+    )(span_qkv, cache_kv)
 
     def swap(part, axis):
         return lax.ppermute(part, axis, xor_perm(2, 1))
@@ -385,7 +396,7 @@
     )(where, block_mask)
 
     got = lax.all_to_all(span_packed, ZZ + HEADS, split_axis=0, concat_axis=0, tiled=True)
-    cache_own = swap_z([cache_packed[k] for k in range(4)])
+    cache_own = swap_z(cache_packed)
     def unpack(kernel, token, name, *outs):
         return pl.pallas_call(
             kernel,
@@ -488,7 +499,19 @@
         name="project",
     )(mixed, out_weight)
     gathered = lax.all_to_all(partial_sums, HEADS, split_axis=0, concat_axis=0, tiled=True)
-    return jnp.sum(gathered.astype(jnp.float32), axis=0).astype(jnp.bfloat16)
+    return pl.pallas_call(
+        sum_kernel,
+        out_shape=b16(32, 4096),
+        in_specs=[whole()],
+        out_specs=anywhere(),
+        scratch_shapes=[
+            pltpu.VMEM((32, 4096), jnp.bfloat16),
+            pltpu.SemaphoreType.DMA((4,)),
+        ],
+        compiler_params=params(),
+        cost_estimate=cost(1),
+        name="sum",
+    )(gathered)
 
 
 def solution(mesh):

time: 128 us -> 129 us (level); the launches traced: 128 us -> 127 us
  local copies, waits for them, and re-layouts: 2.69 us -> 0.88 us
  starting transfers between devices: 22.6 us -> 23.9 us
  transfers between devices with their start and end apart: 9 -> 9, of which waited for: 6 -> 5; matrix products, arithmetic and copies ran while one was open for 1% -> 0% of each run, Pallas kernels for 16% -> 15%
where the time goes in v6:
time: 129 us; the launch traced here: 127 us
  blocking collectives  43.6 us (34%)
  waiting for transfers between devices  30.7 us (24%)
  Pallas kernels  27.3 us (21%)
  starting transfers between devices  23.9 us (19%)
    all_to_all x1, blocking collectives, shards(): lax.all_to_all(partial_sums, HEADS, split_axis=0, concat_axis=0, tiled=True)  29.5 us
    all_to_all x1, blocking collectives, shards(): mixed = lax.all_to_all(state, ZZ, split_axis=0, concat_axis=0, tiled=True)  14.2 us
    ppermute x3, waiting for transfers between devices, swap_z(): lax.ppermute(parts[k], ZZ, turn_perm(4, k))  14.1 us
    ppermute x5, waiting for transfers between devices, swap(): return lax.ppermute(part, axis, xor_perm(2, 1))  13.2 us
    all_to_all x1, starting transfers between devices, shards(): lax.all_to_all(span_packed, ZZ + HEADS, split_axis=0, concat_axis=0, tile...  13.1 us
    ppermute x3, starting transfers between devices, swap_z(): lax.ppermute(parts[k], ZZ, turn_perm(4, k))  9.92 us
    pallas_call x2, Pallas kernels, near(): pl.pallas_call(functools.partial(near_kernel, which, cores), out_shape=(f...  7.9 us
    pallas_call x2, Pallas kernels, own(): pl.pallas_call(functools.partial(own_kernel, which), out_shape=(f32(1024,...  7.14 us
  transfers between devices with their start and end apart: 9, of which 5 were waited for; matrix products, arithmetic and copies ran while one was open for 0% of the time, Pallas kernels for 15%

profile of v6, /device:TPU:32, one launch (start us, length us, event | category | flops | bytes accessed | tf_op | source)
XLA Modules:
  0.0 126.9 jit_solution(17243852819295494636)
XLA Ops:
  0.0 0.0 copy-start.8
  0.0 2.2 %pack.1 = (bf16[32,3,32,128]{3,2,1,0:T(8,128)(2,1)}, bf16[2,128,128]{2,1,0:T(8,128)(2,1)}, bf16[2,128,128]{2,1,0:T(8,128)(2,1)}, bf16[2,128,128]{2,1,0:T(8,128)(2,1)}, bf16[2,128,128]{2,1,0:T(8,128)(2,1)}) custom-call(bf16[3,32,4096]{2,1,0:T(8,128)(2,1)} %span_ref.1, bf16[2,128,512]{2,1,0:T(8,128)(2,1)} %cache_ref.1), custom_call_target="tpu_custom_call" | custom-call | flops 2300000000 | bytes 1024 | tf_op jit(solution)/shard_map/pack/pallas_call | solution.py:366
  2.2 13.1 %all-to-all-start = ((bf16[32,3,32,128]{3,2,1,0:T(8,128)(2,1)}), bf16[32,3,32,128]{3,2,1,0:T(8,128)(2,1)S(1)}, u32[]{:S(2)}, u32[]{:S(2)}) async-start(bf16[32,3,32,128]{3,2,1,0:T(8,128)(2,1)} %get-tuple-element.26), calls=%async_computation | async-start | bytes 1572864 | tf_op jit(solution)/shard_map/all_to_all | solution.py:398
  15.3 2.8 %collective-permute-start = (bf16[2,128,128]{2,1,0:T(8,128)(2,1)}, bf16[2,128,128]{2,1,0:T(8,128)(2,1)S(1)}, u32[]{:S(2)}, u32[]{:S(2)}) collective-permute-start(bf16[2,128,128]{2,1,0:T(8,128)(2,1)} %get-tuple-element.28), channel_id=1, source_target_pairs={{0,32},{32,64},{64,96},{96,0},{1,33},{33,65},{65,97},{97,1},{2,34}... | collective-permute-start | bytes 196616 | tf_op jit(solution)/shard_map/ppermute | solution.py:386
  18.1 3.6 %collective-permute-start.1 = (bf16[2,128,128]{2,1,0:T(8,128)(2,1)}, bf16[2,128,128]{2,1,0:T(8,128)(2,1)S(1)}, u32[]{:S(2)}, u32[]{:S(2)}) collective-permute-start(bf16[2,128,128]{2,1,0:T(8,128)(2,1)} %get-tuple-element.29), channel_id=1, source_target_pairs={{0,64},{32,96},{64,0},{96,32},{1,65},{33,97},{65,1},{97,33},{2,66}... | collective-permute-start | bytes 196616 | tf_op jit(solution)/shard_map/ppermute | solution.py:386
  21.7 3.5 %collective-permute-start.2 = (bf16[2,128,128]{2,1,0:T(8,128)(2,1)}, bf16[2,128,128]{2,1,0:T(8,128)(2,1)S(1)}, u32[]{:S(2)}, u32[]{:S(2)}) collective-permute-start(bf16[2,128,128]{2,1,0:T(8,128)(2,1)} %get-tuple-element.30), channel_id=1, source_target_pairs={{0,96},{32,0},{64,32},{96,64},{1,97},{33,1},{65,33},{97,65},{2,98}... | collective-permute-start | bytes 196616 | tf_op jit(solution)/shard_map/ppermute | solution.py:386
  25.2 0.0 copy-done.8
  25.2 0.1 copy.12.mask_ref
  25.3 0.1 pad_add_fusion.where_ref
  25.4 0.0 copy-start.2
  25.4 1.5 %bias.1 = (f32[32,3072]{1,0:T(8,128)S(1)}, f32[32,3072]{1,0:T(8,128)S(1)}) custom-call(s32[4]{0:T(128)S(1)} %pad_add_fusion.where_ref, s32[1,128,192]{2,1,0:T(8,128)S(1)} %copy.12.mask_ref), custom_call_target="tpu_custom_call" | custom-call | flops 2300000000 | bytes 1024 | tf_op jit(solution)/shard_map/bias/pallas_call | solution.py:388
  26.9 0.0 copy-start.6
  27.0 0.8 copy-done.6
  27.7 0.0 copy-start
  27.7 0.0 copy-start.1
  27.7 0.0 copy-start.3
  27.7 0.0 copy-start.4
  27.7 14.1 %collective-permute-done.c1_ref = bf16[2,128,128]{2,1,0:T(8,128)(2,1)S(1)} collective-permute-done((bf16[2,128,128]{2,1,0:T(8,128)(2,1)}, bf16[2,128,128]{2,1,0:T(8,128)(2,1)S(1)}, u32[]{:S(2)}, u32[]{:S(2)}) %collective-permute-start) | collective-permute-done | bytes 65568 | tf_op jit(solution)/shard_map/ppermute | solution.py:386
  41.8 0.0 collective-permute-done.1.c2_ref
  41.8 0.0 collective-permute-done.2.c3_ref
  41.8 3.4 %all-to-all-done.got_ref = bf16[32,3,32,128]{3,2,1,0:T(8,128)(2,1)S(1)} async-done(((bf16[32,3,32,128]{3,2,1,0:T(8,128)(2,1)}), bf16[32,3,32,128]{3,2,1,0:T(8,128)(2,1)S(1)}, u32[]{:S(2)}, u32[]{:S(2)}) %all-to-all-start) | async-done | bytes 786464 | tf_op jit(solution)/shard_map/all_to_all | solution.py:398
  45.2 0.0 copy-done.2
  45.2 0.1 unpack_keys.1.token_ref
  45.3 0.1 unpack_rest.1
  45.4 0.1 collective-permute-start.5
  45.5 0.8 collective-permute-start.3
  46.2 0.0 collective-permute-start.4
  46.3 0.0 copy-done
  46.3 0.0 copy-done.1
  46.3 0.0 copy-done.3
  46.3 0.0 copy-done.4
  46.3 2.8 %memories.1.token_ref.extra_ref = f32[1024,128]{1,0:T(8,128)S(1)} custom-call(s32[4]{0:T(128)S(1)} %pad_add_fusion.where_ref, s32[2]{0:T(128)S(1)} %copy-done.4, f32[2,4]{1,0:T(2,128)S(1)} %copy-done.3, bf16[1024,128]{1,0:T(8,128)(2,1)S(1)} %get-tuple-element.32.q_ref, bf16[2,512,512]{2,1,0:T(8,128)(2,1)S(1)} %copy-done, bf16[2,512,512]{2,1,0:T(8,128)(2,1)S(1)} %copy-done.1), custom_call_target="tpu_custom_call" | custom-call | flops 1150000 | bytes 1024 | tf_op jit(solution)/shard_map/memories/pallas_call | solution.py:419
  49.1 0.0 collective-permute-done.5.array_ref
  49.1 3.5 %own_keys.2 = (f32[1024,128]{1,0:T(8,128)S(1)}, f32[1024,128]{1,0:T(8,128)S(1)}, f32[1024,128]{1,0:T(8,128)S(1)}) custom-call(bf16[1024,128]{1,0:T(8,128)(2,1)S(1)} %get-tuple-element.32.q_ref, bf16[2,1536,128]{2,1,0:T(8,128)(2,1)S(1)} %get-tuple-element.33.kv0, bf16[2,1536,128]{2,1,0:T(8,128)(2,1)S(1)} %after.3.kv1, ...), custom_call_target="tpu_custom_call" | custom-call | flops 1150000 | bytes 1024 | tf_op jit(solution)/shard_map/own_keys/pallas_call | solution.py:440
  52.7 2.0 %collective-permute-done.4.array_ref = bf16[1024,128]{1,0:T(8,128)(2,1)S(1)} collective-permute-done((bf16[1024,128]{1,0:T(8,128)(2,1)S(1)}, bf16[1024,128]{1,0:T(8,128)(2,1)S(1)}, u32[]{:S(2)}, u32[]{:S(2)}) %collective-permute-start.4) | collective-permute-done | bytes 262176 | tf_op jit(solution)/shard_map/ppermute | solution.py:383
  54.6 0.0 copy-start.7
  54.6 3.6 %own_keys.3 = (f32[1024,128]{1,0:T(8,128)S(1)}, f32[1024,128]{1,0:T(8,128)S(1)}, f32[1024,128]{1,0:T(8,128)S(1)}) custom-call(bf16[1024,128]{1,0:T(8,128)(2,1)S(1)} %after.4.q_ref, bf16[2,1536,128]{2,1,0:T(8,128)(2,1)S(1)} %get-tuple-element.33.kv0, bf16[2,1536,128]{2,1,0:T(8,128)(2,1)S(1)} %after.3.kv1, f32[32,3072]{1,0:T(8,128)S(1)} %get-tuple-element.31.token_ref.bias_ref), custom_call_target="tpu_custom_call" | custom-call | flops 1150000 | bytes 1024 | tf_op jit(solution)/shard_map/own_keys/pallas_call | solution.py:440
  58.2 7.2 %collective-permute-done.3.array_ref = bf16[2,1536,128]{2,1,0:T(8,128)(2,1)S(1)} collective-permute-done((bf16[2,1536,128]{2,1,0:T(8,128)(2,1)S(1)}, bf16[2,1536,128]{2,1,0:T(8,128)(2,1)S(1)}, u32[]{:S(2)}, u32[]{:S(2)}) %collective-permute-start.3) | collective-permute-done | bytes 786464 | tf_op jit(solution)/shard_map/ppermute | solution.py:383
  65.4 0.0 collective-permute-start.6
  65.5 0.0 copy-done.7
  65.5 3.1 %near_keys.3 = (f32[1024,128]{1,0:T(8,128)S(1)}, f32[1024,128]{1,0:T(8,128)S(1)}, f32[1024,128]{1,0:T(8,128)S(1)}) custom-call(s32[4]{0:T(128)S(1)} %pad_add_fusion.where_ref, bf16[1024,128]{1,0:T(8,128)(2,1)S(1)} %after.4.q_ref, bf16[2,1536,128]{2,1,0:T(8,128)(2,1)S(1)} %after.5.refs_0_, f32[32,3072]{1,0:T(8,128)S(1)} %copy-done.7, ...), custom_call_target="tpu_custom_call" | custom-call | flops 2875000064 | bytes 1024 | tf_op jit(solution)/shard_map/near_keys/pallas_call | solution.py:458
  68.5 0.0 collective-permute-done.6.refs_1_.kv_ref
  68.5 3.0 %near_keys_partner.1 = bf16[1056,128]{1,0:T(8,128)(2,1)S(1)} custom-call(s32[4]{0:T(128)S(1)} %pad_add_fusion.where_ref, bf16[1024,128]{1,0:T(8,128)(2,1)S(1)} %after.4.q_ref, bf16[2,1536,128]{2,1,0:T(8,128)(2,1)S(1)} %collective-permute-done.6.refs_1_.kv_ref, f32[32,3072]{1,0:T(8,128)S(1)} %copy-done.7, f32[1024,128]{1,0:T(8,128)S(1)} %get-tuple-element.44.t_ref, ...), custom_call_target="tpu_custom_call" | custom-call | flops 3449999872 | bytes 1024 | tf_op jit(solution)/shard_map/near_keys_partner/pallas_call | solution.py:469
  71.5 0.1 collective-permute-start.7
  71.6 4.8 %near_keys.2 = (f32[1024,128]{1,0:T(8,128)S(1)}, f32[1024,128]{1,0:T(8,128)S(1)}, f32[1024,128]{1,0:T(8,128)S(1)}) custom-call(s32[4]{0:T(128)S(1)} %pad_add_fusion.where_ref, bf16[1024,128]{1,0:T(8,128)(2,1)S(1)} %get-tuple-element.32.q_ref, bf16[2,1536,128]{2,1,0:T(8,128)(2,1)S(1)} %after.5.refs_0_, ...), custom_call_target="tpu_custom_call" | custom-call | flops 5750000128 | bytes 1024 | tf_op jit(solution)/shard_map/near_keys/pallas_call | solution.py:458
  76.4 4.0 %collective-permute-done.7.part_ref = bf16[1056,128]{1,0:T(8,128)(2,1)S(1)} collective-permute-done((bf16[1056,128]{1,0:T(8,128)(2,1)S(1)}, bf16[1056,128]{1,0:T(8,128)(2,1)S(1)}, u32[]{:S(2)}, u32[]{:S(2)}) %collective-permute-start.7) | collective-permute-done | bytes 270368 | tf_op jit(solution)/shard_map/ppermute | solution.py:383
  80.5 0.0 copy-start.5
  80.5 0.4 combine.1
  80.9 14.2 %all_to_all.15.got_ref = bf16[4,256,128]{2,1,0:T(8,128)(2,1)S(1)} all-to-all(bf16[4,256,128]{2,1,0:T(8,128)(2,1)S(1)} %combine.1), channel_id=1, replica_groups=mesh['yl'=2,'z2'=2,'z1'=2,'z0'=2,'c'=2,'x'=4,'yh'=2] {'z2','z1'}, dimensions={0} | all-to-all | bytes 524288 | tf_op jit(solution)/shard_map/all_to_all | solution.py:491
  95.0 0.0 copy-done.5
  95.0 1.3 project.1
  96.3 29.5 %all_to_all.16.got_ref = bf16[8,32,4096]{2,1,0:T(8,128)(2,1)S(1)} all-to-all(bf16[8,32,4096]{2,1,0:T(8,128)(2,1)S(1)} %project.1), channel_id=1, replica_groups=mesh['yl'=2,'z2'=2,'z1'=2,'z0'=2,'c'=2,'x'=4,'yh'=2] {'x','yh'}, dimensions={0} | all-to-all | bytes 4194304 | tf_op jit(solution)/shard_map/all_to_all | solution.py:501
  125.8 0.9 sum.1
  (3 shorter events, 0.0 us)
Async XLA Ops:
  0.0 25.2 %copy-start.8 = (s32[1,128,192]{1,2,0:T(8,128)S(1)}, s32[1,128,192]{1,2,0:T(8,128)}, u32[]{:S(2)}) copy-start(s32[1,128,192]{1,2,0:T(8,128)} %param.12) | copy-start | bytes 294916
  2.2 43.0 %all-to-all-start = ((bf16[32,3,32,128]{3,2,1,0:T(8,128)(2,1)}), bf16[32,3,32,128]{3,2,1,0:T(8,128)(2,1)S(1)}, u32[]{:S(2)}, u32[]{:S(2)}) async-start(bf16[32,3,32,128]{3,2,1,0:T(8,128)(2,1)} %get-tuple-element.26), calls=%async_computation | async-start | bytes 1572864 | tf_op jit(solution)/shard_map/all_to_all | solution.py:398
  15.3 26.5 %collective-permute-start = (bf16[2,128,128]{2,1,0:T(8,128)(2,1)}, bf16[2,128,128]{2,1,0:T(8,128)(2,1)S(1)}, u32[]{:S(2)}, u32[]{:S(2)}) collective-permute-start(bf16[2,128,128]{2,1,0:T(8,128)(2,1)} %get-tuple-element.28), channel_id=1, source_target_pairs={{0,32},{32,64},{64,96},{96,0},{1,33},{33,65},{65,97},{97,1},{2,34}... | collective-permute-start | bytes 196616 | tf_op jit(solution)/shard_map/ppermute | solution.py:386
  18.1 23.8 %collective-permute-start.1 = (bf16[2,128,128]{2,1,0:T(8,128)(2,1)}, bf16[2,128,128]{2,1,0:T(8,128)(2,1)S(1)}, u32[]{:S(2)}, u32[]{:S(2)}) collective-permute-start(bf16[2,128,128]{2,1,0:T(8,128)(2,1)} %get-tuple-element.29), channel_id=1, source_target_pairs={{0,64},{32,96},{64,0},{96,32},{1,65},{33,97},{65,1},{97,33},{2,66}... | collective-permute-start | bytes 196616 | tf_op jit(solution)/shard_map/ppermute | solution.py:386
  21.7 20.1 %collective-permute-start.2 = (bf16[2,128,128]{2,1,0:T(8,128)(2,1)}, bf16[2,128,128]{2,1,0:T(8,128)(2,1)S(1)}, u32[]{:S(2)}, u32[]{:S(2)}) collective-permute-start(bf16[2,128,128]{2,1,0:T(8,128)(2,1)} %get-tuple-element.30), channel_id=1, source_target_pairs={{0,96},{32,0},{64,32},{96,64},{1,97},{33,1},{65,33},{97,65},{2,98}... | collective-permute-start | bytes 196616 | tf_op jit(solution)/shard_map/ppermute | solution.py:386
  25.4 19.9 %copy-start.2 = (bf16[2,128,128]{2,1,0:T(8,128)(2,1)S(1)}, bf16[2,128,128]{2,1,0:T(8,128)(2,1)}, u32[]{:S(2)}) copy-start(bf16[2,128,128]{2,1,0:T(8,128)(2,1)} %get-tuple-element.27.c0_ref) | copy-start | bytes 196612
  26.9 0.8 copy-start.6
  27.7 18.5 %copy-start = (bf16[2,512,512]{2,1,0:T(8,128)(2,1)S(1)}, bf16[2,512,512]{2,1,0:T(8,128)(2,1)}, u32[]{:S(2)}) copy-start(bf16[2,512,512]{2,1,0:T(8,128)(2,1)} %audio_ref.1) | copy-start | bytes 3145732
  27.7 18.5 %copy-start.1 = (bf16[2,512,512]{2,1,0:T(8,128)(2,1)S(1)}, bf16[2,512,512]{2,1,0:T(8,128)(2,1)}, u32[]{:S(2)}) copy-start(bf16[2,512,512]{2,1,0:T(8,128)(2,1)} %video_ref.1) | copy-start | bytes 3145732
  27.7 18.5 %copy-start.3 = (f32[2,4]{1,0:T(2,128)S(1)}, f32[2,4]{1,0:T(2,128)}, u32[]{:S(2)}) copy-start(f32[2,4]{1,0:T(2,128)} %gate_ref.1) | copy-start | bytes 100
  27.7 18.6 %copy-start.4 = (s32[2]{0:T(128)S(1)}, s32[2]{0:T(128)}, u32[]{:S(2)}) copy-start(s32[2]{0:T(128)} %len_ref.1) | copy-start | bytes 28
  45.4 3.7 %collective-permute-start.5 = (bf16[2,1536,128]{2,1,0:T(8,128)(2,1)S(1)}, bf16[2,1536,128]{2,1,0:T(8,128)(2,1)S(1)}, u32[]{:S(2)}, u32[]{:S(2)}) collective-permute-start(bf16[2,1536,128]{2,1,0:T(8,128)(2,1)S(1)} %get-tuple-element.33.kv0), channel_id=1, source_target_pairs={{0,8},{8,0},{1,9},{9,1},{2,10},{10,2},{3,11},{11,3},{4,12},{12,4},... | collective-permute-start | bytes 2359304 | tf_op jit(solution)/shard_map/ppermute | solution.py:383
  45.5 20.0 %collective-permute-start.3 = (bf16[2,1536,128]{2,1,0:T(8,128)(2,1)S(1)}, bf16[2,1536,128]{2,1,0:T(8,128)(2,1)S(1)}, u32[]{:S(2)}, u32[]{:S(2)}) collective-permute-start(bf16[2,1536,128]{2,1,0:T(8,128)(2,1)S(1)} %unpack_keys.1.token_ref), channel_id=1, source_target_pairs={{0,128},{128,0},{1,129},{129,1},{2,130},{130,2},{3,131},{131,3},{4... | collective-permute-start | bytes 2359304 | tf_op jit(solution)/shard_map/ppermute | solution.py:383
  46.2 8.4 %collective-permute-start.4 = (bf16[1024,128]{1,0:T(8,128)(2,1)S(1)}, bf16[1024,128]{1,0:T(8,128)(2,1)S(1)}, u32[]{:S(2)}, u32[]{:S(2)}) collective-permute-start(bf16[1024,128]{1,0:T(8,128)(2,1)S(1)} %get-tuple-element.32.q_ref), channel_id=1, source_target_pairs={{0,16},{16,0},{1,17},{17,1},{2,18},{18,2},{3,19},{19,3},{4,20},{20... | collective-permute-start | bytes 786440 | tf_op jit(solution)/shard_map/ppermute | solution.py:383
  54.6 10.8 %copy-start.7 = (f32[32,3072]{1,0:T(8,128)S(1)}, f32[32,3072]{1,0:T(8,128)}, u32[]{:S(2)}) copy-start(f32[32,3072]{1,0:T(8,128)} %copy-done.6) | copy-start | bytes 1179652
  65.4 3.1 %collective-permute-start.6 = (bf16[2,1536,128]{2,1,0:T(8,128)(2,1)S(1)}, bf16[2,1536,128]{2,1,0:T(8,128)(2,1)S(1)}, u32[]{:S(2)}, u32[]{:S(2)}) collective-permute-start(bf16[2,1536,128]{2,1,0:T(8,128)(2,1)S(1)} %after.5.refs_0_), channel_id=1, source_target_pairs={{0,8},{8,0},{1,9},{9,1},{2,10},{10,2},{3,11},{11,3},{4,12},{12,4},... | collective-permute-start | bytes 2359304 | tf_op jit(solution)/shard_map/ppermute | solution.py:383
  71.5 9.0 %collective-permute-start.7 = (bf16[1056,128]{1,0:T(8,128)(2,1)S(1)}, bf16[1056,128]{1,0:T(8,128)(2,1)S(1)}, u32[]{:S(2)}, u32[]{:S(2)}) collective-permute-start(bf16[1056,128]{1,0:T(8,128)(2,1)S(1)} %near_keys_partner.1), channel_id=1, source_target_pairs={{0,16},{16,0},{1,17},{17,1},{2,18},{18,2},{3,19},{19,3},{4,20},{20... | collective-permute-start | bytes 811016 | tf_op jit(solution)/shard_map/ppermute | solution.py:383
  80.5 14.6 %copy-start.5 = (bf16[512,4096]{1,0:T(8,128)(2,1)S(1)}, bf16[512,4096]{1,0:T(8,128)(2,1)}, u32[]{:S(2)}) copy-start(bf16[512,4096]{1,0:T(8,128)(2,1)} %w_ref.1) | copy-start | bytes 12582916
